TPU v7x, 32 devices: a whole 2x2x4 slice. The times are simulated.
32 devices in a mesh: dp: 2 (over y), ctx: 4 (over z), fsdp: 4 (over x, core).
Axes of the slice: x: 2, y: 2, z: 4, core: 2. Of those that a mesh axis runs over, the one named last changes fastest.
Arguments:
- hidden: bfloat16 [8, 512, 2048], P(('dp', 'fsdp'), 'ctx'), may hold values from -6 to 6
- cotangent: bfloat16 [8, 512, 2048], P(('dp', 'fsdp'), 'ctx'), may hold values from -6 to 6
- span_order: int32 [8], replicated, may hold values from 0 to 7, each once
- norm_gains: float32 [2, 2048], P(None, ('dp', 'ctx', 'fsdp')), may hold values from 0.5 to 1.5
- w_qkv: float32 [2048, 3072], P(('dp', 'ctx', 'fsdp')), may hold values from -0.125 to 0.125
- w_out: float32 [2048, 2048], P(('dp', 'ctx', 'fsdp')), may hold values from -1 to 1
- w_gate_up: float32 [2048, 16384], P(('dp', 'ctx', 'fsdp')), may hold values from -0.125 to 0.125
- w_down: float32 [2048, 8192], P(('dp', 'ctx', 'fsdp')), may hold values from -0.0625 to 0.0625
- mom_gains: float32 [2, 2, 2048], P(None, None, ('dp', 'ctx', 'fsdp')), as said below
- mom_qkv: float32 [2, 2048, 3072], P(None, ('dp', 'ctx', 'fsdp')), as said below
- mom_out: float32 [2, 2048, 2048], P(None, ('dp', 'ctx', 'fsdp')), as said below
- mom_gate_up: float32 [2, 2048, 16384], P(None, ('dp', 'ctx', 'fsdp')), as said below
- mom_down: float32 [2, 2048, 8192], P(None, ('dp', 'ctx', 'fsdp')), as said below
Outputs:
- output: bfloat16 [8, 512, 2048], P(('dp', 'fsdp'), 'ctx')
- grad_hidden: bfloat16 [8, 512, 2048], P(('dp', 'fsdp'), 'ctx')
- grad_gains: float32 [2, 2048], P(None, ('dp', 'ctx', 'fsdp'))
- grad_qkv: float32 [2048, 3072], P(('dp', 'ctx', 'fsdp'))
- grad_out: float32 [2048, 2048], P(('dp', 'ctx', 'fsdp'))
- grad_gate_up: float32 [2048, 16384], P(('dp', 'ctx', 'fsdp'))
- grad_down: float32 [2048, 8192], P(('dp', 'ctx', 'fsdp'))
- new_gains: float32 [2, 2048], P(None, ('dp', 'ctx', 'fsdp'))
- new_qkv: float32 [2048, 3072], P(('dp', 'ctx', 'fsdp'))
- new_out: float32 [2048, 2048], P(('dp', 'ctx', 'fsdp'))
- new_gate_up: float32 [2048, 16384], P(('dp', 'ctx', 'fsdp'))
- new_down: float32 [2048, 8192], P(('dp', 'ctx', 'fsdp'))
- new_mom_gains: float32 [2, 2, 2048], P(None, None, ('dp', 'ctx', 'fsdp'))
- new_mom_qkv: float32 [2, 2048, 3072], P(None, ('dp', 'ctx', 'fsdp'))
- new_mom_out: float32 [2, 2048, 2048], P(None, ('dp', 'ctx', 'fsdp'))
- new_mom_gate_up: float32 [2, 2048, 16384], P(None, ('dp', 'ctx', 'fsdp'))
- new_mom_down: float32 [2, 2048, 8192], P(None, ('dp', 'ctx', 'fsdp'))
Inputs may be any that keep to these rules, and one draw needn't show every extreme that they name: `span_order`: each span number appears exactly once. `mom_gains`: index 0 of the first dimension holds first moments, index 1 roots of second moments, which are positive. `mom_qkv`: index 0 of the first dimension holds first moments, index 1 roots of second moments, which are positive. `mom_out`: index 0 of the first dimension holds first moments, index 1 roots of second moments, which are positive. `mom_gate_up`: index 0 of the first dimension holds first moments, index 1 roots of second moments, which are positive. `mom_down`: index 0 of the first dimension holds first moments, index 1 roots of second moments, which are positive.
All inputs are finite; a program needn't handle non-finite values.
Results may differ from a plain program's by a relative error of at most 0.015.
Values may be sent and summed in bfloat16 or wider, within the bound.
A program may use at most 768 MiB of HBM per device.

v0:
```python
import math

import jax
import jax.numpy as jnp
from jax import lax
from jax.sharding import PartitionSpec as P

H = 32
KV = 8
HD = 64
FF = 8192


EPS_NORM = 1e-05
NEG_FILL = -1000000000.0
THETA = 500000.0
BETA_ONE = 0.9
BETA_TWO = 0.95
ADAM_EPS = 1e-08
DECAY_MATRIX = 0.1
LR_MATRIX = 0.01
LR_OUTPUT = 0.06
LR_GAIN = 0.3


def rope_table(positions):
    half_dim = HD // 2
    index_row = jnp.arange(half_dim, dtype=jnp.float32)
    frequency = jnp.exp(-(2.0 * index_row / HD) * math.log(THETA))
    wavelen = 2.0 * math.pi / frequency
    smooth = (8192.0 / wavelen - 1.0) / 3.0
    scaled = jnp.where(
        wavelen < 2048.0,
        frequency,
        jnp.where(
            wavelen > 8192.0,
            frequency / 32.0,
            (1.0 - smooth) * frequency / 32.0 + smooth * frequency,
        ),
    )
    angles = positions.astype(jnp.float32)[:, None] * scaled[None, :]
    cosine = jnp.cos(angles)
    sine_part = jnp.sin(angles)
    return (jnp.concatenate([cosine, cosine], 1), jnp.concatenate([sine_part, sine_part], 1))


def rope_apply(values_in, cos_tab, sin_tab):
    half_dim = values_in.shape[-1] // 2
    turned = jnp.concatenate([-values_in[..., half_dim:], values_in[..., :half_dim]], -1)
    return values_in * cos_tab[:, None, :] + turned * sin_tab[:, None, :]


def rope_back(grads_in, cos_tab, sin_tab):
    half_dim = grads_in.shape[-1] // 2
    moved = grads_in * sin_tab[:, None, :]
    return grads_in * cos_tab[:, None, :] + jnp.concatenate(
        [moved[..., half_dim:], -moved[..., :half_dim]], -1
    )


def norm_back(grad_entry, normed, inverse, gain):
    grad_gain = jnp.sum(grad_entry * normed, 0)
    grad_normed = grad_entry * gain
    grad_rows = inverse * (grad_normed - normed * jnp.mean(grad_normed * normed, -1, keepdims=True))
    return (grad_rows, grad_gain)


def adamw(weight, gradient, states, step_rate, decay_rate):
    first_mom = BETA_ONE * states[0] + (1.0 - BETA_ONE) * gradient
    root_mom = jnp.sqrt(BETA_TWO * states[1] * states[1] + (1.0 - BETA_TWO) * gradient * gradient)
    first_hat = first_mom / (1.0 - BETA_ONE**3)
    root_hat = root_mom / math.sqrt(1.0 - BETA_TWO**3)
    updated = weight - step_rate * (first_hat / (root_hat + ADAM_EPS) + decay_rate * weight)
    return (updated, jnp.stack([first_mom, root_mom]))


def contract_rows(left_arr, right_arr):
    return lax.dot_general(
        left_arr, right_arr, (((0,), (0,)), ((), ())), preferred_element_type=jnp.float32
    )


def contract_cols(left_arr, right_arr):
    return lax.dot_general(
        left_arr, right_arr, (((1,), (1,)), ((), ())), preferred_element_type=jnp.float32
    )


def ffn_rows(entry_mat, grad_mat, grad_gu_rows, activated):
    return jnp.concatenate(
        [contract_rows(entry_mat, grad_gu_rows), contract_rows(grad_mat, activated)], 1
    )


def shards(
    hidden,
    cotangent,
    span_order,
    norm_gains,
    w_qkv,
    w_out,
    w_gate_up,
    w_down,
    mom_gains,
    mom_qkv,
    mom_out,
    mom_gate_up,
    mom_down,
):
    block_rows = hidden.shape[1]
    span_rows = block_rows // 2
    total_rows = block_rows * lax.axis_size("ctx")
    groups = H // KV
    query_cols = H * HD
    kv_cols = KV * HD
    scale = HD ** (-0.5)
    key_pos = (
        span_order[:, None] * span_rows + jnp.arange(span_rows, dtype=jnp.int32)[None, :]
    ).reshape(-1)
    query_pos = lax.dynamic_slice_in_dim(key_pos, lax.axis_index("ctx") * block_rows, block_rows)
    visible = key_pos[None, :] <= query_pos[:, None]
    cos_tab, sin_tab = rope_table(query_pos)
    gains_c, qkv_c, out_c = (
        lax.all_gather(norm_gains.astype(jnp.bfloat16), ("dp", "ctx", "fsdp"), axis=1, tiled=True),
        lax.all_gather(w_qkv.astype(jnp.bfloat16), ("dp", "ctx", "fsdp"), axis=0, tiled=True),
        lax.all_gather(w_out.astype(jnp.bfloat16), ("dp", "ctx", "fsdp"), axis=0, tiled=True),
    )
    gain_one = gains_c[0].astype(jnp.float32)
    gain_two = gains_c[1].astype(jnp.float32)
    row_in = hidden[0].astype(jnp.float32)
    inv_one = lax.rsqrt(jnp.mean(row_in * row_in, -1, keepdims=True) + EPS_NORM)
    normed_one = row_in * inv_one
    entry_one = (normed_one * gain_one).astype(jnp.bfloat16)
    projected = jnp.dot(entry_one, qkv_c, preferred_element_type=jnp.float32)
    queries = rope_apply(
        projected[:, :query_cols].reshape(block_rows, H, HD), cos_tab, sin_tab
    ).astype(jnp.bfloat16)
    key_rows = rope_apply(
        projected[:, query_cols : query_cols + kv_cols].reshape(block_rows, KV, HD),
        cos_tab,
        sin_tab,
    ).astype(jnp.bfloat16)
    value_rows = projected[:, query_cols + kv_cols :].astype(jnp.bfloat16)
    keys_all, values_all = (
        lax.all_gather(key_rows.reshape(1, block_rows, kv_cols), "ctx", axis=1, tiled=True),
        lax.all_gather(value_rows.reshape(1, block_rows, kv_cols), "ctx", axis=1, tiled=True),
    )
    query_groups = queries.reshape(block_rows, KV, groups, HD).transpose(1, 0, 2, 3)
    key_groups = keys_all.reshape(total_rows, KV, HD).transpose(1, 0, 2)
    value_groups = values_all.reshape(total_rows, KV, HD).transpose(1, 0, 2)

    def forward_group(group_items):
        query_h, key_h, value_h = group_items
        scores = (
            jnp.einsum("tgd,sd->gts", query_h, key_h, preferred_element_type=jnp.float32) * scale
        )
        scores = jnp.where(visible[None], scores, NEG_FILL)
        top_score = jnp.max(scores, -1, keepdims=True)
        exponent = jnp.exp(scores - top_score)
        total_mass = jnp.sum(exponent, -1, keepdims=True)
        probability = (exponent / total_mass).astype(jnp.bfloat16)
        attended_h = jnp.einsum(
            "gts,sd->tgd", probability, value_h, preferred_element_type=jnp.float32
        )
        return (attended_h, (top_score + jnp.log(total_mass))[..., 0])

    attended_g, log_mass = lax.map(forward_group, (query_groups, key_groups, value_groups))
    attended = attended_g.transpose(1, 0, 2, 3).reshape(block_rows, query_cols).astype(jnp.bfloat16)
    middle = row_in + contract_cols(attended, out_c)
    inv_two = lax.rsqrt(jnp.mean(middle * middle, -1, keepdims=True) + EPS_NORM)
    normed_two = middle * inv_two
    entry_two = (normed_two * gain_two).astype(jnp.bfloat16)
    gate_up_c, down_c = (
        lax.all_gather(w_gate_up.astype(jnp.bfloat16), ("dp", "ctx", "fsdp"), axis=0, tiled=True),
        lax.all_gather(w_down.astype(jnp.bfloat16), ("dp", "ctx", "fsdp"), axis=0, tiled=True),
    )
    gate_up = jnp.dot(entry_two, gate_up_c, preferred_element_type=jnp.float32)
    gate_part = gate_up[:, :FF]
    up_part = gate_up[:, FF:]
    sigmoid_gate = jax.nn.sigmoid(gate_part)
    silu_gate = gate_part * sigmoid_gate
    activated = (silu_gate * up_part).astype(jnp.bfloat16)
    output = (middle + contract_cols(activated, down_c)).astype(jnp.bfloat16)[None]
    grad_top_low = cotangent[0]
    grad_top = grad_top_low.astype(jnp.float32)
    gate_up_back, down_back = (
        lax.all_gather(w_gate_up.astype(jnp.bfloat16), ("dp", "ctx", "fsdp"), axis=0, tiled=True),
        lax.all_gather(w_down.astype(jnp.bfloat16), ("dp", "ctx", "fsdp"), axis=0, tiled=True),
    )
    grad_act = jnp.dot(grad_top_low, down_back, preferred_element_type=jnp.float32)
    grad_gate = grad_act * up_part * sigmoid_gate * (1.0 + gate_part * (1.0 - sigmoid_gate))
    grad_up = grad_act * silu_gate
    grad_gu_rows = jnp.concatenate([grad_gate, grad_up], 1).astype(jnp.bfloat16)
    ffn_grads = lax.psum_scatter(
        ffn_rows(entry_two, grad_top_low, grad_gu_rows, activated),
        ("dp", "ctx", "fsdp"),
        scatter_dimension=0,
        tiled=True,
    )
    grad_entry_two = contract_cols(grad_gu_rows, gate_up_back)
    grad_mid_norm, grad_gain_two = norm_back(grad_entry_two, normed_two, inv_two, gain_two)
    grad_middle = grad_top + grad_mid_norm
    grad_branch = grad_middle.astype(jnp.bfloat16)
    grad_attended = jnp.dot(grad_branch, out_c, preferred_element_type=jnp.float32).astype(
        jnp.bfloat16
    )
    term_out = contract_rows(grad_branch, attended)
    grad_groups = grad_attended.reshape(block_rows, KV, groups, HD).transpose(1, 0, 2, 3)

    def backward_group(group_items):
        query_h, key_h, value_h, grad_h, mass_h = group_items
        scores = (
            jnp.einsum("tgd,sd->gts", query_h, key_h, preferred_element_type=jnp.float32) * scale
        )
        scores = jnp.where(visible[None], scores, NEG_FILL)
        probability = jnp.exp(scores - mass_h[..., None])
        prob_low = probability.astype(jnp.bfloat16)
        grad_prob = jnp.einsum("tgd,sd->gts", grad_h, value_h, preferred_element_type=jnp.float32)
        delta_row = jnp.sum(probability * grad_prob, -1, keepdims=True)
        grad_scores = jnp.where(visible[None], probability * (grad_prob - delta_row), 0.0).astype(
            jnp.bfloat16
        )
        grad_query = (
            jnp.einsum("gts,sd->tgd", grad_scores, key_h, preferred_element_type=jnp.float32)
            * scale
        )
        grad_key = (
            jnp.einsum("gts,tgd->sd", grad_scores, query_h, preferred_element_type=jnp.float32)
            * scale
        )
        grad_value = jnp.einsum("gts,tgd->sd", prob_low, grad_h, preferred_element_type=jnp.float32)
        return (grad_query, grad_key, grad_value)

    grad_query_g, grad_key_g, grad_value_g = lax.map(
        backward_group, (query_groups, key_groups, value_groups, grad_groups, log_mass)
    )
    grad_queries = grad_query_g.transpose(1, 0, 2, 3).reshape(block_rows, H, HD)
    grad_keys_all = grad_key_g.transpose(1, 0, 2).reshape(1, total_rows, kv_cols)
    grad_values_all = grad_value_g.transpose(1, 0, 2).reshape(1, total_rows, kv_cols)
    grad_key_rows, grad_value_rows = (
        lax.psum_scatter(
            grad_keys_all.astype(jnp.bfloat16), "ctx", scatter_dimension=1, tiled=True
        ).astype(jnp.float32),
        lax.psum_scatter(
            grad_values_all.astype(jnp.bfloat16), "ctx", scatter_dimension=1, tiled=True
        ).astype(jnp.float32),
    )
    grad_projected = jnp.concatenate(
        [
            rope_back(grad_queries, cos_tab, sin_tab).reshape(block_rows, query_cols),
            rope_back(grad_key_rows.reshape(block_rows, KV, HD), cos_tab, sin_tab).reshape(
                block_rows, kv_cols
            ),
            grad_value_rows.reshape(block_rows, kv_cols),
        ],
        1,
    ).astype(jnp.bfloat16)
    term_qkv = contract_rows(entry_one, grad_projected)
    grad_entry_one = contract_cols(grad_projected, qkv_c)
    grad_row_norm, grad_gain_one = norm_back(grad_entry_one, normed_one, inv_one, gain_one)
    grad_hidden = (grad_middle + grad_row_norm).astype(jnp.bfloat16)[None]
    grad_gains, grad_qkv, grad_out = (
        lax.psum_scatter(
            jnp.stack([grad_gain_one, grad_gain_two]),
            ("dp", "ctx", "fsdp"),
            scatter_dimension=1,
            tiled=True,
        ),
        lax.psum_scatter(term_qkv, ("dp", "ctx", "fsdp"), scatter_dimension=0, tiled=True),
        lax.psum_scatter(term_out, ("dp", "ctx", "fsdp"), scatter_dimension=0, tiled=True),
    )
    grad_gate_up = ffn_grads[:, : 2 * FF]
    grad_down = ffn_grads[:, 2 * FF :]
    new_gains, new_mom_gains = adamw(norm_gains, grad_gains, mom_gains, LR_GAIN, 0.0)
    new_qkv, new_mom_qkv = adamw(w_qkv, grad_qkv, mom_qkv, LR_MATRIX, DECAY_MATRIX)
    new_out, new_mom_out = adamw(w_out, grad_out, mom_out, LR_OUTPUT, DECAY_MATRIX)
    new_gate_up, new_mom_gate_up = adamw(
        w_gate_up, grad_gate_up, mom_gate_up, LR_MATRIX, DECAY_MATRIX
    )
    new_down, new_mom_down = adamw(w_down, grad_down, mom_down, LR_MATRIX, DECAY_MATRIX)
    return (
        output,
        grad_hidden,
        grad_gains,
        grad_qkv,
        grad_out,
        grad_gate_up,
        grad_down,
        new_gains,
        new_qkv,
        new_out,
        new_gate_up,
        new_down,
        new_mom_gains,
        new_mom_qkv,
        new_mom_out,
        new_mom_gate_up,
        new_mom_down,
    )


def solution(mesh):
    in_specs = (
        P(("dp", "fsdp"), "ctx", None),
        P(("dp", "fsdp"), "ctx", None),
        P(),
        P(None, ("dp", "ctx", "fsdp")),
        P(("dp", "ctx", "fsdp"), None),
        P(("dp", "ctx", "fsdp"), None),
        P(("dp", "ctx", "fsdp"), None),
        P(("dp", "ctx", "fsdp"), None),
        P(None, None, ("dp", "ctx", "fsdp")),
        P(None, ("dp", "ctx", "fsdp"), None),
        P(None, ("dp", "ctx", "fsdp"), None),
        P(None, ("dp", "ctx", "fsdp"), None),
        P(None, ("dp", "ctx", "fsdp"), None),
    )
    out_specs = (
        P(("dp", "fsdp"), "ctx", None),
        P(("dp", "fsdp"), "ctx", None),
        P(None, ("dp", "ctx", "fsdp")),
        P(("dp", "ctx", "fsdp"), None),
        P(("dp", "ctx", "fsdp"), None),
        P(("dp", "ctx", "fsdp"), None),
        P(("dp", "ctx", "fsdp"), None),
        P(None, ("dp", "ctx", "fsdp")),
        P(("dp", "ctx", "fsdp"), None),
        P(("dp", "ctx", "fsdp"), None),
        P(("dp", "ctx", "fsdp"), None),
        P(("dp", "ctx", "fsdp"), None),
        P(None, None, ("dp", "ctx", "fsdp")),
        P(None, ("dp", "ctx", "fsdp"), None),
        P(None, ("dp", "ctx", "fsdp"), None),
        P(None, ("dp", "ctx", "fsdp"), None),
        P(None, ("dp", "ctx", "fsdp"), None),
    )
    return jax.shard_map(shards, mesh=mesh, in_specs=in_specs, out_specs=out_specs, check_vma=False)
```

profile of v0, /device:TPU:0, one launch (start us, length us, event | category | flops | bytes accessed | tf_op | source)
XLA Modules:
  0.0 3139.9 jit_solution(434635563135551219)
XLA Ops:
  11.1 3.7 convert_element_type.138
  17.7 43.3 %all-gather.2 = bf16[32,64,2]{1,2,0:T(2,128)(2,1)S(1)} all-gather(bf16[1,64,2]{1,2,0:T(2,128)(2,1)S(1)} %convert_bitcast_fusion), channel_id=1, replica_groups=mesh['dp'=2,'ctx'=4,'fsdp'=4] {'dp','ctx','fsdp'}, dimensions={0}, use_global_device_ids=true | all-gather | bytes 8448 | tf_op jit(solution)/shard_map/all_gather | solution.py:124
  62.9 47.3 %all-gather.8.cloned.1.call-done = bf16[2048,3072]{1,0:T(8,128)(2,1)} async-done(((bf16[64,3072]{1,0:T(8,128)(2,1)}), bf16[2048,3072]{1,0:T(8,128)(2,1)}) %all-gather.8.cloned.1.call-update) | async-done | bytes 12582928 | tf_op jit(solution)/shard_map/all_gather | solution.py:125
  110.3 6.5 fusion.110
  117.9 19.1 all-gather
  138.4 21.0 all-gather.1
  163.1 22.0 while.30
  185.1 11.1 all-gather.10.cloned.1.call-done
  196.1 6.3 multiply_reduce_fusion.3
  202.5 352.1 %all-gather.12.cloned.1.call-done = bf16[2048,16384]{1,0:T(8,128)(2,1)} async-done(((bf16[64,16384]{1,0:T(8,128)(2,1)}), bf16[2048,16384]{1,0:T(8,128)(2,1)}) %all-gather.12.cloned.1.call-update) | async-done | bytes 67108880 | tf_op jit(solution)/shard_map/all_gather | solution.py:174
  554.5 27.4 fusion.123
  582.0 168.9 %all-gather.14.cloned.1.call-done = bf16[2048,8192]{1,0:T(8,128)(2,1)} async-done(((bf16[64,8192]{1,0:T(8,128)(2,1)}), bf16[2048,8192]{1,0:T(8,128)(2,1)}) %all-gather.14.cloned.1.call-update) | async-done | bytes 33554448 | tf_op jit(solution)/shard_map/all_gather | solution.py:175
  750.8 18.7 multiply_convert_fusion.1
  769.6 31.1 multiply_reduce_fusion.1
  803.3 4.7 convolution_convert_fusion
  809.0 65.1 %while.31 = (s32[]{:T(128)}, f32[8,128,4,64]{1,3,2,0:T(8,128)}, bf16[8,512,64]{1,2,0:T(8,128)(2,1)}, bf16[8,512,64]{1,2,0:T(8,128)(2,1)}, bf16[8,512,64]{1,2,0:T...) while((s32[]{:T(128)}, f32[8,128,4,64]{1,3,2,0:T(8,128)}, ...), condition=%wide.region_9.10_spmd.clone.clone, body=%wide.region_7.9_spmd.clone.sunk.clone | while | flops 171575296 | bytes 12662393 | solution.py:234
  883.2 14.4 reduce-scatter.21.cloned.1.call-done
  898.7 21.4 reduce-scatter.19.cloned.1.call-done
  921.5 10.7 fusion.84
  933.7 8.2 fusion.104
  942.9 10.8 fusion.101
  955.3 24.7 convolution_bitcast_fusion.4
  980.0 45.9 %fusion.67 = f32[2048,16384]{1,0:T(8,128)} fusion(bf16[128,8192]{1,0:T(8,128)(2,1)} %get-tuple-element.213, bf16[128,8192]{1,0:T(8,128)(2,1)} %copy-done.13, f32[128,2048]{1,0:T(8,128)S(1)} %get-tuple-element.239, f32[2048]{0:T(1024)S(1)} %bitcast.347, f32[128]{0:T(128)S(1)} %copy-done.28), kind=kOutput, calls=%fused_computation.92 | convolution fusion | flops 8599109632 | bytes 139469312 | tf_op jit(solution)/shard_map/dot_general | solution.py:78
  1025.8 133.2 %pad_maximum_fusion = f32[2048,24576]{1,0:T(8,128)} fusion(f32[2048,8192]{1,0:T(8,128)} %convolution_bitcast_fusion.4, f32[2048,16384]{1,0:T(8,128)} %fusion.67), kind=kLoop, calls=%fused_computation.74 | loop fusion | flops 50331648 | bytes 402653184 | tf_op jit(solution)/shard_map/concatenate | solution.py:90
  1161.1 17.2 fusion.70
  1181.5 65.8 %reduce-scatter.15.cloned.1.call-done = f32[64,2048]{1,0:T(8,128)} async-done(((f32[2048,2048]{1,0:T(8,128)}), f32[64,2048]{1,0:T(8,128)}) %reduce-scatter.15.cloned.1.call-update) | async-done | bytes 524304 | tf_op jit(solution)/shard_map/reduce_scatter | solution.py:270
  1251.1 253.1 %reduce-scatter.13.cloned.1.call-done = f32[64,3072]{1,0:T(8,128)} async-done(((f32[2048,3072]{1,0:T(8,128)}), f32[64,3072]{1,0:T(8,128)}) %reduce-scatter.13.cloned.1.call-update) | async-done | bytes 786448 | tf_op jit(solution)/shard_map/reduce_scatter | solution.py:269
  1508.1 1600.4 %reduce-scatter.17.cloned.1.call-done = f32[64,24576]{1,0:T(8,128)} async-done(((f32[2048,24576]{1,0:T(8,128)}), f32[64,24576]{1,0:T(8,128)}) %reduce-scatter.17.cloned.1.call-update) | async-done | bytes 6291472 | tf_op jit(solution)/shard_map/reduce_scatter | solution.py:194
  3108.4 4.3 fusion.77
  3113.1 8.3 fusion.100
  3123.6 3.0 fusion.108
  3126.6 4.0 pad_maximum_fusion.1
  (265 shorter events, 138.0 us)
Async XLA Ops:
  7.2 103.1 %all-gather.8.cloned.1.call-start = ((), (), s32[]{:S(2)}) async-start(), calls=%async_computation.6 | async-start | bytes 12976128 | tf_op jit(solution)/shard_map/all_gather | solution.py:125
  9.2 186.9 %all-gather.10.cloned.1.call-start = ((), (), s32[]{:S(2)}) async-start(), calls=%async_computation.7 | async-start | bytes 8650752 | tf_op jit(solution)/shard_map/all_gather | solution.py:126
  11.0 543.5 %all-gather.12.cloned.1.call-start = ((), (), s32[]{:S(2)}) async-start(), calls=%async_computation.8 | async-start | bytes 69206016 | tf_op jit(solution)/shard_map/all_gather | solution.py:174
  14.8 46.4 %copy-start.37 = (s32[8]{0:T(128)S(1)}, s32[8]{0:T(128)}, u32[]{:S(2)}) copy-start(s32[8]{0:T(128)} %param.19) | copy-start | bytes 100
  14.8 47.9 %copy-start.5 = (bf16[1,128,2048]{2,1,0:T(8,128)(2,1)S(1)}, bf16[1,128,2048]{2,1,0:T(8,128)(2,1)}, u32[]{:S(2)}) copy-start(bf16[1,128,2048]{2,1,0:T(8,128)(2,1)} %param.17) | copy-start | bytes 1572868
  14.8 736.0 %all-gather.14.cloned.1.call-start = ((), (), s32[]{:S(2)}) async-start(), calls=%async_computation.9 | async-start | bytes 34603008 | tf_op jit(solution)/shard_map/all_gather | solution.py:175
  17.6 879.9 %reduce-scatter.21.cloned.1.call-start = ((), (), s32[]{:S(2)}) async-start(), calls=%async_computation.14 | async-start | bytes 655360
  62.9 53.9 %copy-start.30 = (f32[128]{0:T(128)}, f32[128]{0:T(128)S(1)}, u32[]{:S(2)}) copy-start(f32[128]{0:T(128)S(1)} %add_rsqrt_fusion.1) | copy-start | bytes 1540
  62.9 879.0 %copy-start.25 = (f32[1,2048]{1,0:T(1,128)}, f32[1,2048]{1,0:T(1,128)S(1)}, u32[]{:S(2)}) copy-start(f32[1,2048]{1,0:T(1,128)S(1)} %get-tuple-element.232) | copy-start | bytes 24580
  138.4 24.7 copy-start.16
  185.0 17.4 copy-start.17
  202.5 777.5 %copy-start = (f32[128,2048]{1,0:T(8,128)}, f32[128,2048]{1,0:T(8,128)S(1)}, u32[]{:S(2)}) copy-start(f32[128,2048]{1,0:T(8,128)S(1)} %get-tuple-element.239) | copy-start | bytes 3145732
  202.5 598.2 %copy-start.27 = (f32[128]{0:T(128)}, f32[128]{0:T(128)S(1)}, u32[]{:S(2)}) copy-start(f32[128]{0:T(128)S(1)} %add_rsqrt_fusion) | copy-start | bytes 1540
  769.6 31.1 copy-start.13
  877.5 42.6 %reduce-scatter.19.cloned.1.call-start = ((), (), s32[]{:S(2)}) async-start(), calls=%async_computation.13 | async-start | bytes 655360
  880.9 298.6 %reduce-scatter.23.cloned.1.call-start = ((), (), s32[]{:S(2)}) async-start(), calls=%async_computation.15 | async-start | bytes 1081344
  881.2 40.2 %copy-start.6 = (bf16[1,128,2048]{2,1,0:T(8,128)(2,1)S(1)}, bf16[1,128,2048]{2,1,0:T(8,128)(2,1)}, u32[]{:S(2)}) copy-start(bf16[1,128,2048]{2,1,0:T(8,128)(2,1)} %param.17) | copy-start | bytes 1572868
  881.3 40.2 %copy-start.31 = (f32[128]{0:T(128)S(1)}, f32[128]{0:T(128)}, u32[]{:S(2)}) copy-start(f32[128]{0:T(128)} %copy-done.30) | copy-start | bytes 1540
  933.6 313.7 %reduce-scatter.15.cloned.1.call-start = ((), (), s32[]{:S(2)}) async-start(), calls=%async_computation.11 | async-start | bytes 17301504 | tf_op jit(solution)/shard_map/reduce_scatter | solution.py:270
  941.9 562.3 %reduce-scatter.13.cloned.1.call-start = ((), (), s32[]{:S(2)}) async-start(), calls=%async_computation.10 | async-start | bytes 25952256 | tf_op jit(solution)/shard_map/reduce_scatter | solution.py:269
  953.7 2154.7 %reduce-scatter.17.cloned.1.call-start = ((), (), s32[]{:S(2)}) async-start(), calls=%async_computation.12 | async-start | bytes 207618048 | tf_op jit(solution)/shard_map/reduce_scatter | solution.py:194
  955.3 24.7 copy-start.28
  1161.0 17.2 copy-start.4
  1161.0 17.2 copy-start.7
  1161.0 17.2 copy-start.24
  1161.0 17.2 copy-start.26
  1161.0 17.2 copy-start.32
  1161.1 19.3 copy-start.34
  1161.1 19.3 copy-start.36
  1178.3 325.9 %copy-start.21 = (f32[64,3072]{1,0:T(8,128)S(1)}, f32[64,3072]{1,0:T(8,128)}, u32[]{:S(2)}) copy-start(f32[64,3072]{1,0:T(8,128)} %param.21) | copy-start | bytes 2359300
  1178.3 325.9 %copy-start.23 = (f32[2,64,3072]{2,1,0:T(8,128)S(1)}, f32[2,64,3072]{2,1,0:T(8,128)}, u32[]{:S(2)}) copy-start(f32[2,64,3072]{2,1,0:T(8,128)} %param.26) | copy-start | bytes 4718596
  1180.3 326.5 %copy-start.33 = (f32[2,64]{1,0:T(2,128)}, f32[2,64]{1,0:T(2,128)S(1)}, u32[]{:S(2)}) copy-start(f32[2,64]{1,0:T(2,128)S(1)} %copy.83) | copy-start | bytes 1540
  (17 other events, 97.0 us)
Sparse Core Ops, SparseCore 0:
  11.5 98.7 all-gather.7
  113.7 82.3 all-gather.9
  199.5 354.9 all-gather.11
  557.8 192.9 all-gather.13
  877.7 19.8 reduce-scatter.20
  900.2 19.8 reduce-scatter.18
  933.7 133.4 reduce-scatter.22
  1070.2 177.0 reduce-scatter.14
  1255.4 248.6 reduce-scatter.12
  1510.4 1597.9 reduce-scatter.16
where the time goes:
time: 3150 us; the launch traced here: 3140 us
  waiting for transfers between devices  2530 us (80%)
  matrix products  295 us (9%)
  other arithmetic  187 us (6%)
  blocking collectives  83.4 us (3%)
    reduce_scatter x1, waiting for transfers between devices, shards(): lax.psum_scatter(ffn_rows(entry_two, grad_top_low, grad_gu_rows, activate...  1600 us
    all_gather x1, waiting for transfers between devices, shards(): lax.all_gather(w_gate_up.astype(jnp.bfloat16), ('dp', 'ctx', 'fsdp'), axi...  352 us
    reduce_scatter x1, waiting for transfers between devices, shards(): lax.psum_scatter(term_qkv, ('dp', 'ctx', 'fsdp'), scatter_dimension=0, ti...  253 us
    all_gather x1, waiting for transfers between devices, shards(): lax.all_gather(w_down.astype(jnp.bfloat16), ('dp', 'ctx', 'fsdp'), axis=0...  169 us
    concatenate x1, other arithmetic, ffn_rows(): jnp.concatenate([contract_rows(entry_mat, grad_gu_rows), contract_rows(gr...  133 us
    dot_general x4, matrix products, contract_rows(): lax.dot_general(left_arr, right_arr, (((0,), (0,)), ((), ())), preferred_...  89.5 us
    reduce_scatter x1, waiting for transfers between devices, shards(): lax.psum_scatter(term_out, ('dp', 'ctx', 'fsdp'), scatter_dimension=0, ti...  65.8 us
    dot_general x4, matrix products, contract_cols(): lax.dot_general(left_arr, right_arr, (((1,), (1,)), ((), ())), preferred_...  65.3 us
  transfers between devices with their start and end apart: 10, of which 9 were waited for; matrix products, arithmetic and copies ran while one was open for 11% of the time, Pallas kernels for 0%

commit v1 on v0

v1 whole, which is shorter than its diff:
```python
import functools
import math

import jax
import jax.numpy as jnp
from jax import lax
from jax.experimental import pallas as pl
from jax.experimental.pallas import tpu as pltpu
from jax.sharding import Mesh
from jax.sharding import PartitionSpec as P

MESH = pl.DeviceIdType.MESH
BF = jnp.bfloat16
F32 = jnp.float32
H = 32
KV = 8
HD = 64
FF = 8192


EPS_NORM = 1e-05
NEG_FILL = -1000000000.0
THETA = 500000.0
BETA_ONE = 0.9
BETA_TWO = 0.95
ADAM_EPS = 1e-08
DECAY_MATRIX = 0.1
LR_MATRIX = 0.01
LR_OUTPUT = 0.06
LR_GAIN = 0.3


def rope_table(positions):
    half_dim = HD // 2
    index_row = jnp.arange(half_dim, dtype=jnp.float32)
    frequency = jnp.exp(-(2.0 * index_row / HD) * math.log(THETA))
    wavelen = 2.0 * math.pi / frequency
    smooth = (8192.0 / wavelen - 1.0) / 3.0
    scaled = jnp.where(
        wavelen < 2048.0,
        frequency,
        jnp.where(
            wavelen > 8192.0,
            frequency / 32.0,
            (1.0 - smooth) * frequency / 32.0 + smooth * frequency,
        ),
    )
    angles = positions.astype(jnp.float32)[:, None] * scaled[None, :]
    cosine = jnp.cos(angles)
    sine_part = jnp.sin(angles)
    return (jnp.concatenate([cosine, cosine], 1), jnp.concatenate([sine_part, sine_part], 1))


def adamw(weight, gradient, states, step_rate, decay_rate):
    first_mom = BETA_ONE * states[0] + (1.0 - BETA_ONE) * gradient
    root_mom = jnp.sqrt(BETA_TWO * states[1] * states[1] + (1.0 - BETA_TWO) * gradient * gradient)
    first_hat = first_mom / (1.0 - BETA_ONE**3)
    root_hat = root_mom / math.sqrt(1.0 - BETA_TWO**3)
    updated = weight - step_rate * (first_hat / (root_hat + ADAM_EPS) + decay_rate * weight)
    return (updated, jnp.stack([first_mom, root_mom]))


def contract_rows(left_arr, right_arr):
    return lax.dot_general(
        left_arr, right_arr, (((0,), (0,)), ((), ())), preferred_element_type=jnp.float32
    )


def contract_cols(left_arr, right_arr):
    return lax.dot_general(
        left_arr, right_arr, (((1,), (1,)), ((), ())), preferred_element_type=jnp.float32
    )


def wrap(value, size):
    return lax.rem(value + size, size)


def remote(src, dst, send_sem, recv_sem, **where):
    return pltpu.make_async_remote_copy(
        src_ref=src,
        dst_ref=dst,
        send_sem=send_sem,
        recv_sem=recv_sem,
        device_id=where,
        device_id_type=MESH,
    )


def greet(places):
    barrier = pltpu.get_barrier_semaphore()
    for where in places:
        pl.semaphore_signal(barrier, inc=1, device_id=where, device_id_type=MESH)
    pl.semaphore_wait(barrier, len(places))


def greet_line(line, pair):
    barrier = pltpu.get_barrier_semaphore()
    here = lax.axis_index("ctx")

    @pl.when(here > 0)
    def _():
        pl.semaphore_signal(barrier, inc=1, device_id={"ctx": here - 1}, device_id_type=MESH)

    @pl.when(here < line - 1)
    def _():
        pl.semaphore_signal(barrier, inc=1, device_id={"ctx": here + 1}, device_id_type=MESH)

    if pair > 1:
        pl.semaphore_signal(
            barrier, inc=1, device_id={"core": 1 - lax.axis_index("core")}, device_id_type=MESH
        )
    ends = (here == 0).astype(jnp.int32) + (here == line - 1).astype(jnp.int32)
    pl.semaphore_wait(barrier, 2 - ends + (1 if pair > 1 else 0))


def gather_kernel(line, pair, many, *refs):
    ins, outs = refs[:many], refs[many : 2 * many]
    own_sem, line_send, line_recv, core_send, core_recv = refs[2 * many :]
    here = lax.axis_index("ctx")
    core = lax.axis_index("core")
    greet_line(line, pair)

    def hop(item, way, step, source=None):
        block = here - step if way == 0 else here + step
        target = here + 1 if way == 0 else here - 1
        place = outs[item].at[core, block]
        return remote(
            place if source is None else source,
            place,
            line_send.at[item, way, step],
            line_recv.at[item, way, step],
            ctx=target,
        )

    def arrived(item, way, step):
        block = here - 1 - step if way == 0 else here + 1 + step
        place = outs[item].at[core, block]
        return remote(
            place, place, line_send.at[item, way, step], line_recv.at[item, way, step], ctx=here
        )

    def share(item, way, step, source=None):
        block = here - 1 - step if way == 0 else here + 1 + step
        place = outs[item].at[core, block]
        return remote(
            place if source is None else source,
            place,
            core_send.at[item, way, step + 1],
            core_recv.at[item, way, step + 1],
            core=1 - core,
        )

    def shared(item, way, step):
        block = here - 1 - step if way == 0 else here + 1 + step
        place = outs[item].at[1 - core, block]
        return remote(
            place,
            place,
            core_send.at[item, way, step + 1],
            core_recv.at[item, way, step + 1],
            core=1 - core,
        )

    def sends(way):
        return here < line - 1 if way == 0 else here > 0

    def has(way, step):
        return here - 1 - step >= 0 if way == 0 else here + 1 + step <= line - 1

    for item in range(many):
        for way in range(2):

            @pl.when(sends(way))
            def _(item=item, way=way):
                hop(item, way, 0, ins[item]).start()

        if pair > 1:
            share(item, 0, -1, ins[item]).start()
        pltpu.make_async_copy(ins[item], outs[item].at[core, here], own_sem.at[item]).start()
    for step in range(line - 1):
        for item in range(many):
            for way in range(2):

                @pl.when(has(way, step))
                def _(item=item, way=way, step=step):
                    arrived(item, way, step).wait_recv()
                    if step + 1 < line - 1:

                        @pl.when(sends(way))
                        def _():
                            hop(item, way, step + 1).start()

                    if pair > 1:
                        share(item, way, step).start()

    for item in range(many):
        pltpu.make_async_copy(ins[item], outs[item].at[core, here], own_sem.at[item]).wait()
        if pair > 1:
            share(item, 0, -1, ins[item]).wait_send()
            shared(item, 0, -1).wait_recv()
        for way in range(2):

            @pl.when(sends(way))
            def _(item=item, way=way):
                hop(item, way, 0, ins[item]).wait_send()

            for step in range(line - 1):

                @pl.when(has(way, step))
                def _(item=item, way=way, step=step):
                    if step + 1 < line - 1:

                        @pl.when(sends(way))
                        def _():
                            hop(item, way, step + 1).wait_send()

                    if pair > 1:
                        share(item, way, step).wait_send()
                        shared(item, way, step).wait_recv()


def gather_tokens(sizes, collective_id, *arrays):
    line, pair = sizes["ctx"], sizes["core"]
    many = len(arrays)
    any_spec = pl.BlockSpec(memory_space=pl.ANY)
    outs = pl.pallas_call(
        functools.partial(gather_kernel, line, pair, many),
        out_shape=[jax.ShapeDtypeStruct((pair, line) + a.shape, a.dtype) for a in arrays],
        in_specs=[any_spec] * many,
        out_specs=[any_spec] * many,
        scratch_shapes=[
            pltpu.SemaphoreType.DMA((many,)),
            pltpu.SemaphoreType.DMA((many, 2, line)),
            pltpu.SemaphoreType.DMA((many, 2, line)),
            pltpu.SemaphoreType.DMA((many, 2, line)),
            pltpu.SemaphoreType.DMA((many, 2, line)),
        ],
        compiler_params=pltpu.CompilerParams(collective_id=collective_id, has_side_effects=True),
    )(*arrays)
    return [o.reshape((-1,) + a.shape[1:]) for o, a in zip(outs, arrays)]


def add_rows(rows, out_ref, *parts):
    def one(index, carry):
        at = pl.ds(pl.multiple_of(index * 16, 16), 16)
        total = parts[0][at, :].astype(F32)
        for part in parts[1:]:
            total = total + part[at, :].astype(F32)
        out_ref[at, :] = total.astype(out_ref.dtype)
        return carry

    lax.fori_loop(0, rows // 16, one, 0)


def scatter_kernel(line, pair, part_ref, out_ref, near, mine, going, landed, core_send, core_recv, line_send, line_recv):
    rows = out_ref.shape[0]
    here = lax.axis_index("ctx")
    core = lax.axis_index("core")
    greet_line(line, pair)

    def to_core(block):
        return remote(
            part_ref.at[1 - core, block],
            near.at[block],
            core_send.at[block],
            core_recv.at[block],
            core=1 - core,
        )

    def onward(way, block):
        return remote(
            going.at[way, block],
            landed.at[way, block],
            line_send.at[way, block],
            line_recv.at[way, block],
            ctx=here + 1 if way == 0 else here - 1,
        )

    order = []
    for step in range(line):
        order += [line - 1 - step, step]
    order = list(dict.fromkeys(order))
    if pair > 1:
        for block in order:
            to_core(block).start()
    ready = set()
    for step in range(line):
        for way, block in ((0, line - 1 - step), (1, step)):
            if block not in ready:
                ready.add(block)
                if pair > 1:
                    to_core(block).wait_recv()
            goes = here < block if way == 0 else here > block
            first = here == 0 if way == 0 else here == line - 1

            @pl.when(goes & first)
            def _(way=way, block=block):
                terms = [part_ref.at[core, block]] + ([near.at[block]] if pair > 1 else [])
                add_rows(rows, going.at[way, block], *terms)
                onward(way, block).start()

            @pl.when(goes & jnp.logical_not(first))
            def _(way=way, block=block):
                onward(way, block).wait_recv()
                terms = [part_ref.at[core, block]] + ([near.at[block]] if pair > 1 else [])
                add_rows(rows, going.at[way, block], *terms, landed.at[way, block])
                onward(way, block).start()

    for block in range(line):

        @pl.when(here == block)
        def _(block=block):
            terms = [part_ref.at[core, block]] + ([near.at[block]] if pair > 1 else [])
            if block > 0:
                onward(0, block).wait_recv()
                terms.append(landed.at[0, block])
            if block < line - 1:
                onward(1, block).wait_recv()
                terms.append(landed.at[1, block])
            add_rows(rows, out_ref, *terms)

    for block in range(line):
        if pair > 1:
            to_core(block).wait_send()
        for way in range(2):
            goes = here < block if way == 0 else here > block

            @pl.when(goes)
            def _(way=way, block=block):
                onward(way, block).wait_send()


def scatter_tokens(sizes, collective_id, terms):
    line, pair = sizes["ctx"], sizes["core"]
    columns = terms.shape[1]
    rows = terms.shape[0] // (line * pair)
    vmem = pl.BlockSpec(memory_space=pltpu.VMEM)
    return pl.pallas_call(
        functools.partial(scatter_kernel, line, pair),
        out_shape=jax.ShapeDtypeStruct((rows, columns), F32),
        in_specs=[vmem],
        out_specs=vmem,
        scratch_shapes=[
            pltpu.VMEM((line, rows, columns), BF),
            pltpu.VMEM((8, 128), F32),
            pltpu.VMEM((2, line, rows, columns), BF),
            pltpu.VMEM((2, line, rows, columns), BF),
            pltpu.SemaphoreType.DMA((line,)),
            pltpu.SemaphoreType.DMA((line,)),
            pltpu.SemaphoreType.DMA((2, line)),
            pltpu.SemaphoreType.DMA((2, line)),
        ],
        compiler_params=pltpu.CompilerParams(
            collective_id=collective_id, has_side_effects=True, vmem_limit_bytes=50 * 2**20
        ),
    )(terms.reshape(pair, line, rows, columns))


def blocks_in_order(line, pair):
    away = sorted(range(line), key=lambda d: min(d, line - d))
    return [(dz, dc) for dz in away for dc in range(pair)]


def greet_all(sizes):
    names = ("dp", "ctx", "x", "core")
    at = {name: lax.axis_index(name) for name in names}
    places = []
    for dz, dc in blocks_in_order(sizes["ctx"], sizes["core"]):
        if dz or dc:
            places.append(
                {"ctx": wrap(at["ctx"] + dz, sizes["ctx"]), "core": wrap(at["core"] + dc, sizes["core"])}
            )
    for name in ("dp", "x"):
        for step in range(1, sizes[name]):
            places.append({name: wrap(at[name] + step, sizes[name])})
    greet(places)


def spread_kernel(sizes, w_ref, o_ref, own_sem, f_send, f_recv, a_send, a_recv, b_send, b_recv):
    line, pair = sizes["ctx"], sizes["core"]
    at = {name: lax.axis_index(name) for name in ("dp", "ctx", "x", "core")}
    greet_all(sizes)
    order = blocks_in_order(line, pair)

    def first(index):
        dz, dc = order[index]
        z, c = wrap(at["ctx"] + dz, line), wrap(at["core"] + dc, pair)
        return remote(
            w_ref.at[z * pair + c],
            o_ref.at[at["dp"], at["ctx"], at["x"], at["core"]],
            f_send.at[index],
            f_recv.at[index],
            ctx=z,
            core=c,
        )

    def place(index, moved):
        dz, dc = order[index]
        z, c = wrap(at["ctx"] - dz, line), wrap(at["core"] - dc, pair)
        spot = {name: wrap(at[name] - moved.get(name, 0), sizes[name]) for name in ("dp", "x")}
        return o_ref.at[spot["dp"], z, spot["x"], c]

    def came(index):
        spot = place(index, {})
        return remote(spot, spot, f_send.at[index], f_recv.at[index], core=at["core"])

    def axes(index):
        dz, dc = order[index]
        return ("x", "dp") if (dz + dc) % 2 == 0 else ("dp", "x")

    def hop_one(index, step):
        name = axes(index)[0]
        spot = place(index, {})
        return remote(
            spot,
            spot,
            a_send.at[index, step],
            a_recv.at[index, step],
            **{name: wrap(at[name] + step, sizes[name])},
        )

    def one_came(index, step):
        name = axes(index)[0]
        spot = place(index, {name: step})
        return remote(spot, spot, a_send.at[index, step], a_recv.at[index, step], core=at["core"])

    def hop_two(index, step, far):
        name, other = axes(index)
        spot = place(index, {name: step})
        return remote(
            spot,
            spot,
            b_send.at[index, step, far],
            b_recv.at[index, step, far],
            **{other: wrap(at[other] + far, sizes[other])},
        )

    def two_came(index, step, far):
        name, other = axes(index)
        spot = place(index, {name: step, other: far})
        return remote(
            spot, spot, b_send.at[index, step, far], b_recv.at[index, step, far], core=at["core"]
        )

    own = pltpu.make_async_copy(
        w_ref.at[at["ctx"] * pair + at["core"]],
        o_ref.at[at["dp"], at["ctx"], at["x"], at["core"]],
        own_sem,
    )
    own.start()
    for index in range(1, len(order)):
        first(index).start()
    late = 2
    for tick in range(len(order) + late):
        if tick < len(order):
            if tick == 0:
                own.wait()
            else:
                came(tick).wait_recv()
            name, other = axes(tick)
            for step in range(1, sizes[name]):
                hop_one(tick, step).start()
            for far in range(1, sizes[other]):
                hop_two(tick, 0, far).start()
        if tick >= late:
            index = tick - late
            name, other = axes(index)
            for step in range(1, sizes[name]):
                one_came(index, step).wait_recv()
                for far in range(1, sizes[other]):
                    hop_two(index, step, far).start()
    for index in range(len(order)):
        if index:
            first(index).wait_send()
        name, other = axes(index)
        for step in range(sizes[name]):
            if step:
                hop_one(index, step).wait_send()
            for far in range(1, sizes[other]):
                hop_two(index, step, far).wait_send()
                two_came(index, step, far).wait_recv()


def spread_weights(sizes, collective_id, packed):
    group, rows, columns = packed.shape
    steps = max(sizes["dp"], sizes["x"])
    any_spec = pl.BlockSpec(memory_space=pl.ANY)
    out = pl.pallas_call(
        functools.partial(spread_kernel, sizes),
        out_shape=jax.ShapeDtypeStruct(
            (sizes["dp"], sizes["ctx"], sizes["x"], sizes["core"], rows, columns), packed.dtype
        ),
        in_specs=[any_spec],
        out_specs=any_spec,
        scratch_shapes=[
            pltpu.SemaphoreType.DMA,
            pltpu.SemaphoreType.DMA((group,)),
            pltpu.SemaphoreType.DMA((group,)),
            pltpu.SemaphoreType.DMA((group, steps)),
            pltpu.SemaphoreType.DMA((group, steps)),
            pltpu.SemaphoreType.DMA((group, steps, steps)),
            pltpu.SemaphoreType.DMA((group, steps, steps)),
        ],
        compiler_params=pltpu.CompilerParams(collective_id=collective_id, has_side_effects=True),
    )(packed)
    return out.reshape(-1, columns)


def collect_kernel(
    sizes, g_ref, o_ref, near_a, near_b, part, far_in, done, own_sem, a_send, a_recv, b_send, b_recv, f_send, f_recv
):
    line, pair = sizes["ctx"], sizes["core"]
    rows = o_ref.shape[1]
    at = {name: lax.axis_index(name) for name in ("dp", "ctx", "x", "core")}
    greet_all(sizes)
    order = blocks_in_order(line, pair)[::-1]
    me = at["ctx"] * pair + at["core"]

    def spot_of(index):
        dz, dc = order[index]
        return wrap(at["ctx"] + dz, line), wrap(at["core"] + dc, pair)

    def axes(index):
        dz, dc = order[index]
        return ("dp", "x") if (dz + dc) % 2 == 0 else ("x", "dp")

    def landing(index, step):
        slot = sum(axes(i)[0] == axes(index)[0] for i in range(index))
        return (near_a if axes(index)[0] == "dp" else near_b).at[slot, step - 1]

    def terms(index, first_at):
        z, c = spot_of(index)
        if axes(index)[0] == "dp":
            return g_ref.at[first_at, z, :, c]
        return g_ref.at[:, z, first_at, c]

    def hop_one(index, step):
        name = axes(index)[0]
        to = wrap(at[name] + step, sizes[name])
        return remote(
            terms(index, to), landing(index, step), a_send.at[index, step], a_recv.at[index, step], **{name: to}
        )

    def hop_two(index, far):
        other = axes(index)[1]
        to = wrap(at[other] + far, sizes[other])
        return remote(
            part.at[index, to], far_in.at[index, far - 1], b_send.at[index, far], b_recv.at[index, far], **{other: to}
        )

    def last(index):
        z, c = spot_of(index)
        return remote(done.at[index], o_ref.at[me], f_send.at[index], f_recv.at[index], ctx=z, core=c)

    def last_came(index):
        dz, dc = order[index]
        z, c = wrap(at["ctx"] - dz, line), wrap(at["core"] - dc, pair)
        spot = o_ref.at[z * pair + c]
        return remote(spot, spot, f_send.at[index], f_recv.at[index], core=at["core"])

    own = pltpu.make_async_copy(done.at[len(order) - 1], o_ref.at[me], own_sem)
    for index in range(len(order)):
        name = axes(index)[0]
        for step in range(1, sizes[name]):
            hop_one(index, step).start()
    late = 2
    for tick in range(len(order) + late):
        if tick < len(order):
            name, other = axes(tick)
            for step in range(1, sizes[name]):
                hop_one(tick, step).wait_recv()
            kept = terms(tick, at[name])
            for place in range(sizes[other]):
                add_rows(
                    rows,
                    part.at[tick, place],
                    kept.at[place],
                    *[landing(tick, step).at[place] for step in range(1, sizes[name])],
                )
            for far in range(1, sizes[other]):
                hop_two(tick, far).start()
        if tick >= late:
            index = tick - late
            other = axes(index)[1]
            for far in range(1, sizes[other]):
                hop_two(index, far).wait_recv()
            add_rows(
                rows,
                done.at[index],
                part.at[index, at[other]],
                *[far_in.at[index, far - 1] for far in range(1, sizes[other])],
            )
            if index < len(order) - 1:
                last(index).start()
            else:
                own.start()
    for index in range(len(order)):
        name, other = axes(index)
        for step in range(1, sizes[name]):
            hop_one(index, step).wait_send()
        for far in range(1, sizes[other]):
            hop_two(index, far).wait_send()
        if index < len(order) - 1:
            last(index).wait_send()
            last_came(index).wait_recv()
    own.wait()


def collect_grads(sizes, collective_id, grads):
    columns = grads.shape[1]
    group = sizes["ctx"] * sizes["core"]
    rows = grads.shape[0] // (group * sizes["dp"] * sizes["x"])
    steps = max(sizes["dp"], sizes["x"])
    half = (group + 1) // 2
    return pl.pallas_call(
        functools.partial(collect_kernel, sizes),
        out_shape=jax.ShapeDtypeStruct((group, rows, columns), BF),
        in_specs=[pl.BlockSpec(memory_space=pltpu.VMEM)],
        out_specs=pl.BlockSpec(memory_space=pl.ANY),
        scratch_shapes=[
            pltpu.VMEM((half, max(1, sizes["dp"] - 1), sizes["x"], rows, columns), BF),
            pltpu.VMEM((half, max(1, sizes["x"] - 1), sizes["dp"], rows, columns), BF),
            pltpu.VMEM((group, steps, rows, columns), BF),
            pltpu.VMEM((group, max(1, steps - 1), rows, columns), BF),
            pltpu.VMEM((group, rows, columns), BF),
            pltpu.SemaphoreType.DMA,
            pltpu.SemaphoreType.DMA((group, steps)),
            pltpu.SemaphoreType.DMA((group, steps)),
            pltpu.SemaphoreType.DMA((group, steps)),
            pltpu.SemaphoreType.DMA((group, steps)),
            pltpu.SemaphoreType.DMA((group,)),
            pltpu.SemaphoreType.DMA((group,)),
        ],
        compiler_params=pltpu.CompilerParams(
            collective_id=collective_id, has_side_effects=True, vmem_limit_bytes=58 * 2**20
        ),
    )(grads.reshape(sizes["dp"], sizes["ctx"], sizes["x"], sizes["core"], rows, columns))


def turned(values):
    half_dim = values.shape[-1] // 2
    return jnp.concatenate([-values[..., half_dim:], values[..., :half_dim]], -1)


def turned_back(values):
    half_dim = values.shape[-1] // 2
    return jnp.concatenate([values[..., half_dim:], -values[..., :half_dim]], -1)


def norm_back(grad_entry, normed, inverse, gain):
    grad_gain = jnp.sum(grad_entry * normed, 0)
    grad_normed = grad_entry * gain
    grad_rows = inverse * (grad_normed - normed * jnp.mean(grad_normed * normed, -1, keepdims=True))
    return (grad_rows, grad_gain)


def dot(left, right):
    return jnp.dot(left, right, preferred_element_type=F32)


def split_columns(array, group, sections):
    rows = array.shape[0]
    pieces, start = [], 0
    for width in sections:
        piece = array[:, start : start + width].reshape(rows, group, width // group)
        pieces.append(piece.transpose(1, 0, 2))
        start += width
    return jnp.concatenate(pieces, 2)


def shards(
    sizes,
    hidden,
    cotangent,
    span_order,
    norm_gains,
    w_qkv,
    w_out,
    w_gate_up,
    w_down,
    mom_gains,
    mom_qkv,
    mom_out,
    mom_gate_up,
    mom_down,
):
    everyone = ("dp", "ctx", "x", "core")
    line, pair = sizes["ctx"], sizes["core"]
    group = line * pair
    block_rows, width = hidden.shape[1:]
    total_rows = block_rows * line
    span_rows = total_rows // span_order.shape[0]
    heads, kv_heads = H // group, KV // group
    ratio = heads // kv_heads
    query_cols, kv_cols, unit_cols = heads * HD, kv_heads * HD, FF // group
    scale = HD ** (-0.5)
    key_pos = (
        span_order[:, None] * span_rows + jnp.arange(span_rows, dtype=jnp.int32)[None, :]
    ).reshape(-1)
    visible = key_pos[None, :] <= key_pos[:, None]
    cos_tab, sin_tab = rope_table(key_pos)
    cos_tab, sin_tab = cos_tab[None, :, None, :], sin_tab[None, :, None, :]

    packed = jnp.concatenate(
        [
            split_columns(w_qkv.astype(BF), group, (H * HD, KV * HD, KV * HD)),
            split_columns(w_out.astype(BF), group, (H * HD,)),
            split_columns(w_gate_up.astype(BF), group, (FF, FF)),
            split_columns(w_down.astype(BF), group, (FF,)),
        ],
        2,
    )
    qkv_width = query_cols + 2 * kv_cols
    ends = [qkv_width, qkv_width + query_cols, qkv_width + query_cols + 2 * unit_cols]
    gains_c = lax.all_gather(norm_gains.astype(BF), everyone, axis=1, tiled=True)
    weights = spread_weights(sizes, 0, packed)
    qkv_c = weights[:, : ends[0]]
    out_c = weights[:, ends[0] : ends[1]]
    gate_up_c = weights[:, ends[1] : ends[2]]
    down_c = weights[:, ends[2] :]

    gain_one = gains_c[0].astype(F32)
    gain_two = gains_c[1].astype(F32)
    row_in = hidden[0].astype(F32)
    inv_one = lax.rsqrt(jnp.mean(row_in * row_in, -1, keepdims=True) + EPS_NORM)
    normed_one = row_in * inv_one
    entry_one, cot = gather_tokens(
        sizes, 1, (normed_one * gain_one).astype(BF), cotangent[0]
    )

    projected = dot(entry_one, qkv_c).reshape(pair, total_rows, qkv_width)
    queries = projected[..., :query_cols].reshape(pair, total_rows, heads, HD)
    key_rows = projected[..., query_cols : query_cols + kv_cols].reshape(
        pair, total_rows, kv_heads, HD
    )
    value_rows = projected[..., query_cols + kv_cols :].reshape(pair, total_rows, kv_heads, HD)
    queries = (queries * cos_tab + turned(queries) * sin_tab).astype(BF)
    key_rows = (key_rows * cos_tab + turned(key_rows) * sin_tab).astype(BF)
    value_rows = value_rows.astype(BF)
    queries = queries.reshape(pair, total_rows, kv_heads, ratio, HD)

    def product(spec, left, right):
        return jnp.einsum(spec, left, right, preferred_element_type=F32)

    scores = product("stkgd,sukd->skgtu", queries, key_rows) * scale
    scores = jnp.where(visible, scores, NEG_FILL)
    top_score = jnp.max(scores, -1, keepdims=True)
    exponent = jnp.exp(scores - top_score)
    probability = exponent / jnp.sum(exponent, -1, keepdims=True)
    prob_low = probability.astype(BF)
    attended = product("skgtu,sukd->stkgd", prob_low, value_rows).astype(BF)
    attended = attended.reshape(pair * total_rows, query_cols)

    middle = row_in + scatter_tokens(sizes, 2, contract_cols(attended, out_c).astype(BF))
    inv_two = lax.rsqrt(jnp.mean(middle * middle, -1, keepdims=True) + EPS_NORM)
    normed_two = middle * inv_two
    (entry_two,) = gather_tokens(sizes, 3, (normed_two * gain_two).astype(BF))

    gate_up = dot(entry_two, gate_up_c)
    gate_part = gate_up[:, :unit_cols]
    up_part = gate_up[:, unit_cols:]
    sigmoid_gate = jax.nn.sigmoid(gate_part)
    silu_gate = gate_part * sigmoid_gate
    activated = (silu_gate * up_part).astype(BF)
    summed = scatter_tokens(sizes, 4, contract_cols(activated, down_c).astype(BF))
    output = (middle + summed).astype(BF)[None]
    grad_act = dot(cot, down_c)
    grad_gate = grad_act * up_part * sigmoid_gate * (1.0 + gate_part * (1.0 - sigmoid_gate))
    grad_up = grad_act * silu_gate
    grad_gu = jnp.concatenate([grad_gate, grad_up], 1).astype(BF)
    grad_entry_two = scatter_tokens(sizes, 5, contract_cols(grad_gu, gate_up_c).astype(BF))
    grad_top = cotangent[0].astype(F32)
    grad_mid_norm, grad_gain_two = norm_back(grad_entry_two, normed_two, inv_two, gain_two)
    grad_middle = grad_top + grad_mid_norm
    (grad_branch,) = gather_tokens(sizes, 6, grad_middle.astype(BF))

    grad_attended = dot(grad_branch, out_c).astype(BF)
    grad_heads = grad_attended.reshape(pair, total_rows, kv_heads, ratio, HD)
    grad_prob = product("stkgd,sukd->skgtu", grad_heads, value_rows)
    delta_row = jnp.sum(probability * grad_prob, -1, keepdims=True)
    grad_scores = jnp.where(visible, probability * (grad_prob - delta_row), 0.0).astype(BF)
    grad_queries = product("skgtu,sukd->stkgd", grad_scores, key_rows) * scale
    grad_keys = product("skgtu,stkgd->sukd", grad_scores, queries) * scale
    grad_values = product("skgtu,stkgd->sukd", prob_low, grad_heads)
    grad_queries = grad_queries.reshape(pair, total_rows, heads, HD)
    grad_queries = grad_queries * cos_tab + turned_back(grad_queries * sin_tab)
    grad_keys = grad_keys * cos_tab + turned_back(grad_keys * sin_tab)
    grad_projected = jnp.concatenate(
        [
            grad_queries.reshape(-1, query_cols),
            grad_keys.reshape(-1, kv_cols),
            grad_values.reshape(-1, kv_cols),
        ],
        1,
    ).astype(BF)
    grad_entry_one = scatter_tokens(sizes, 7, contract_cols(grad_projected, qkv_c).astype(BF))
    grad_row_norm, grad_gain_one = norm_back(grad_entry_one, normed_one, inv_one, gain_one)
    grad_hidden = (grad_middle + grad_row_norm).astype(BF)[None]

    terms = jnp.concatenate(
        [
            contract_rows(entry_one, grad_projected).astype(BF),
            contract_rows(grad_branch, attended).astype(BF),
            contract_rows(entry_two, grad_gu).astype(BF),
            contract_rows(cot, activated).astype(BF),
        ],
        1,
    )
    grads = collect_grads(sizes, 8, terms).astype(F32)
    grad_gains = lax.psum_scatter(
        jnp.stack([grad_gain_one, grad_gain_two]), everyone, scatter_dimension=1, tiled=True
    )

    def joined(*bounds):
        return jnp.concatenate(
            [
                grads[:, :, low:high].transpose(1, 0, 2).reshape(grads.shape[1], -1)
                for low, high in zip(bounds[:-1], bounds[1:])
            ],
            1,
        )

    grad_qkv = joined(0, query_cols, query_cols + kv_cols, ends[0])
    grad_out = joined(ends[0], ends[1])
    grad_gate_up = joined(ends[1], ends[1] + unit_cols, ends[2])
    grad_down = joined(ends[2], ends[2] + unit_cols)
    new_gains, new_mom_gains = adamw(norm_gains, grad_gains, mom_gains, LR_GAIN, 0.0)
    new_qkv, new_mom_qkv = adamw(w_qkv, grad_qkv, mom_qkv, LR_MATRIX, DECAY_MATRIX)
    new_out, new_mom_out = adamw(w_out, grad_out, mom_out, LR_OUTPUT, DECAY_MATRIX)
    new_gate_up, new_mom_gate_up = adamw(
        w_gate_up, grad_gate_up, mom_gate_up, LR_MATRIX, DECAY_MATRIX
    )
    new_down, new_mom_down = adamw(w_down, grad_down, mom_down, LR_MATRIX, DECAY_MATRIX)
    return (
        output,
        grad_hidden,
        grad_gains,
        grad_qkv,
        grad_out,
        grad_gate_up,
        grad_down,
        new_gains,
        new_qkv,
        new_out,
        new_gate_up,
        new_down,
        new_mom_gains,
        new_mom_qkv,
        new_mom_out,
        new_mom_gate_up,
        new_mom_down,
    )


def solution(mesh):
    shape = dict(mesh.shape)
    pair = 2 if shape["ctx"] * 2 <= KV and shape["fsdp"] % 2 == 0 else 1
    sizes = {"dp": shape["dp"], "ctx": shape["ctx"], "x": shape["fsdp"] // pair, "core": pair}
    finer = Mesh(mesh.devices.reshape(tuple(sizes.values())), tuple(sizes))
    tokens = P(("dp", "x", "core"), "ctx", None)
    everyone = ("dp", "ctx", "x", "core")
    rows, gains = P(everyone, None), P(None, everyone)
    row_moments, gain_moments = P(None, everyone, None), P(None, None, everyone)
    weights = (gains, rows, rows, rows, rows)
    moments = (gain_moments, row_moments, row_moments, row_moments, row_moments)
    return jax.shard_map(
        functools.partial(shards, sizes),
        mesh=finer,
        in_specs=(tokens, tokens, P()) + weights + moments,
        out_specs=(tokens, tokens) + weights + weights + moments,
        check_vma=False,
    )
```

time: 3150 us -> 1030 us (0.33)
  waiting for transfers between devices: 2530 us -> 0.02 us
  Pallas kernels: 0 us -> 704 us
  matrix products: 295 us -> 105 us
  other arithmetic: 187 us -> 63 us
  local copies, waits for them, and re-layouts: 24.4 us -> 99 us
  blocking collectives: 83.4 us -> 43 us
    reduce_scatter x3 -> x0, waiting for transfers between devices: 1920 us -> none  [the longest x1 1600 us: shards(): lax.psum_scatter(ffn_rows(entry_two, grad_top_low, grad_gu_rows, activate...]
    pallas_call x0 -> x9, Pallas kernels: none -> 704 us  [the longest x4 229 us: scatter_tokens(): pl.pallas_call(functools.partial(scatter_kernel, line, pair), out_shape=j...]
    all_gather x4 -> x0, waiting for transfers between devices: 579 us -> none  [the longest x1 352 us: shards(): lax.all_gather(w_gate_up.astype(jnp.bfloat16), ('dp', 'ctx', 'fsdp'), axi...]
    concatenate x5 -> x3, other arithmetic: 133 us -> 7.23 us  [the longest x1 7.14 us: shards(): jnp.concatenate([contract_rows(entry_one, grad_projected).astype(BF), con...]
    dot_general x60 -> x10, matrix products: 140 us -> 46.8 us  [the longest x4 30.4 us: dot(): return jnp.dot(left, right, preferred_element_type=F32)]
    dot_general x4, matrix products: 89.5 us -> 24.7 us  [contract_rows(): lax.dot_general(left_arr, right_arr, (((0,), (0,)), ((), ())), preferred_...]
    all_gather x3 -> x1, blocking collectives: 83.4 us -> 43 us  [shards(): lax.all_gather(norm_gains.astype(BF), everyone, axis=1, tiled=True)]
    unnamed x13 -> x2, waiting for transfers between devices: 35.9 us -> 0.02 us
  transfers between devices with their start and end apart: 10 -> 1, of which waited for: 9 -> 0; matrix products, arithmetic and copies ran while one was open for 11% -> 14% of each run, Pallas kernels for 0% -> 23%
where the time goes in v1:
time: 1030 us
  Pallas kernels  704 us (68%)
  matrix products  105 us (10%)
  local copies, waits for them, and re-layouts  99 us (10%)
  other arithmetic  63 us (6%)
  blocking collectives  43 us (4%)
  between operations  15.4 us (1%)
    pallas_call x4, Pallas kernels, scatter_tokens(): pl.pallas_call(functools.partial(scatter_kernel, line, pair), out_shape=j...  229 us
    pallas_call x1, Pallas kernels, collect_grads(): pl.pallas_call(functools.partial(collect_kernel, sizes), out_shape=jax.Sh...  178 us
    pallas_call x3, Pallas kernels, gather_tokens(): pl.pallas_call(functools.partial(gather_kernel, line, pair, many), out_sh...  154 us
    pallas_call x1, Pallas kernels, spread_weights(): pl.pallas_call(functools.partial(spread_kernel, sizes), out_shape=jax.Sha...  142 us
    all_gather x1, blocking collectives, shards(): lax.all_gather(norm_gains.astype(BF), everyone, axis=1, tiled=True)  43 us
    dot_general x4, matrix products, contract_cols(): lax.dot_general(left_arr, right_arr, (((1,), (1,)), ((), ())), preferred_...  33.1 us
    dot_general x4, matrix products, dot(): return jnp.dot(left, right, preferred_element_type=F32)  30.4 us
    dot_general x4, matrix products, contract_rows(): lax.dot_general(left_arr, right_arr, (((0,), (0,)), ((), ())), preferred_...  24.7 us
  transfers between devices with their start and end apart: 1, of which 0 were waited for; matrix products, arithmetic and copies ran while one was open for 14% of the time, Pallas kernels for 23%

profile of v1, /device:TPU:0, one launch (start us, length us, event | category | flops | bytes accessed | tf_op | source)
XLA Modules:
  0.0 1028.8 jit_solution(11249868935986791898)
XLA Ops:
  13.1 43.0 %all-gather = bf16[32,64,2]{1,2,0:T(2,128)(2,1)S(1)} all-gather(bf16[1,64,2]{1,2,0:T(2,128)(2,1)S(1)} %convert_bitcast_fusion), channel_id=1, replica_groups=mesh['dp'=2,'ctx'=4,'x'=2,'core'=2] {'dp','ctx','x','core'}, dimensions={0}, use_global_device_ids=true | all-gather | bytes 8448 | tf_op jit(solution)/shard_map/all_gather | solution.py:716
  62.9 5.9 concatenate.102.w_ref
  68.8 142.0 %shard_map.261 = bf16[2,4,2,2,64,3712]{5,4,3,2,1,0:T(8,128)(2,1)} custom-call(bf16[8,64,3712]{2,1,0:T(8,128)(2,1)} %concatenate.102.w_ref), custom_call_target="tpu_custom_call" | custom-call | tf_op jit(solution)/shard_map/pallas_call | solution.py:489
  211.8 72.5 %shard_map.260 = (bf16[2,4,128,2048]{3,2,1,0:T(8,128)(2,1)}, bf16[2,4,128,2048]{3,2,1,0:T(8,128)(2,1)}) custom-call(bf16[128,2048]{1,0:T(8,128)(2,1)} %fusion.65.refs_0_, bf16[128,2048]{1,0:T(8,128)(2,1)} %bitcast.341), custom_call_target="tpu_custom_call" | custom-call | tf_op jit(solution)/shard_map/pallas_call | solution.py:227
  284.3 4.5 fusion.42
  299.1 4.6 convolution_convert_fusion.2
  303.6 55.3 %shard_map.262 = f32[128,2048]{1,0:T(8,128)S(1)} custom-call(bf16[2,4,128,2048]{3,2,1,0:T(8,128)(2,1)} %bitcast.326), custom_call_target="tpu_custom_call" | custom-call | tf_op jit(solution)/shard_map/pallas_call | solution.py:339
  360.3 41.5 %shard_map.263 = bf16[2,4,128,2048]{3,2,1,0:T(8,128)(2,1)} custom-call(bf16[128,2048]{1,0:T(8,128)(2,1)} %multiply_convert_fusion.3.refs_0_), custom_call_target="tpu_custom_call" | custom-call | tf_op jit(solution)/shard_map/pallas_call | solution.py:227
  401.7 12.6 %fusion.8 = f32[1024,2048]{1,0:T(8,128)S(1)} fusion(bf16[1024,2048]{1,0:T(8,128)(2,1)} %bitcast.349, bf16[2048,3712]{1,0:T(8,128)(2,1)} %bitcast.329), kind=kOutput, calls=%fused_computation.15 | convolution fusion | flops 8589934592 | bytes 20971520 | tf_op jit(solution)/shard_map/dot_general | solution.py:659
  414.4 9.6 multiply_convert_fusion.1
  424.0 14.1 %fusion.26 = bf16[1024,2048]{1,0:T(8,128)(2,1)} fusion(bf16[2048,3712]{1,0:T(8,128)(2,1)} %bitcast.331, bf16[1024,1024]{1,0:T(8,128)(2,1)S(1)} %get-tuple-element.30, bf16[1024,1024]{1,0:T(8,128)(2,1)S(1)} %get-tuple-element.29), kind=kOutput, calls=%fused_computation.48 | convolution fusion | flops 8600420352 | bytes 16777216 | tf_op jit(solution)/shard_map/dot_general | solution.py:70
  438.1 55.4 %shard_map.265 = f32[128,2048]{1,0:T(8,128)S(1)} custom-call(bf16[2,4,128,2048]{3,2,1,0:T(8,128)(2,1)} %bitcast.343), custom_call_target="tpu_custom_call" | custom-call | tf_op jit(solution)/shard_map/pallas_call | solution.py:339
  496.2 40.2 %shard_map.266 = bf16[2,4,128,2048]{3,2,1,0:T(8,128)(2,1)} custom-call(bf16[128,2048]{1,0:T(8,128)(2,1)} %fusion.114.refs_0_), custom_call_target="tpu_custom_call" | custom-call | tf_op jit(solution)/shard_map/pallas_call | solution.py:227
  536.4 3.7 convolution_convert_fusion.7
  541.2 4.9 fusion.62
  546.2 5.2 fusion
  552.2 2.9 fusion.19
  560.3 6.0 convolution_convert_fusion.1
  566.3 55.7 %shard_map.267 = f32[128,2048]{1,0:T(8,128)S(1)} custom-call(bf16[2,4,128,2048]{3,2,1,0:T(8,128)(2,1)} %bitcast.344), custom_call_target="tpu_custom_call" | custom-call | tf_op jit(solution)/shard_map/pallas_call | solution.py:339
  623.9 9.6 convolution_convert_fusion.3
  633.5 8.4 convolution_convert_fusion.4
  641.9 12.0 %convolution_convert_fusion = bf16[2048,2048]{0,1:T(8,128)(2,1)S(1)} fusion(bf16[1024,2048]{1,0:T(8,128)(2,1)S(1)} %bitcast.350, bf16[1024,1024]{1,0:T(8,128)(2,1)} %copy-done.71, bf16[1024,1024]{1,0:T(8,128)(2,1)} %copy-done.70), kind=kOutput, calls=%fused_computation.10 | convolution fusion | flops 8602517504 | bytes 16777216 | tf_op jit(solution)/shard_map/dot_general | solution.py:64
  658.5 7.1 pad_maximum_fusion
  665.6 19.0 %copy.103 = bf16[2048,3712]{1,0:T(8,128)(2,1)} copy(bf16[2048,3712]{0,1:T(8,128)(2,1)} %pad_maximum_fusion) | data formatting | bytes 30408704 | tf_op jit(solution)/shard_map/concatenate | solution.py:801
  684.6 178.4 %shard_map.268 = bf16[8,64,3712]{2,1,0:T(8,128)(2,1)} custom-call(bf16[2,4,2,2,64,3712]{5,4,3,2,1,0:T(8,128)(2,1)} %bitcast.323), custom_call_target="tpu_custom_call" | custom-call | tf_op jit(solution)/shard_map/pallas_call | solution.py:616
  865.7 3.1 copy-done.3
  874.2 8.0 slice_bitcast_fusion.1
  882.2 62.7 %shard_map.264 = f32[128,2048]{1,0:T(8,128)S(1)} custom-call(bf16[2,4,128,2048]{3,2,1,0:T(8,128)(2,1)} %bitcast.342), custom_call_target="tpu_custom_call" | custom-call | tf_op jit(solution)/shard_map/pallas_call | solution.py:339
  980.2 4.1 copy.108
  989.9 5.4 multiply_subtract_fusion.1
  1002.8 4.6 multiply_subtract_fusion
  1014.7 4.0 pad_maximum_fusion.1
  (272 shorter events, 107.1 us)
Async XLA Ops:
  7.2 51.1 %copy-start.11 = (f32[64,8192]{1,0:T(8,128)S(1)}, f32[64,8192]{1,0:T(8,128)}, u32[]{:S(2)}) copy-start(f32[64,8192]{1,0:T(8,128)} %param.20) | copy-start | bytes 6291460
  7.2 1012.5 %reduce-scatter.4.cloned.1.call-start = ((), (), s32[]{:S(2)}) async-start(), calls=%async_computation.1 | async-start | bytes 1081344
  56.2 154.6 %copy-start.49 = (f32[1,2048]{1,0:T(1,128)}, f32[1,2048]{1,0:T(1,128)S(1)}, u32[]{:S(2)}) copy-start(f32[1,2048]{1,0:T(1,128)S(1)} %get-tuple-element.69) | copy-start | bytes 24580
  56.2 438.3 %copy-start.45 = (f32[1,2048]{1,0:T(1,128)}, f32[1,2048]{1,0:T(1,128)S(1)}, u32[]{:S(2)}) copy-start(f32[1,2048]{1,0:T(1,128)S(1)} %get-tuple-element.68) | copy-start | bytes 24580
  68.8 142.0 %copy-start.8 = (bf16[1,128,2048]{2,1,0:T(8,128)(2,1)S(1)}, bf16[1,128,2048]{2,1,0:T(8,128)(2,1)}, u32[]{:S(2)}) copy-start(bf16[1,128,2048]{2,1,0:T(8,128)(2,1)} %param.13) | copy-start | bytes 1572868
  68.8 142.0 %copy-start.59 = (f32[128]{0:T(128)S(1)}, f32[128]{0:T(128)}, u32[]{:S(2)}) copy-start(f32[128]{0:T(128)} %add_rsqrt_fusion.1) | copy-start | bytes 1540
  359.1 135.4 %copy-start.4 = (f32[128,2048]{1,0:T(8,128)}, f32[128,2048]{1,0:T(8,128)S(1)}, u32[]{:S(2)}) copy-start(f32[128,2048]{1,0:T(8,128)S(1)} %get-tuple-element.26) | copy-start | bytes 3145732
  359.1 135.4 %copy-start.57 = (f32[128]{0:T(128)}, f32[128]{0:T(128)S(1)}, u32[]{:S(2)}) copy-start(f32[128]{0:T(128)S(1)} %add_rsqrt_fusion) | copy-start | bytes 1540
  401.7 12.7 %copy-start.68 = (bf16[2,4,128,2048]{3,2,1,0:T(8,128)(2,1)S(1)}, bf16[2,4,128,2048]{3,2,1,0:T(8,128)(2,1)}, u32[]{:S(2)}) copy-start(bf16[2,4,128,2048]{3,2,1,0:T(8,128)(2,1)} %get-tuple-element.20) | copy-start | bytes 12582916
  424.0 14.1 %copy-start.70 = (bf16[1024,1024]{1,0:T(8,128)(2,1)}, bf16[1024,1024]{1,0:T(8,128)(2,1)S(1)}, u32[]{:S(2)}) copy-start(bf16[1024,1024]{1,0:T(8,128)(2,1)S(1)} %get-tuple-element.29) | copy-start | bytes 6291460
  424.0 14.1 %copy-start.71 = (bf16[1024,1024]{1,0:T(8,128)(2,1)}, bf16[1024,1024]{1,0:T(8,128)(2,1)S(1)}, u32[]{:S(2)}) copy-start(bf16[1024,1024]{1,0:T(8,128)(2,1)S(1)} %get-tuple-element.30) | copy-start | bytes 6291460
  438.1 57.0 %copy-start.20 = (bf16[1,128,2048]{2,1,0:T(8,128)(2,1)S(1)}, bf16[1,128,2048]{2,1,0:T(8,128)(2,1)}, u32[]{:S(2)}) copy-start(bf16[1,128,2048]{2,1,0:T(8,128)(2,1)} %param.14) | copy-start | bytes 1572868
  541.2 10.9 %slice-start = ((s8[8388608]{0:T(1024)(128)(4,1)}), s8[4194304]{0:T(1024)(128)(4,1)S(1)}, s32[]{:S(2)}) async-start(s8[8388608]{0:T(1024)(128)(4,1)} %bitcast.321), calls=%async_computation.2 | async-start | bytes 8388608
  546.2 5.9 slice-start.1
  552.1 8.2 copy-start.51
  560.3 6.0 copy-start.38
  566.3 55.8 %copy-start.50 = (f32[1,2048]{1,0:T(1,128)S(1)}, f32[1,2048]{1,0:T(1,128)}, u32[]{:S(2)}) copy-start(f32[1,2048]{1,0:T(1,128)} %copy-done.49) | copy-start | bytes 24580
  566.3 55.8 %copy-start.60 = (f32[128]{0:T(128)S(1)}, f32[128]{0:T(128)}, u32[]{:S(2)}) copy-start(f32[128]{0:T(128)} %add_rsqrt_fusion.1) | copy-start | bytes 1540
  566.3 56.2 %copy-start.55 = (f32[2048]{0:T(1024)S(1)}, f32[2048]{0:T(1024)}, u32[]{:S(2)}) copy-start(f32[2048]{0:T(1024)} %get-tuple-element.21) | copy-start | bytes 24580
  623.9 9.6 copy-start.69
  633.5 8.4 copy-start.22
  641.9 12.0 %copy-start.23 = (bf16[2,4,128,2048]{3,2,1,0:T(8,128)(2,1)S(1)}, bf16[2,4,128,2048]{3,2,1,0:T(8,128)(2,1)}, u32[]{:S(2)}) copy-start(bf16[2,4,128,2048]{3,2,1,0:T(8,128)(2,1)} %shard_map.266) | copy-start | bytes 12582916
  952.0 8.5 copy-start.26
  954.0 6.4 copy-start.28
  954.0 6.4 copy-start.42
  954.0 6.4 copy-start.40
  954.0 6.4 copy-start.41
  954.0 6.5 copy-start.19
  989.9 11.2 %slice-start.2 = ((s8[8388608]{0:T(1024)(128)(4,1)}), s8[4194304]{0:T(1024)(128)(4,1)S(1)}, s32[]{:S(2)}) async-start(s8[8388608]{0:T(1024)(128)(4,1)} %bitcast.324), calls=%async_computation.4 | async-start | bytes 8388608
  995.2 5.8 slice-start.3
  1014.7 5.9 copy-start.64
  1014.7 5.9 copy-start.65
  (45 other events, 119.2 us)
Sparse Core Ops, SparseCore 0:
  624.0 135.3 reduce-scatter.3

commit v2 on v1

v2 whole, which is shorter than its diff:
```python
import functools
import math

import jax
import jax.numpy as jnp
from jax import lax
from jax.experimental import pallas as pl
from jax.experimental.pallas import tpu as pltpu
from jax.sharding import Mesh
from jax.sharding import PartitionSpec as P

MESH = pl.DeviceIdType.MESH
BF = jnp.bfloat16
F32 = jnp.float32
H = 32
KV = 8
HD = 64
FF = 8192


EPS_NORM = 1e-05
NEG_FILL = -1000000000.0
THETA = 500000.0
BETA_ONE = 0.9
BETA_TWO = 0.95
ADAM_EPS = 1e-08
DECAY_MATRIX = 0.1
LR_MATRIX = 0.01
LR_OUTPUT = 0.06
LR_GAIN = 0.3


def rope_table(positions):
    half_dim = HD // 2
    index_row = jnp.arange(half_dim, dtype=jnp.float32)
    frequency = jnp.exp(-(2.0 * index_row / HD) * math.log(THETA))
    wavelen = 2.0 * math.pi / frequency
    smooth = (8192.0 / wavelen - 1.0) / 3.0
    scaled = jnp.where(
        wavelen < 2048.0,
        frequency,
        jnp.where(
            wavelen > 8192.0,
            frequency / 32.0,
            (1.0 - smooth) * frequency / 32.0 + smooth * frequency,
        ),
    )
    angles = positions.astype(jnp.float32)[:, None] * scaled[None, :]
    cosine = jnp.cos(angles)
    sine_part = jnp.sin(angles)
    return (jnp.concatenate([cosine, cosine], 1), jnp.concatenate([sine_part, sine_part], 1))


def adamw(weight, gradient, states, step_rate, decay_rate):
    first_mom = BETA_ONE * states[0] + (1.0 - BETA_ONE) * gradient
    root_mom = jnp.sqrt(BETA_TWO * states[1] * states[1] + (1.0 - BETA_TWO) * gradient * gradient)
    first_hat = first_mom / (1.0 - BETA_ONE**3)
    root_hat = root_mom / math.sqrt(1.0 - BETA_TWO**3)
    updated = weight - step_rate * (first_hat / (root_hat + ADAM_EPS) + decay_rate * weight)
    return (updated, jnp.stack([first_mom, root_mom]))


def contract_rows(left_arr, right_arr):
    return lax.dot_general(
        left_arr, right_arr, (((0,), (0,)), ((), ())), preferred_element_type=jnp.float32
    )


def contract_cols(left_arr, right_arr):
    return lax.dot_general(
        left_arr, right_arr, (((1,), (1,)), ((), ())), preferred_element_type=jnp.float32
    )


def wrap(value, size):
    return lax.rem(value + size, size)


def remote(src, dst, send_sem, recv_sem, **where):
    return pltpu.make_async_remote_copy(
        src_ref=src,
        dst_ref=dst,
        send_sem=send_sem,
        recv_sem=recv_sem,
        device_id=where,
        device_id_type=MESH,
    )


def greet(places):
    barrier = pltpu.get_barrier_semaphore()
    for where in places:
        pl.semaphore_signal(barrier, inc=1, device_id=where, device_id_type=MESH)
    pl.semaphore_wait(barrier, len(places))


def greet_line(line, pair):
    barrier = pltpu.get_barrier_semaphore()
    here = lax.axis_index("ctx")

    @pl.when(here > 0)
    def _():
        pl.semaphore_signal(barrier, inc=1, device_id={"ctx": here - 1}, device_id_type=MESH)

    @pl.when(here < line - 1)
    def _():
        pl.semaphore_signal(barrier, inc=1, device_id={"ctx": here + 1}, device_id_type=MESH)

    if pair > 1:
        pl.semaphore_signal(
            barrier, inc=1, device_id={"core": 1 - lax.axis_index("core")}, device_id_type=MESH
        )
    ends = (here == 0).astype(jnp.int32) + (here == line - 1).astype(jnp.int32)
    pl.semaphore_wait(barrier, 2 - ends + (1 if pair > 1 else 0))


class Travel:
    @staticmethod
    def sems(many, line):
        return [pltpu.SemaphoreType.DMA((many,))] + [pltpu.SemaphoreType.DMA((many, 2, line))] * 4

    def __init__(self, line, pair, ins, outs, own_sem, line_send, line_recv, core_send, core_recv):
        self.line, self.pair, self.ins, self.outs = line, pair, ins, outs
        self.own_sem, self.line_sems, self.core_sems = own_sem, (line_send, line_recv), (core_send, core_recv)
        self.here = lax.axis_index("ctx")
        self.core = lax.axis_index("core")

    def block(self, way, step):
        return self.here - 1 - step if way == 0 else self.here + 1 + step

    def copy(self, sems, at, source, place, **where):
        return remote(place if source is None else source, place, sems[0].at[at], sems[1].at[at], **where)

    def hop(self, item, way, step, source=None):
        place = self.outs[item].at[self.core, self.block(way, step - 1)]
        target = self.here + 1 if way == 0 else self.here - 1
        return self.copy(self.line_sems, (item, way, step), source, place, ctx=target)

    def arrived(self, item, way, step):
        place = self.outs[item].at[self.core, self.block(way, step)]
        return self.copy(self.line_sems, (item, way, step), None, place, ctx=self.here)

    def share(self, item, way, step, source=None):
        place = self.outs[item].at[self.core, self.block(way, step)]
        return self.copy(self.core_sems, (item, way, step + 1), source, place, core=1 - self.core)

    def shared(self, item, way, step):
        place = self.outs[item].at[1 - self.core, self.block(way, step)]
        return self.copy(self.core_sems, (item, way, step + 1), None, place, core=1 - self.core)

    def own(self, item):
        place = self.outs[item].at[self.core, self.here]
        return pltpu.make_async_copy(self.ins[item], place, self.own_sem.at[item])

    def sends(self, way):
        return self.here < self.line - 1 if way == 0 else self.here > 0

    def has(self, way, step):
        return self.block(way, step) >= 0 if way == 0 else self.block(way, step) <= self.line - 1

    def begin(self):
        for item in range(len(self.ins)):
            for way in range(2):

                @pl.when(self.sends(way))
                def _(item=item, way=way):
                    self.hop(item, way, 0, self.ins[item]).start()

            if self.pair > 1:
                self.share(item, 0, -1, self.ins[item]).start()
            self.own(item).start()

    def step(self, step):
        for item in range(len(self.ins)):
            for way in range(2):

                @pl.when(self.has(way, step))
                def _(item=item, way=way):
                    self.arrived(item, way, step).wait_recv()
                    if step + 1 < self.line - 1:

                        @pl.when(self.sends(way))
                        def _():
                            self.hop(item, way, step + 1).start()

                    if self.pair > 1:
                        self.share(item, way, step).start()

    def end(self):
        for item in range(len(self.ins)):
            self.own(item).wait()
            if self.pair > 1:
                self.share(item, 0, -1, self.ins[item]).wait_send()
                self.shared(item, 0, -1).wait_recv()
            for way in range(2):

                @pl.when(self.sends(way))
                def _(item=item, way=way):
                    self.hop(item, way, 0, self.ins[item]).wait_send()

                for step in range(self.line - 1):

                    @pl.when(self.has(way, step))
                    def _(item=item, way=way, step=step):
                        if step + 1 < self.line - 1:

                            @pl.when(self.sends(way))
                            def _():
                                self.hop(item, way, step + 1).wait_send()

                        if self.pair > 1:
                            self.share(item, way, step).wait_send()
                            self.shared(item, way, step).wait_recv()


def gather_kernel(line, pair, many, *refs):
    greet_line(line, pair)
    travel = Travel(line, pair, refs[:many], refs[many : 2 * many], *refs[2 * many :])
    travel.begin()
    for step in range(line - 1):
        travel.step(step)
    travel.end()


def gather_tokens(sizes, collective_id, *arrays):
    line, pair = sizes["ctx"], sizes["core"]
    many = len(arrays)
    any_spec = pl.BlockSpec(memory_space=pl.ANY)
    outs = pl.pallas_call(
        functools.partial(gather_kernel, line, pair, many),
        out_shape=[jax.ShapeDtypeStruct((pair, line) + a.shape, a.dtype) for a in arrays],
        in_specs=[any_spec] * many,
        out_specs=[any_spec] * many,
        scratch_shapes=Travel.sems(many, line),
        compiler_params=pltpu.CompilerParams(collective_id=collective_id, has_side_effects=True),
    )(*arrays)
    return [o.reshape((-1,) + a.shape[1:]) for o, a in zip(outs, arrays)]


def add_rows(rows, out_ref, *parts):
    def one(index, carry):
        at = pl.ds(pl.multiple_of(index * 16, 16), 16)
        total = parts[0][at, :].astype(F32)
        for part in parts[1:]:
            total = total + part[at, :].astype(F32)
        out_ref[at, :] = total.astype(out_ref.dtype)
        return carry

    lax.fori_loop(0, rows // 16, one, 0)


def scatter_kernel(line, pair, part_ref, out_ref, near, mine, going, landed, core_send, core_recv, line_send, line_recv):
    rows = out_ref.shape[0]
    here = lax.axis_index("ctx")
    core = lax.axis_index("core")
    greet_line(line, pair)

    def to_core(block):
        return remote(
            part_ref.at[1 - core, block],
            near.at[block],
            core_send.at[block],
            core_recv.at[block],
            core=1 - core,
        )

    def onward(way, block):
        return remote(
            going.at[way, block],
            landed.at[way, block],
            line_send.at[way, block],
            line_recv.at[way, block],
            ctx=here + 1 if way == 0 else here - 1,
        )

    order = []
    for step in range(line):
        order += [line - 1 - step, step]
    order = list(dict.fromkeys(order))
    if pair > 1:
        for block in order:
            to_core(block).start()
    ready = set()
    for step in range(line):
        for way, block in ((0, line - 1 - step), (1, step)):
            if block not in ready:
                ready.add(block)
                if pair > 1:
                    to_core(block).wait_recv()
            goes = here < block if way == 0 else here > block
            first = here == 0 if way == 0 else here == line - 1

            @pl.when(goes & first)
            def _(way=way, block=block):
                terms = [part_ref.at[core, block]] + ([near.at[block]] if pair > 1 else [])
                add_rows(rows, going.at[way, block], *terms)
                onward(way, block).start()

            @pl.when(goes & jnp.logical_not(first))
            def _(way=way, block=block):
                onward(way, block).wait_recv()
                terms = [part_ref.at[core, block]] + ([near.at[block]] if pair > 1 else [])
                add_rows(rows, going.at[way, block], *terms, landed.at[way, block])
                onward(way, block).start()

    for block in range(line):

        @pl.when(here == block)
        def _(block=block):
            terms = [part_ref.at[core, block]] + ([near.at[block]] if pair > 1 else [])
            if block > 0:
                onward(0, block).wait_recv()
                terms.append(landed.at[0, block])
            if block < line - 1:
                onward(1, block).wait_recv()
                terms.append(landed.at[1, block])
            add_rows(rows, out_ref, *terms)

    for block in range(line):
        if pair > 1:
            to_core(block).wait_send()
        for way in range(2):
            goes = here < block if way == 0 else here > block

            @pl.when(goes)
            def _(way=way, block=block):
                onward(way, block).wait_send()


def scatter_tokens(sizes, collective_id, terms):
    line, pair = sizes["ctx"], sizes["core"]
    columns = terms.shape[1]
    rows = terms.shape[0] // (line * pair)
    vmem = pl.BlockSpec(memory_space=pltpu.VMEM)
    return pl.pallas_call(
        functools.partial(scatter_kernel, line, pair),
        out_shape=jax.ShapeDtypeStruct((rows, columns), F32),
        in_specs=[vmem],
        out_specs=vmem,
        scratch_shapes=[
            pltpu.VMEM((line, rows, columns), BF),
            pltpu.VMEM((8, 128), F32),
            pltpu.VMEM((2, line, rows, columns), BF),
            pltpu.VMEM((2, line, rows, columns), BF),
            pltpu.SemaphoreType.DMA((line,)),
            pltpu.SemaphoreType.DMA((line,)),
            pltpu.SemaphoreType.DMA((2, line)),
            pltpu.SemaphoreType.DMA((2, line)),
        ],
        compiler_params=pltpu.CompilerParams(
            collective_id=collective_id, has_side_effects=True, vmem_limit_bytes=50 * 2**20
        ),
    )(terms.reshape(pair, line, rows, columns))


def blocks_in_order(line, pair):
    away = sorted(range(line), key=lambda d: min(d, line - d))
    return [(dz, dc) for dz in away for dc in range(pair)]


def greet_all(sizes):
    names = ("dp", "ctx", "x", "core")
    at = {name: lax.axis_index(name) for name in names}
    places = []
    for dz, dc in blocks_in_order(sizes["ctx"], sizes["core"]):
        if dz or dc:
            places.append(
                {"ctx": wrap(at["ctx"] + dz, sizes["ctx"]), "core": wrap(at["core"] + dc, sizes["core"])}
            )
    for name in ("dp", "x"):
        for step in range(1, sizes[name]):
            places.append({name: wrap(at[name] + step, sizes[name])})
    greet(places)


def pack_member(refs, member, rows, group, tall, wide):
    qkv_ref, out_ref, gate_up_ref, down_ref, gain_ref = refs
    heads, keys, units = H * HD // group, KV * HD // group, FF // group
    low = lambda values: values.astype(BF)
    tall[member, :, :heads] = low(qkv_ref[:, member * heads : (member + 1) * heads])
    key_at, value_at = H * HD + member * keys, (H + KV) * HD + member * keys
    tall[member, :, heads : heads + 2 * keys] = low(
        jnp.concatenate(
            [qkv_ref[:, key_at : key_at + keys], qkv_ref[:, value_at : value_at + keys]], 1
        )
    )
    tall[member, :, heads + 2 * keys : 2 * heads + 2 * keys] = low(
        out_ref[:, member * heads : (member + 1) * heads]
    )
    tall[member, :, 2 * heads + 2 * keys :] = low(gain_ref[...])
    wide[member, :, :units] = low(gate_up_ref[:, member * units : (member + 1) * units])
    wide[member, :, units : 2 * units] = low(
        gate_up_ref[:, FF + member * units : FF + (member + 1) * units]
    )
    wide[member, :, 2 * units :] = low(down_ref[:, member * units : (member + 1) * units])


def spread_kernel(sizes, *refs):
    weight_refs, hidden_ref = refs[:5], refs[5]
    outs, hidden_out = refs[6:8], refs[8]
    packs = refs[9:11]
    own_sem, f_send, f_recv, a_send, a_recv, b_send, b_recv = refs[11:18]
    travel_sems = refs[18:]
    line, pair = sizes["ctx"], sizes["core"]
    group = line * pair
    rows = packs[0].shape[1]
    at = {name: lax.axis_index(name) for name in ("dp", "ctx", "x", "core")}
    greet_all(sizes)
    order = blocks_in_order(line, pair)
    me = at["ctx"] * pair + at["core"]
    travel = Travel(line, pair, [hidden_ref], [hidden_out], *travel_sems)
    travel.begin()

    def first(kind, index):
        dz, dc = order[index]
        z, c = wrap(at["ctx"] + dz, line), wrap(at["core"] + dc, pair)
        return remote(
            packs[kind].at[z * pair + c],
            outs[kind].at[at["dp"], at["ctx"], at["x"], at["core"]],
            f_send.at[kind, index],
            f_recv.at[kind, index],
            ctx=z,
            core=c,
        )

    def place(kind, index, moved):
        dz, dc = order[index]
        z, c = wrap(at["ctx"] - dz, line), wrap(at["core"] - dc, pair)
        spot = {name: wrap(at[name] - moved.get(name, 0), sizes[name]) for name in ("dp", "x")}
        return outs[kind].at[spot["dp"], z, spot["x"], c]

    def came(kind, index):
        spot = place(kind, index, {})
        return remote(spot, spot, f_send.at[kind, index], f_recv.at[kind, index], core=at["core"])

    def axes(index):
        dz, dc = order[index]
        return ("x", "dp") if (dz + dc) % 2 == 0 else ("dp", "x")

    def hop_one(kind, index, step):
        name = axes(index)[0]
        spot = place(kind, index, {})
        return remote(
            spot,
            spot,
            a_send.at[kind, index, step],
            a_recv.at[kind, index, step],
            **{name: wrap(at[name] + step, sizes[name])},
        )

    def one_came(kind, index, step):
        name = axes(index)[0]
        spot = place(kind, index, {name: step})
        return remote(
            spot, spot, a_send.at[kind, index, step], a_recv.at[kind, index, step], core=at["core"]
        )

    def hop_two(kind, index, step, far):
        name, other = axes(index)
        spot = place(kind, index, {name: step})
        return remote(
            spot,
            spot,
            b_send.at[kind, index, step, far],
            b_recv.at[kind, index, step, far],
            **{other: wrap(at[other] + far, sizes[other])},
        )

    def two_came(kind, index, step, far):
        name, other = axes(index)
        spot = place(kind, index, {name: step, other: far})
        return remote(
            spot,
            spot,
            b_send.at[kind, index, step, far],
            b_recv.at[kind, index, step, far],
            core=at["core"],
        )

    def own(kind):
        return pltpu.make_async_copy(
            packs[kind].at[me],
            outs[kind].at[at["dp"], at["ctx"], at["x"], at["core"]],
            own_sem.at[kind],
        )

    def onward(kind, index):
        name, other = axes(index)
        for step in range(1, sizes[name]):
            hop_one(kind, index, step).start()
        for far in range(1, sizes[other]):
            hop_two(kind, index, 0, far).start()

    def onward_two(kind, index):
        name, other = axes(index)
        for step in range(1, sizes[name]):
            one_came(kind, index, step).wait_recv()
            for far in range(1, sizes[other]):
                hop_two(kind, index, step, far).start()

    for member in range(group):
        pack_member(weight_refs, member, rows, group, *packs)
    ahead, late = 3, 1
    for kind in range(2):
        own(kind).start()
        for index in range(1, 1 + ahead):
            first(kind, index).start()
    for tick in range(group + late):
        if tick < group:
            for kind in range(2):
                if tick == 0:
                    own(kind).wait()
                else:
                    came(kind, tick).wait_recv()
                onward(kind, tick)
                if 1 + ahead <= tick + ahead < group and tick:
                    first(kind, tick + ahead).start()
        if tick % 2 == 1 and tick // 2 < line - 1:
            travel.step(tick // 2)
        if tick >= late:
            for kind in range(2):
                onward_two(kind, tick - late)
    travel.end()
    for kind in range(2):
        for index in range(group):
            if index:
                first(kind, index).wait_send()
            name, other = axes(index)
            for step in range(sizes[name]):
                if step:
                    hop_one(kind, index, step).wait_send()
                for far in range(1, sizes[other]):
                    hop_two(kind, index, step, far).wait_send()
                    two_came(kind, index, step, far).wait_recv()


def spread_weights(sizes, collective_id, hidden, gains, *weights):
    line, pair = sizes["ctx"], sizes["core"]
    group = line * pair
    rows = weights[0].shape[0]
    steps = max(sizes["dp"], sizes["x"])
    tall, wide = (2 * H * HD + 2 * KV * HD) // group + 128, 3 * FF // group
    gain_tile = jnp.pad(gains.T, ((0, 0), (0, 126)))
    any_spec = pl.BlockSpec(memory_space=pl.ANY)
    vmem = pl.BlockSpec(memory_space=pltpu.VMEM)
    everyone = (sizes["dp"], line, sizes["x"], pair, rows)
    low, high, tokens = pl.pallas_call(
        functools.partial(spread_kernel, sizes),
        out_shape=[
            jax.ShapeDtypeStruct(everyone + (tall,), BF),
            jax.ShapeDtypeStruct(everyone + (wide,), BF),
            jax.ShapeDtypeStruct((pair, line) + hidden.shape, BF),
        ],
        in_specs=[vmem] * 5 + [any_spec],
        out_specs=[any_spec] * 3,
        scratch_shapes=[
            pltpu.VMEM((group, rows, tall), BF),
            pltpu.VMEM((group, rows, wide), BF),
            pltpu.SemaphoreType.DMA((2,)),
            pltpu.SemaphoreType.DMA((2, group)),
            pltpu.SemaphoreType.DMA((2, group)),
            pltpu.SemaphoreType.DMA((2, group, steps)),
            pltpu.SemaphoreType.DMA((2, group, steps)),
            pltpu.SemaphoreType.DMA((2, group, steps, steps)),
            pltpu.SemaphoreType.DMA((2, group, steps, steps)),
            *Travel.sems(1, line),
        ],
        compiler_params=pltpu.CompilerParams(
            collective_id=collective_id, has_side_effects=True, vmem_limit_bytes=40 * 2**20
        ),
    )(*weights, gain_tile, hidden)
    return low.reshape(-1, tall), high.reshape(-1, wide), tokens.reshape(-1, hidden.shape[1])


def collect_kernel(sizes, widths, *refs):
    many = len(widths)
    pieces = grad_pieces(sizes)
    lefts, rights = refs[: 2 * many : 2], refs[1 : 2 * many : 2]
    refs = refs[2 * many :]
    outs, refs = refs[: len(pieces)], refs[len(pieces) :]
    held, refs = refs[: 2 * many], refs[2 * many :]
    terms, near, far_in = refs[:3]
    load_sem, own_sem, a_send, a_recv, b_send, b_recv, f_send, f_recv = refs[3:]
    line, pair = sizes["ctx"], sizes["core"]
    rows = terms.shape[-2]
    across = sizes["x"] * pair * rows
    at = {name: lax.axis_index(name) for name in ("dp", "ctx", "x", "core")}
    me = at["ctx"] * pair + at["core"]
    loads = [
        pltpu.make_async_copy(source, target, load_sem.at[i])
        for i, (source, target) in enumerate(zip((r for two in zip(lefts, rights) for r in two), held))
    ]
    for load in loads:
        load.start()
    greet_all(sizes)
    away = sorted(range(line), key=lambda d: -min(d, line - d))
    order = [(dz, dc) for dz in away for dc in range(pair)]

    def spot_of(index):
        dz, dc = order[index]
        return wrap(at["ctx"] + dz, line), wrap(at["core"] + dc, pair)

    def axes(index):
        dz, dc = order[index]
        return ("dp", "x") if (dz + dc) % 2 == 0 else ("x", "dp")

    def multiply(tick):
        z = wrap(at["ctx"] + away[tick], line)
        start = 0
        for item, width in enumerate(widths):
            left, right = held[2 * item], held[2 * item + 1]
            step = math.gcd(width, 512)

            @pl.loop(0, sizes["dp"])
            def _(dp, left=left, right=right, start=start, width=width, step=step):
                lanes = pl.ds(pl.multiple_of((dp * line + z) * across, 128), across)
                left_t = left[:, lanes].T

                @pl.loop(0, width // step)
                def _(part):
                    columns = pl.ds(pl.multiple_of(part * step, 128), step)
                    into = pl.ds(pl.multiple_of(start + part * step, 128), step)
                    product = dot(left_t, right[:, columns]).astype(BF)
                    for x in range(sizes["x"]):
                        for core in range(pair):
                            low = (x * pair + core) * rows
                            terms[tick, dp, x, core, :, into] = product[low : low + rows]

            start += width

    def block_terms(index, first_at, other_at):
        spot = {axes(index)[0]: first_at, axes(index)[1]: other_at}
        return terms.at[index // pair, spot["dp"], spot["x"], spot_of(index)[1]]

    def hop_one(index, step, place):
        name = axes(index)[0]
        to = wrap(at[name] + step, sizes[name])
        return remote(
            block_terms(index, to, place),
            near.at[index, (step - 1) * sizes[axes(index)[1]] + place],
            a_send.at[index, step, place],
            a_recv.at[index, step, place],
            **{name: to},
        )

    def hop_two(index, far):
        name, other = axes(index)
        to = wrap(at[other] + far, sizes[other])
        return remote(
            block_terms(index, at[name], to),
            far_in.at[index, far - 1],
            b_send.at[index, far],
            b_recv.at[index, far],
            **{other: to},
        )

    def done(index):
        name, other = axes(index)
        return block_terms(index, at[name], at[other])

    def piece_at(piece, member):
        _, width, offset = pieces[piece]
        return outs[piece].at[:, pl.ds(pl.multiple_of(member * width, 128), width)]

    def last(index, piece):
        z, c = spot_of(index)
        _, width, offset = pieces[piece]
        source = done(index).at[:, pl.ds(offset, width)]
        target = piece_at(piece, me)
        if index == len(order) - pair:
            return pltpu.make_async_copy(source, target, own_sem.at[piece])
        return remote(
            source, target, f_send.at[index, piece], f_recv.at[index, piece], ctx=z, core=c
        )

    def last_came(index, piece):
        dz, dc = order[index]
        z, c = wrap(at["ctx"] - dz, line), wrap(at["core"] - dc, pair)
        spot = piece_at(piece, z * pair + c)
        return remote(
            spot, spot, f_send.at[index, piece], f_recv.at[index, piece], core=at["core"]
        )

    def sum_one(index):
        name, other = axes(index)
        for far in list(range(1, sizes[other])) + [0]:
            place = wrap(at[other] + far, sizes[other])
            for step in range(1, sizes[name]):
                hop_one(index, step, place).wait_recv()
            kept = block_terms(index, at[name], place)
            add_rows(rows, kept, kept, *[near.at[index, (step - 1) * sizes[other] + place] for step in range(1, sizes[name])])
            if far:
                hop_two(index, far).start()

    def sum_two(index):
        other = axes(index)[1]
        for far in range(1, sizes[other]):
            hop_two(index, far).wait_recv()
        add_rows(
            rows, done(index), done(index), *[far_in.at[index, far - 1] for far in range(1, sizes[other])]
        )
        for piece in range(len(pieces)):
            last(index, piece).start()

    late, later = 1, 2
    for tick in range(line + later):
        if tick < line:
            if tick == 0:
                for load in loads:
                    load.wait()
            multiply(tick)
            for index in range(tick * pair, (tick + 1) * pair):
                name, other = axes(index)
                for far in list(range(1, sizes[other])) + [0]:
                    for step in range(1, sizes[name]):
                        hop_one(index, step, wrap(at[other] + far, sizes[other])).start()
        if late <= tick < line + late:
            for index in range((tick - late) * pair, (tick - late + 1) * pair):
                sum_one(index)
        if tick >= later:
            for index in range((tick - later) * pair, (tick - later + 1) * pair):
                sum_two(index)
    for index in range(len(order)):
        name, other = axes(index)
        for step in range(1, sizes[name]):
            for place in range(sizes[other]):
                hop_one(index, step, place).wait_send()
        for far in range(1, sizes[other]):
            hop_two(index, far).wait_send()
        for piece in range(len(pieces)):
            if index == len(order) - pair:
                last(index, piece).wait()
            else:
                last(index, piece).wait_send()
                last_came(index, piece).wait_recv()


def grad_pieces(sizes):
    group = sizes["ctx"] * sizes["core"]
    heads, keys, units = H * HD // group, KV * HD // group, FF // group
    pieces, offset = [], 0
    for name, width in (
        ("gate", units),
        ("up", units),
        ("down", units),
        ("query", heads),
        ("key_value", 2 * keys),
        ("out", heads),
    ):
        pieces.append((name, width, offset))
        offset += width
    return pieces


def collect_grads(sizes, collective_id, *factors):
    line, pair = sizes["ctx"], sizes["core"]
    group = line * pair
    rows = factors[0].shape[1] // (group * sizes["dp"] * sizes["x"])
    widths = [right.shape[1] for right in factors[1::2]]
    total = sum(widths)
    pieces = grad_pieces(sizes)
    steps = max(sizes["dp"], sizes["x"])
    any_spec = pl.BlockSpec(memory_space=pl.ANY)
    dma = pltpu.SemaphoreType.DMA
    return pl.pallas_call(
        functools.partial(collect_kernel, sizes, widths),
        out_shape=[jax.ShapeDtypeStruct((rows, group * width), BF) for _, width, _ in pieces],
        in_specs=[any_spec] * len(factors),
        out_specs=[any_spec] * len(pieces),
        scratch_shapes=[
            *[pltpu.VMEM(factor.shape, factor.dtype) for factor in factors],
            pltpu.VMEM((line, sizes["dp"], sizes["x"], pair, rows, total), BF),
            pltpu.VMEM((group, sizes["dp"] * sizes["x"] - min(sizes["dp"], sizes["x"]), rows, total), BF),
            pltpu.VMEM((group, steps - 1, rows, total), BF),
            dma((len(factors),)),
            dma((len(pieces),)),
            dma((group, steps, steps)),
            dma((group, steps, steps)),
            dma((group, steps)),
            dma((group, steps)),
            dma((group, len(pieces))),
            dma((group, len(pieces))),
        ],
        compiler_params=pltpu.CompilerParams(
            collective_id=collective_id, has_side_effects=True, vmem_limit_bytes=62 * 2**20
        ),
    )(*factors)


def adamw_kernel(step_rate, decay_rate, grad_ref, weight_ref, state_ref, grad_out, weight_out, state_out):
    gradient = grad_ref[...].astype(F32)
    grad_out[...] = gradient
    updated, states = adamw(weight_ref[...], gradient, state_ref[...], step_rate, decay_rate)
    weight_out[...] = updated
    state_out[...] = states


def adamw_columns(gradient, weight, states, step_rate, decay_rate):
    rows, columns = weight.shape
    step = math.gcd(columns, 1024)
    flat = pl.BlockSpec((rows, step), lambda i: (0, i))
    deep = pl.BlockSpec((2, rows, step), lambda i: (0, 0, i))
    return pl.pallas_call(
        functools.partial(adamw_kernel, step_rate, decay_rate),
        grid=(columns // step,),
        out_shape=[
            jax.ShapeDtypeStruct(weight.shape, F32),
            jax.ShapeDtypeStruct(weight.shape, F32),
            jax.ShapeDtypeStruct(states.shape, F32),
        ],
        in_specs=[flat, flat, deep],
        out_specs=[flat, flat, deep],
    )(gradient, weight, states)


def turned(values):
    half_dim = values.shape[-1] // 2
    return jnp.concatenate([-values[..., half_dim:], values[..., :half_dim]], -1)


def turned_back(values):
    half_dim = values.shape[-1] // 2
    return jnp.concatenate([values[..., half_dim:], -values[..., :half_dim]], -1)


def norm_back(grad_entry, normed, inverse, gain):
    grad_gain = jnp.sum(grad_entry * normed, 0)
    grad_normed = grad_entry * gain
    grad_rows = inverse * (grad_normed - normed * jnp.mean(grad_normed * normed, -1, keepdims=True))
    return (grad_rows, grad_gain)


def dot(left, right):
    return jnp.dot(left, right, preferred_element_type=F32)


def shards(
    sizes,
    hidden,
    cotangent,
    span_order,
    norm_gains,
    w_qkv,
    w_out,
    w_gate_up,
    w_down,
    mom_gains,
    mom_qkv,
    mom_out,
    mom_gate_up,
    mom_down,
):
    everyone = ("dp", "ctx", "x", "core")
    line, pair = sizes["ctx"], sizes["core"]
    group = line * pair
    block_rows, width = hidden.shape[1:]
    total_rows = block_rows * line
    span_rows = total_rows // span_order.shape[0]
    heads, kv_heads = H // group, KV // group
    ratio = heads // kv_heads
    query_cols, kv_cols, unit_cols = heads * HD, kv_heads * HD, FF // group
    scale = HD ** (-0.5)
    key_pos = (
        span_order[:, None] * span_rows + jnp.arange(span_rows, dtype=jnp.int32)[None, :]
    ).reshape(-1)
    visible = key_pos[None, :] <= key_pos[:, None]
    cos_tab, sin_tab = rope_table(key_pos)
    cos_tab, sin_tab = cos_tab[None, :, None, :], sin_tab[None, :, None, :]

    qkv_width = query_cols + 2 * kv_cols
    low, high, hidden_all = spread_weights(
        sizes, 0, hidden[0], norm_gains, w_qkv, w_out, w_gate_up, w_down
    )
    qkv_c = low[:, :qkv_width]
    out_c = low[:, qkv_width : qkv_width + query_cols]
    gains = low[:, qkv_width + query_cols :].astype(F32)[:, :2].T
    gain_one, gain_two = gains[0], gains[1]
    gate_up_c = high[:, : 2 * unit_cols]
    down_c = high[:, 2 * unit_cols :]

    def normed(rows):
        inverse = lax.rsqrt(jnp.mean(rows * rows, -1, keepdims=True) + EPS_NORM)
        return rows * inverse, inverse

    row_in = hidden[0].astype(F32)
    normed_one, inv_one = normed(row_in)
    entry_one = (normed(hidden_all.astype(F32))[0] * gain_one).astype(BF)
    (cot,) = gather_tokens(sizes, 1, cotangent[0])

    projected = dot(entry_one, qkv_c).reshape(pair, total_rows, qkv_width)
    queries = projected[..., :query_cols].reshape(pair, total_rows, heads, HD)
    key_rows = projected[..., query_cols : query_cols + kv_cols].reshape(
        pair, total_rows, kv_heads, HD
    )
    value_rows = projected[..., query_cols + kv_cols :].reshape(pair, total_rows, kv_heads, HD)
    queries = (queries * cos_tab + turned(queries) * sin_tab).astype(BF)
    key_rows = (key_rows * cos_tab + turned(key_rows) * sin_tab).astype(BF)
    value_rows = value_rows.astype(BF)
    queries = queries.reshape(pair, total_rows, kv_heads, ratio, HD)

    def product(spec, left, right):
        return jnp.einsum(spec, left, right, preferred_element_type=F32)

    scores = product("stkgd,sukd->skgtu", queries, key_rows) * scale
    scores = jnp.where(visible, scores, NEG_FILL)
    top_score = jnp.max(scores, -1, keepdims=True)
    exponent = jnp.exp(scores - top_score)
    probability = exponent / jnp.sum(exponent, -1, keepdims=True)
    prob_low = probability.astype(BF)
    attended = product("skgtu,sukd->stkgd", prob_low, value_rows).astype(BF)
    attended = attended.reshape(pair * total_rows, query_cols)

    middle = row_in + scatter_tokens(sizes, 2, contract_cols(attended, out_c).astype(BF))
    normed_two, inv_two = normed(middle)
    (entry_two,) = gather_tokens(sizes, 3, (normed_two * gain_two).astype(BF))

    gate_up = dot(entry_two, gate_up_c)
    gate_part = gate_up[:, :unit_cols]
    up_part = gate_up[:, unit_cols:]
    sigmoid_gate = jax.nn.sigmoid(gate_part)
    silu_gate = gate_part * sigmoid_gate
    activated = (silu_gate * up_part).astype(BF)
    summed = scatter_tokens(sizes, 4, contract_cols(activated, down_c).astype(BF))
    output = (middle + summed).astype(BF)[None]
    grad_act = dot(cot, down_c)
    grad_gate = grad_act * up_part * sigmoid_gate * (1.0 + gate_part * (1.0 - sigmoid_gate))
    grad_up = grad_act * silu_gate
    grad_gu = jnp.concatenate([grad_gate, grad_up], 1).astype(BF)
    grad_entry_two = scatter_tokens(sizes, 5, contract_cols(grad_gu, gate_up_c).astype(BF))
    grad_top = cotangent[0].astype(F32)
    grad_mid_norm, grad_gain_two = norm_back(grad_entry_two, normed_two, inv_two, gain_two)
    grad_middle = grad_top + grad_mid_norm
    (grad_branch,) = gather_tokens(sizes, 6, grad_middle.astype(BF))

    grad_attended = dot(grad_branch, out_c).astype(BF)
    grad_heads = grad_attended.reshape(pair, total_rows, kv_heads, ratio, HD)
    grad_prob = product("stkgd,sukd->skgtu", grad_heads, value_rows)
    delta_row = jnp.sum(probability * grad_prob, -1, keepdims=True)
    grad_scores = jnp.where(visible, probability * (grad_prob - delta_row), 0.0).astype(BF)
    grad_queries = product("skgtu,sukd->stkgd", grad_scores, key_rows) * scale
    grad_keys = product("skgtu,stkgd->sukd", grad_scores, queries) * scale
    grad_values = product("skgtu,stkgd->sukd", prob_low, grad_heads)
    grad_queries = grad_queries.reshape(pair, total_rows, heads, HD)
    grad_queries = grad_queries * cos_tab + turned_back(grad_queries * sin_tab)
    grad_keys = grad_keys * cos_tab + turned_back(grad_keys * sin_tab)
    grad_projected = jnp.concatenate(
        [
            grad_queries.reshape(-1, query_cols),
            grad_keys.reshape(-1, kv_cols),
            grad_values.reshape(-1, kv_cols),
        ],
        1,
    ).astype(BF)
    grad_entry_one = scatter_tokens(sizes, 7, contract_cols(grad_projected, qkv_c).astype(BF))
    grad_row_norm, grad_gain_one = norm_back(grad_entry_one, normed_one, inv_one, gain_one)
    grad_hidden = (grad_middle + grad_row_norm).astype(BF)[None]

    grad_gate, grad_up, grad_down, grad_query, grad_key_value, grad_out = collect_grads(
        sizes, 8, entry_two, grad_gu, cot, activated, entry_one, grad_projected, grad_branch, attended
    )
    grad_gains = lax.psum_scatter(
        jnp.stack([grad_gain_one, grad_gain_two]), everyone, scatter_dimension=1, tiled=True
    )
    rows = w_qkv.shape[0]
    grad_key_value = grad_key_value.reshape(rows, group, 2, kv_cols).transpose(0, 2, 1, 3)
    grad_qkv = jnp.concatenate([grad_query, grad_key_value.reshape(rows, -1)], 1)
    grad_gate_up = jnp.concatenate([grad_gate, grad_up], 1)
    new_gains, new_mom_gains = adamw(norm_gains, grad_gains, mom_gains, LR_GAIN, 0.0)
    grad_qkv, new_qkv, new_mom_qkv = adamw_columns(grad_qkv, w_qkv, mom_qkv, LR_MATRIX, DECAY_MATRIX)
    grad_out, new_out, new_mom_out = adamw_columns(grad_out, w_out, mom_out, LR_OUTPUT, DECAY_MATRIX)
    grad_gate_up, new_gate_up, new_mom_gate_up = adamw_columns(
        grad_gate_up, w_gate_up, mom_gate_up, LR_MATRIX, DECAY_MATRIX
    )
    grad_down, new_down, new_mom_down = adamw_columns(
        grad_down, w_down, mom_down, LR_MATRIX, DECAY_MATRIX
    )
    return (
        output,
        grad_hidden,
        grad_gains,
        grad_qkv,
        grad_out,
        grad_gate_up,
        grad_down,
        new_gains,
        new_qkv,
        new_out,
        new_gate_up,
        new_down,
        new_mom_gains,
        new_mom_qkv,
        new_mom_out,
        new_mom_gate_up,
        new_mom_down,
    )


def solution(mesh):
    shape = dict(mesh.shape)
    pair = 2 if shape["ctx"] * 2 <= KV and shape["fsdp"] % 2 == 0 else 1
    sizes = {"dp": shape["dp"], "ctx": shape["ctx"], "x": shape["fsdp"] // pair, "core": pair}
    finer = Mesh(mesh.devices.reshape(tuple(sizes.values())), tuple(sizes))
    tokens = P(("dp", "x", "core"), "ctx", None)
    everyone = ("dp", "ctx", "x", "core")
    rows, gains = P(everyone, None), P(None, everyone)
    row_moments, gain_moments = P(None, everyone, None), P(None, None, everyone)
    weights = (gains, rows, rows, rows, rows)
    moments = (gain_moments, row_moments, row_moments, row_moments, row_moments)
    return jax.shard_map(
        functools.partial(shards, sizes),
        mesh=finer,
        in_specs=(tokens, tokens, P()) + weights + moments,
        out_specs=(tokens, tokens) + weights + weights + moments,
        check_vma=False,
    )
```

time: 1030 us -> 896 us (0.87)
  local copies, waits for them, and re-layouts: 99 us -> 42.6 us
  blocking collectives: 43 us -> 0 us
  matrix products: 105 us -> 80.3 us
  other arithmetic: 63 us -> 39.8 us
    all_gather x1 -> x0, blocking collectives: 43 us -> none  [shards(): lax.all_gather(norm_gains.astype(BF), everyone, axis=1, tiled=True)]
    concatenate x11 -> x0, local copies, waits for them, and re-layouts: 33.5 us -> none  [the longest x1 19 us: shards(): jnp.concatenate([contract_rows(entry_one, grad_projected).astype(BF), con...]
    dot_general x4 -> x0, matrix products: 24.7 us -> none  [contract_rows(): lax.dot_general(left_arr, right_arr, (((0,), (0,)), ((), ())), preferred_...]
    transpose x13 -> x0, local copies, waits for them, and re-layouts: 23.8 us -> none  [the longest x10 22.5 us: joined(): grads[:, :, low:high].transpose(1, 0, 2).reshape(grads.shape[1], -1)]
    pallas_call x2 -> x6, Pallas kernels: 320 us -> 336 us  [the longest x1 152 us: collect_grads(): pl.pallas_call(functools.partial(collect_kernel, sizes, widths), out_shap...]
    sub x4 -> x0, other arithmetic: 14.2 us -> none  [adamw(): weight - step_rate * (first_hat / (root_hat + ADAM_EPS) + decay_rate * we...]
    unnamed x167 -> x75, local copies, waits for them, and re-layouts: 23.6 us -> 18.2 us
  transfers between devices with their start and end apart: 1 -> 1, of which waited for: 0 -> 0; matrix products, arithmetic and copies ran while one was open for 14% -> 3% of each run, Pallas kernels for 23% -> 28%
where the time goes in v2:
time: 896 us; the launch traced here: 888 us
  Pallas kernels  710 us (79%)
  matrix products  80.3 us (9%)
  local copies, waits for them, and re-layouts  42.6 us (5%)
  other arithmetic  39.8 us (4%)
  between operations  15 us (2%)
    pallas_call x4, Pallas kernels, scatter_tokens(): pl.pallas_call(functools.partial(scatter_kernel, line, pair), out_shape=j...  226 us
    pallas_call x1, Pallas kernels, collect_grads(): pl.pallas_call(functools.partial(collect_kernel, sizes, widths), out_shap...  152 us
    pallas_call x1, Pallas kernels, spread_weights(): pl.pallas_call(functools.partial(spread_kernel, sizes), out_shape=[jax.Sh...  150 us
    pallas_call x3, Pallas kernels, gather_tokens(): pl.pallas_call(functools.partial(gather_kernel, line, pair, many), out_sh...  148 us
    pallas_call x4, Pallas kernels, adamw_columns(): pl.pallas_call(functools.partial(adamw_kernel, step_rate, decay_rate), gr...  34 us
    dot_general x4, matrix products, contract_cols(): lax.dot_general(left_arr, right_arr, (((1,), (1,)), ((), ())), preferred_...  29.8 us
    dot_general x4, matrix products, dot(): return jnp.dot(left, right, preferred_element_type=F32)  28.7 us
    dot_general x6, matrix products, product(): return jnp.einsum(spec, left, right, preferred_element_type=F32)  21.8 us
  transfers between devices with their start and end apart: 1, of which 0 were waited for; matrix products, arithmetic and copies ran while one was open for 3% of the time, Pallas kernels for 28%

profile of v2, /device:TPU:0, one launch (start us, length us, event | category | flops | bytes accessed | tf_op | source)
XLA Modules:
  0.0 888.1 jit_solution(15639950103813108296)
XLA Ops:
  13.9 149.8 %shard_map.260 = (bf16[2,4,2,2,64,768]{5,4,3,2,1,0:T(8,128)(2,1)S(1)}, bf16[2,4,2,2,64,3072]{5,4,3,2,1,0:T(8,128)(2,1)}, bf16[2,4,128,2048]{3,2,1,0:T(8,128)(2,1)S(1)}) custom-call(f32[64,3072]{1,0:T(8,128)S(1)} %copy-done.7, f32[64,2048]{1,0:T(8,128)S(1)} %copy-done.8, f32[64,16384]{1,0:T(8,128)} %weight_ref.6, f32[64,8192]{1,0:T(8,128)S(1)} %copy-done.5, ...), custom_call_target="tpu_custom_call" | custom-call | tf_op jit(solution)/shard_map/pallas_call | solution.py:547
  167.2 3.4 fusion.7
  174.5 66.8 %shard_map.264 = bf16[2,4,128,2048]{3,2,1,0:T(8,128)(2,1)} custom-call(bf16[128,2048]{1,0:T(8,128)(2,1)} %bitcast.229), custom_call_target="tpu_custom_call" | custom-call | tf_op jit(solution)/shard_map/pallas_call | solution.py:229
  247.6 3.4 fusion.42
  252.5 4.6 convolution_convert_fusion.1
  257.1 55.3 %shard_map.261 = f32[128,2048]{1,0:T(8,128)S(1)} custom-call(bf16[2,4,128,2048]{3,2,1,0:T(8,128)(2,1)} %bitcast.218), custom_call_target="tpu_custom_call" | custom-call | tf_op jit(solution)/shard_map/pallas_call | solution.py:335
  313.8 41.4 %shard_map.262 = bf16[2,4,128,2048]{3,2,1,0:T(8,128)(2,1)} custom-call(bf16[128,2048]{1,0:T(8,128)(2,1)} %multiply_convert_fusion.1.refs_0_), custom_call_target="tpu_custom_call" | custom-call | tf_op jit(solution)/shard_map/pallas_call | solution.py:229
  355.2 12.6 %fusion.12 = f32[1024,2048]{1,0:T(8,128)S(1)} fusion(bf16[1024,2048]{1,0:T(8,128)(2,1)} %bitcast.221, bf16[2048,3072]{1,0:T(8,128)(2,1)} %bitcast.254), kind=kOutput, calls=%fused_computation.19 | convolution fusion | flops 8589934592 | bytes 20971520 | tf_op jit(solution)/shard_map/dot_general | solution.py:834
  367.9 9.6 %fusion.18 = (bf16[1024,1024]{1,0:T(8,128)(2,1)S(1)}, bf16[1024,1024]{1,0:T(8,128)(2,1)S(1)}, bf16[1024,1024]{1,0:T(8,128)(2,1)}) fusion(f32[1024,2048]{1,0:T(8,128)S(1)} %fusion.12, bf16[1024,2048]{1,0:T(8,128)(2,1)S(1)} %bitcast.220, bf16[2048,3072]{1,0:T(8,128)(2,1)} %bitcast.255), kind=kOutput, calls=%fused_computation.28 | convolution fusion | flops 4310695936 | bytes 23068672 | tf_op jit(solution)/shard_map/dot_general | solution.py:834
  378.8 12.6 %fusion.25 = bf16[1024,2048]{1,0:T(8,128)(2,1)} fusion(bf16[2048,3072]{1,0:T(8,128)(2,1)} %bitcast.256, bf16[1024,1024]{1,0:T(8,128)(2,1)S(1)} %get-tuple-element.66, bf16[1024,1024]{1,0:T(8,128)(2,1)S(1)} %get-tuple-element.65), kind=kOutput, calls=%fused_computation.38 | convolution fusion | flops 8600420352 | bytes 16777216 | tf_op jit(solution)/shard_map/dot_general | solution.py:70
  391.5 55.5 %shard_map.265 = f32[128,2048]{1,0:T(8,128)S(1)} custom-call(bf16[2,4,128,2048]{3,2,1,0:T(8,128)(2,1)} %bitcast.233), custom_call_target="tpu_custom_call" | custom-call | tf_op jit(solution)/shard_map/pallas_call | solution.py:335
  448.5 40.3 %shard_map.266 = bf16[2,4,128,2048]{3,2,1,0:T(8,128)(2,1)} custom-call(bf16[128,2048]{1,0:T(8,128)(2,1)} %fusion.81.refs_0_), custom_call_target="tpu_custom_call" | custom-call | tf_op jit(solution)/shard_map/pallas_call | solution.py:229
  488.7 4.5 convolution_convert_fusion.3
  496.6 6.6 fusion.51
  503.3 7.0 fusion.2
  516.1 7.3 fusion.15
  530.2 2.7 copy.101
  532.9 3.2 reshape.333
  536.1 2.7 copy.99
  538.8 3.4 reshape.331
  544.7 4.4 convolution_convert_fusion
  549.1 55.3 %shard_map.267 = f32[128,2048]{1,0:T(8,128)S(1)} custom-call(bf16[2,4,128,2048]{3,2,1,0:T(8,128)(2,1)} %bitcast.231), custom_call_target="tpu_custom_call" | custom-call | tf_op jit(solution)/shard_map/pallas_call | solution.py:335
  608.3 4.9 pad_maximum_fusion.refs_1_
  613.2 3.0 fusion.1.refs_4_
  616.2 8.3 convolution_convert_fusion.2
  624.5 60.3 %shard_map.263 = f32[128,2048]{1,0:T(8,128)S(1)} custom-call(bf16[2,4,128,2048]{3,2,1,0:T(8,128)(2,1)} %bitcast.232), custom_call_target="tpu_custom_call" | custom-call | tf_op jit(solution)/shard_map/pallas_call | solution.py:335
  685.8 151.8 %shard_map.268 = (bf16[64,8192]{1,0:T(8,128)(2,1)}, bf16[64,8192]{1,0:T(8,128)(2,1)}, bf16[64,8192]{1,0:T(8,128)(2,1)}, bf16[64,2048]{1,0:T(8,128)(2,1)}, bf16[6...) custom-call(bf16[1024,2048]{1,0:T(8,128)(2,1)} %bitcast.222, bf16[1024,2048]{1,0:T(8,128)(2,1)} %pad_maximum_fusion.refs_1_, ...), custom_call_target="tpu_custom_call" | custom-call | tf_op jit(solution)/shard_map/pallas_call | solution.py:765
  838.9 3.6 fusion.66
  844.8 2.7 shard_map.270
  847.5 4.5 shard_map.269
  852.0 9.1 %shard_map.272 = (f32[64,8192]{1,0:T(8,128)}, f32[64,8192]{1,0:T(8,128)}, f32[2,64,8192]{2,1,0:T(8,128)}) custom-call(bf16[64,8192]{1,0:T(8,128)(2,1)} %get-tuple-element.49.grad_ref, f32[64,8192]{1,0:T(8,128)} %weight_ref.7, f32[2,64,8192]{2,1,0:T(8,128)} %state_ref.7), custom_call_target="tpu_custom_call" | custom-call | tf_op jit(solution)/shard_map/pallas_call | solution.py:803
  861.1 17.7 %shard_map.271 = (f32[64,16384]{1,0:T(8,128)}, f32[64,16384]{1,0:T(8,128)}, f32[2,64,16384]{2,1,0:T(8,128)}) custom-call(bf16[64,16384]{1,0:T(8,128)(2,1)} %pad_maximum_fusion.1.grad_ref, f32[64,16384]{1,0:T(8,128)} %weight_ref.6, f32[2,64,16384]{2,1,0:T(8,128)} %state_ref.6), custom_call_target="tpu_custom_call" | custom-call | tf_op jit(solution)/shard_map/pallas_call | solution.py:803
  (133 shorter events, 54.8 us)
Async XLA Ops:
  7.2 871.6 %reduce-scatter.4.cloned.1.call-start = ((), (), s32[]{:S(2)}) async-start(), calls=%async_computation.1 | async-start | bytes 1081344
  9.1 1.0 copy-start.3
  10.1 1.6 copy-start.5
  11.7 1.1 copy-start.7
  12.8 1.0 copy-start.8
  163.7 2.0 copy-start
  163.7 3.0 copy-start.9
  167.2 3.4 copy-start.10
  172.5 1.1 copy-start.24
  242.8 1.5 copy-start.18
  244.2 3.4 copy-start.12
  257.1 55.3 %copy-start.4 = (bf16[1,128,2048]{2,1,0:T(8,128)(2,1)S(1)}, bf16[1,128,2048]{2,1,0:T(8,128)(2,1)}, u32[]{:S(2)}) copy-start(bf16[1,128,2048]{2,1,0:T(8,128)(2,1)} %param.13) | copy-start | bytes 1572868
  312.7 134.6 %copy-start.13 = (f32[128,2048]{1,0:T(8,128)}, f32[128,2048]{1,0:T(8,128)S(1)}, u32[]{:S(2)}) copy-start(f32[128,2048]{1,0:T(8,128)S(1)} %get-tuple-element.64) | copy-start | bytes 3145732
  355.2 12.7 %copy-start.14 = (bf16[2,4,128,2048]{3,2,1,0:T(8,128)(2,1)S(1)}, bf16[2,4,128,2048]{3,2,1,0:T(8,128)(2,1)}, u32[]{:S(2)}) copy-start(bf16[2,4,128,2048]{3,2,1,0:T(8,128)(2,1)} %shard_map.264) | copy-start | bytes 12582916
  377.5 1.4 copy-start.22
  377.5 14.0 %copy-start.23 = (bf16[1024,1024]{1,0:T(8,128)(2,1)}, bf16[1024,1024]{1,0:T(8,128)(2,1)S(1)}, u32[]{:S(2)}) copy-start(bf16[1024,1024]{1,0:T(8,128)(2,1)S(1)} %get-tuple-element.66) | copy-start | bytes 6291460
  391.5 55.9 %copy-start.17 = (bf16[1,128,2048]{2,1,0:T(8,128)(2,1)S(1)}, bf16[1,128,2048]{2,1,0:T(8,128)(2,1)}, u32[]{:S(2)}) copy-start(bf16[1,128,2048]{2,1,0:T(8,128)(2,1)} %param.14) | copy-start | bytes 1572868
  496.6 6.6 copy-start.29
  503.3 7.0 copy-start.25
  523.4 1.9 copy-start.19
  538.8 5.3 copy-start.26
  542.2 2.5 copy-start.11
  544.7 4.4 copy-start.20
  549.1 58.1 %copy-start.16 = (bf16[32,8,2,512]{3,1,2,0:T(8,128)(2,1)S(1)}, bf16[32,8,2,512]{3,1,2,0:T(8,128)(2,1)}, u32[]{:S(2)}) copy-start(bf16[32,8,2,512]{3,1,2,0:T(8,128)(2,1)} %copy-done.15) | copy-start | bytes 1572868
  608.3 4.9 copy-start.1
  613.2 3.0 copy-start.21
  838.9 3.7 copy-start.27
  838.9 3.6 copy-start.28
  838.9 5.1 copy-start.30
  861.1 18.5 %copy-start.31 = (f32[2,64]{1,0:T(2,128)S(1)}, f32[2,64]{1,0:T(2,128)}, u32[]{:S(2)}) copy-start(f32[2,64]{1,0:T(2,128)} %param.16) | copy-start | bytes 1540
  861.1 18.5 %copy-start.33 = (f32[2,2,64]{2,1,0:T(2,128)S(1)}, f32[2,2,64]{2,1,0:T(2,128)}, u32[]{:S(2)}) copy-start(f32[2,2,64]{2,1,0:T(2,128)} %param.21) | copy-start | bytes 3076
  879.7 1.2 copy-start.32
  (3 other events, 2.7 us)
Sparse Core Ops, SparseCore 0:
  607.4 136.2 reduce-scatter.3

commit v3 on v2

--- a/solution.py
+++ b/solution.py
@@ -132,24 +132,24 @@
         return remote(place if source is None else source, place, sems[0].at[at], sems[1].at[at], **where)
 
     def hop(self, item, way, step, source=None):
-        place = self.outs[item].at[self.core, self.block(way, step - 1)]
+        place = self.outs[item](self.core, self.block(way, step - 1))
         target = self.here + 1 if way == 0 else self.here - 1
         return self.copy(self.line_sems, (item, way, step), source, place, ctx=target)
 
     def arrived(self, item, way, step):
-        place = self.outs[item].at[self.core, self.block(way, step)]
+        place = self.outs[item](self.core, self.block(way, step))
         return self.copy(self.line_sems, (item, way, step), None, place, ctx=self.here)
 
     def share(self, item, way, step, source=None):
-        place = self.outs[item].at[self.core, self.block(way, step)]
+        place = self.outs[item](self.core, self.block(way, step))
         return self.copy(self.core_sems, (item, way, step + 1), source, place, core=1 - self.core)
 
     def shared(self, item, way, step):
-        place = self.outs[item].at[1 - self.core, self.block(way, step)]
+        place = self.outs[item](1 - self.core, self.block(way, step))
         return self.copy(self.core_sems, (item, way, step + 1), None, place, core=1 - self.core)
 
     def own(self, item):
-        place = self.outs[item].at[self.core, self.here]
+        place = self.outs[item](self.core, self.here)
         return pltpu.make_async_copy(self.ins[item], place, self.own_sem.at[item])
 
     def sends(self, way):
@@ -168,7 +168,8 @@
 
             if self.pair > 1:
                 self.share(item, 0, -1, self.ins[item]).start()
-            self.own(item).start()
+            if self.ins[item] is not None:
+                self.own(item).start()
 
     def step(self, step):
         for item in range(len(self.ins)):
@@ -188,7 +189,8 @@
 
     def end(self):
         for item in range(len(self.ins)):
-            self.own(item).wait()
+            if self.ins[item] is not None:
+                self.own(item).wait()
             if self.pair > 1:
                 self.share(item, 0, -1, self.ins[item]).wait_send()
                 self.shared(item, 0, -1).wait_recv()
@@ -211,30 +213,6 @@
                         if self.pair > 1:
                             self.share(item, way, step).wait_send()
                             self.shared(item, way, step).wait_recv()
-
-
-def gather_kernel(line, pair, many, *refs):
-    greet_line(line, pair)
-    travel = Travel(line, pair, refs[:many], refs[many : 2 * many], *refs[2 * many :])
-    travel.begin()
-    for step in range(line - 1):
-        travel.step(step)
-    travel.end()
-
-
-def gather_tokens(sizes, collective_id, *arrays):
-    line, pair = sizes["ctx"], sizes["core"]
-    many = len(arrays)
-    any_spec = pl.BlockSpec(memory_space=pl.ANY)
-    outs = pl.pallas_call(
-        functools.partial(gather_kernel, line, pair, many),
-        out_shape=[jax.ShapeDtypeStruct((pair, line) + a.shape, a.dtype) for a in arrays],
-        in_specs=[any_spec] * many,
-        out_specs=[any_spec] * many,
-        scratch_shapes=Travel.sems(many, line),
-        compiler_params=pltpu.CompilerParams(collective_id=collective_id, has_side_effects=True),
-    )(*arrays)
-    return [o.reshape((-1,) + a.shape[1:]) for o, a in zip(outs, arrays)]
 
 
 def add_rows(rows, out_ref, *parts):
@@ -249,108 +227,355 @@
     lax.fori_loop(0, rows // 16, one, 0)
 
 
-def scatter_kernel(line, pair, part_ref, out_ref, near, mine, going, landed, core_send, core_recv, line_send, line_recv):
-    rows = out_ref.shape[0]
-    here = lax.axis_index("ctx")
-    core = lax.axis_index("core")
+class Reduce:
+    @staticmethod
+    def sems(*outer):
+        dma = pltpu.SemaphoreType.DMA
+        return lambda line: [dma(outer), dma(outer), dma(outer + (2, line)), dma(outer + (2, line))]
+
+    @staticmethod
+    def room(line, pair, rows, columns, *outer):
+        return [
+            pltpu.VMEM(outer + (pair, line, rows, columns), BF),
+            pltpu.VMEM(outer + (line, rows, columns), BF),
+            pltpu.VMEM(outer + (line + 1, rows, columns), BF),
+        ]
+
+    def __init__(self, line, pair, part, near, landed, core_send, core_recv, line_send, line_recv, at):
+        self.line, self.pair, self.at = line, pair, at
+        self.part, self.near, self.landed = part, near, landed
+        self.core_sems, self.line_sems = (core_send, core_recv), (line_send, line_recv)
+        self.here, self.core = lax.axis_index("ctx"), lax.axis_index("core")
+        self.rows = part.shape[-2]
+
+    def mine(self, block):
+        return self.part.at[self.at + (self.core, block)]
+
+    def across(self):
+        return remote(
+            self.part.at[self.at + (1 - self.core,)],
+            self.near.at[self.at],
+            self.core_sems[0].at[self.at],
+            self.core_sems[1].at[self.at],
+            core=1 - self.core,
+        )
+
+    def slot(self, way, block):
+        return self.landed.at[self.at + (block + 1 if way == 0 else block,)]
+
+    def onward(self, way, block, here):
+        index = self.at + (way, block)
+        return remote(
+            self.mine(block),
+            self.slot(way, block),
+            self.line_sems[0].at[index],
+            self.line_sems[1].at[index],
+            ctx=here + 1 if way == 0 else here - 1,
+        )
+
+    def begin(self):
+        if self.pair > 1:
+            self.across().start()
+
+    def settle(self):
+        if self.pair > 1:
+            self.across().wait_recv()
+
+    def terms(self, block):
+        return [self.mine(block)] + ([self.near.at[self.at + (block,)]] if self.pair > 1 else [])
+
+    def relay(self, way, block, here):
+        @pl.when(self.here == here)
+        def _():
+            terms = self.terms(block)
+            if here != (0 if way == 0 else self.line - 1):
+                self.onward(way, block, here).wait_recv()
+                terms.append(self.slot(way, block))
+            if len(terms) > 1:
+                add_rows(self.rows, self.mine(block), *terms)
+            self.onward(way, block, here).start()
+
+    def finish(self, here, total_ref):
+        @pl.when(self.here == here)
+        def _():
+            terms = self.terms(here)
+            for way, has in ((0, here > 0), (1, here < self.line - 1)):
+                if has:
+                    self.onward(way, here, here).wait_recv()
+                    terms.append(self.slot(way, here))
+            add_rows(self.rows, total_ref, *terms)
+
+    def drain(self):
+        if self.pair > 1:
+            self.across().wait_send()
+        for here in range(self.line):
+
+            @pl.when(self.here == here)
+            def _(here=here):
+                for block in range(self.line):
+                    if block != here:
+                        self.onward(0 if block > here else 1, block, here).wait_send()
+
+    def plan(self, start, total_ref, after):
+        ends, steps = self.line - 1, [(start, self.begin), (start + LAG, self.settle)]
+        for way in range(2):
+            for block in range(self.line):
+                for here in range(self.line):
+                    if here < block if way == 0 else here > block:
+                        wait = ends - block if way == 0 else block
+                        depth = here if way == 0 else ends - here
+                        when = start + LAG + wait * SEND + depth * HOP
+                        steps.append((when, functools.partial(self.relay, way, block, here)))
+        finish = start + LAG + ends * HOP + 0.5
+        for here in range(self.line):
+            steps.append((finish, functools.partial(self.finish, here, total_ref)))
+        steps.append((finish, after))
+        return steps, finish
+
+
+SEND, HOP, LAG = 3.0, 4.5, 2.5
+
+
+def run_steps(steps):
+    for _, step in sorted(steps, key=lambda item: item[0]):
+        step()
+
+
+def scatter_kernel(line, pair, chunks, terms_ref, out_ref, part, near, landed, total, load_sem, *sems):
+    rows = part.shape[-2]
+    loads = [
+        pltpu.make_async_copy(
+            terms_ref.at[:, :, pl.ds(chunk * rows, rows)], part.at[chunk], load_sem.at[chunk]
+        )
+        for chunk in range(chunks)
+    ]
+    for load in loads:
+        load.start()
     greet_line(line, pair)
-
-    def to_core(block):
-        return remote(
-            part_ref.at[1 - core, block],
-            near.at[block],
-            core_send.at[block],
-            core_recv.at[block],
-            core=1 - core,
-        )
-
-    def onward(way, block):
-        return remote(
-            going.at[way, block],
-            landed.at[way, block],
-            line_send.at[way, block],
-            line_recv.at[way, block],
-            ctx=here + 1 if way == 0 else here - 1,
-        )
-
-    order = []
-    for step in range(line):
-        order += [line - 1 - step, step]
-    order = list(dict.fromkeys(order))
-    if pair > 1:
-        for block in order:
-            to_core(block).start()
-    ready = set()
-    for step in range(line):
-        for way, block in ((0, line - 1 - step), (1, step)):
-            if block not in ready:
-                ready.add(block)
-                if pair > 1:
-                    to_core(block).wait_recv()
-            goes = here < block if way == 0 else here > block
-            first = here == 0 if way == 0 else here == line - 1
-
-            @pl.when(goes & first)
-            def _(way=way, block=block):
-                terms = [part_ref.at[core, block]] + ([near.at[block]] if pair > 1 else [])
-                add_rows(rows, going.at[way, block], *terms)
-                onward(way, block).start()
-
-            @pl.when(goes & jnp.logical_not(first))
-            def _(way=way, block=block):
-                onward(way, block).wait_recv()
-                terms = [part_ref.at[core, block]] + ([near.at[block]] if pair > 1 else [])
-                add_rows(rows, going.at[way, block], *terms, landed.at[way, block])
-                onward(way, block).start()
-
-    for block in range(line):
-
-        @pl.when(here == block)
-        def _(block=block):
-            terms = [part_ref.at[core, block]] + ([near.at[block]] if pair > 1 else [])
-            if block > 0:
-                onward(0, block).wait_recv()
-                terms.append(landed.at[0, block])
-            if block < line - 1:
-                onward(1, block).wait_recv()
-                terms.append(landed.at[1, block])
-            add_rows(rows, out_ref, *terms)
-
-    for block in range(line):
-        if pair > 1:
-            to_core(block).wait_send()
-        for way in range(2):
-            goes = here < block if way == 0 else here > block
-
-            @pl.when(goes)
-            def _(way=way, block=block):
-                onward(way, block).wait_send()
+    sums = [Reduce(line, pair, part, near, landed, *sems, (chunk,)) for chunk in range(chunks)]
+    steps = []
+    for chunk, one in enumerate(sums):
+
+        def after(chunk=chunk):
+            out_ref[chunk * rows : (chunk + 1) * rows, :] = total[...]
+
+        start = chunk * (line - 1) * SEND
+        steps.append((start, loads[chunk].wait))
+        steps += one.plan(start, total, after)[0]
+    run_steps(steps)
+    for one in sums:
+        one.drain()
 
 
 def scatter_tokens(sizes, collective_id, terms):
     line, pair = sizes["ctx"], sizes["core"]
     columns = terms.shape[1]
     rows = terms.shape[0] // (line * pair)
-    vmem = pl.BlockSpec(memory_space=pltpu.VMEM)
+    chunks = 4
     return pl.pallas_call(
-        functools.partial(scatter_kernel, line, pair),
+        functools.partial(scatter_kernel, line, pair, chunks),
         out_shape=jax.ShapeDtypeStruct((rows, columns), F32),
-        in_specs=[vmem],
-        out_specs=vmem,
+        in_specs=[pl.BlockSpec(memory_space=pl.ANY)],
+        out_specs=pl.BlockSpec(memory_space=pltpu.VMEM),
         scratch_shapes=[
-            pltpu.VMEM((line, rows, columns), BF),
-            pltpu.VMEM((8, 128), F32),
-            pltpu.VMEM((2, line, rows, columns), BF),
-            pltpu.VMEM((2, line, rows, columns), BF),
-            pltpu.SemaphoreType.DMA((line,)),
-            pltpu.SemaphoreType.DMA((line,)),
-            pltpu.SemaphoreType.DMA((2, line)),
-            pltpu.SemaphoreType.DMA((2, line)),
+            *Reduce.room(line, pair, rows // chunks, columns, chunks),
+            pltpu.VMEM((rows // chunks, columns), F32),
+            pltpu.SemaphoreType.DMA((chunks,)),
+            *Reduce.sems(chunks)(line),
         ],
         compiler_params=pltpu.CompilerParams(
-            collective_id=collective_id, has_side_effects=True, vmem_limit_bytes=50 * 2**20
+            collective_id=collective_id, has_side_effects=True, vmem_limit_bytes=40 * 2**20
         ),
     )(terms.reshape(pair, line, rows, columns))
+
+
+def middle_kernel(line, pair, chunks, *refs):
+    heads_ref, low_ref, high_ref, hidden_ref, cot_ref, gain_ref = refs[:6]
+    output_ref, grad_mid_ref, gain_grad_ref, branch_ref, entry_ref, cots_ref, act_ref, dgu_ref = refs[6:14]
+    out_w, ffn_w, part, near, landed, total, middle, branch, load_sem = refs[14:23]
+    reduce_sems, travel_sems = refs[23:27], refs[27:]
+    width = hidden_ref.shape[1]
+    rows = part.shape[-2]
+    tokens = pair * line * rows
+    query_cols = out_w.shape[1]
+    units = ffn_w.shape[1] // 3
+    core, here = lax.axis_index("core"), lax.axis_index("ctx")
+    first_col = low_ref.shape[1] - 128 - query_cols
+    loads = [
+        pltpu.make_async_copy(low_ref.at[:, pl.ds(first_col, query_cols)], out_w, load_sem.at[0]),
+        pltpu.make_async_copy(high_ref, ffn_w, load_sem.at[1]),
+    ]
+    for load in loads:
+        load.start()
+    greet_line(line, pair)
+    steps = []
+    sums, travels = [], []
+
+    def chunk_rows(chunk):
+        return slice(chunk * rows, (chunk + 1) * rows)
+
+    def reducer(kind, chunk):
+        one = Reduce(line, pair, part, near, landed, *reduce_sems, (kind, chunk))
+        sums.append(one)
+        return one
+
+    def traveller(kind, chunk, source, place, start):
+        one = Travel(line, pair, [source], [place], *[sem.at[kind, chunk] for sem in travel_sems])
+        travels.append(one)
+        steps.append((start, one.begin))
+        for step in range(line - 1):
+            steps.append((start + (step + 1) * HOP, functools.partial(one.step, step)))
+        finish = start + line * HOP - 1.0
+        steps.append((finish, one.end))
+        return finish
+
+    def product(chunk):
+        mine = heads_ref[:, :, chunk_rows(chunk), :].reshape(tokens, query_cols)
+
+        @pl.loop(0, width // 512)
+        def _(index):
+            at = pl.ds(pl.multiple_of(index * 512, 512), 512)
+            term = contract_cols(mine, out_w[at, :]).astype(BF)
+            part[0, chunk, :, :, :, at] = term.reshape(pair, line, rows, 512)
+
+    def norm_rows(chunk):
+        mid = hidden_ref[chunk_rows(chunk), :].astype(F32) + total[...]
+        middle[chunk_rows(chunk), :] = mid
+        inverse = lax.rsqrt(jnp.mean(mid * mid, -1, keepdims=True) + EPS_NORM)
+        entry_ref[chunk, core, here] = (mid * inverse * gain_ref[...]).astype(BF)
+
+    def units_part(chunk, index, count):
+        size = units // count
+        entry = entry_ref[chunk].reshape(tokens, width)
+        low, high = index * size, (index + 1) * size
+        gate = dot(entry, ffn_w[:, low:high])
+        up = dot(entry, ffn_w[:, units + low : units + high])
+        grad_act = dot(cots_ref[chunk].reshape(tokens, width), ffn_w[:, 2 * units + low : 2 * units + high])
+        sigmoid = 1.0 / (1.0 + jnp.exp(-gate))
+        silu = gate * sigmoid
+        act_ref[chunk, :, low:high] = (silu * up).astype(BF)
+        dgu_ref[chunk, :, low:high] = (grad_act * up * sigmoid * (1.0 + gate * (1.0 - sigmoid))).astype(BF)
+        dgu_ref[chunk, :, units + low : units + high] = (grad_act * silu).astype(BF)
+
+    def back_part(chunk, index, count):
+        size = width // count
+        at = slice(index * size, (index + 1) * size)
+        term = contract_cols(dgu_ref[chunk], ffn_w[at, : 2 * units]).astype(BF)
+        part[1, chunk, :, :, :, at] = term.reshape(pair, line, rows, size)
+
+    def down_part(chunk, index, count):
+        size = width // count
+        at = slice(index * size, (index + 1) * size)
+        term = contract_cols(act_ref[chunk], ffn_w[at, 2 * units :]).astype(BF)
+        part[2, chunk, :, :, :, at] = term.reshape(pair, line, rows, size)
+
+    def norm_rows_back(chunk):
+        mid = middle[chunk_rows(chunk), :]
+        inverse = lax.rsqrt(jnp.mean(mid * mid, -1, keepdims=True) + EPS_NORM)
+        normed = mid * inverse
+        grad_entry = total[...]
+        gain_term = jnp.sum(grad_entry * normed, 0, keepdims=True)
+        if chunk == 0:
+            gain_grad_ref[...] = gain_term
+        else:
+            gain_grad_ref[...] += gain_term
+        grad_normed = grad_entry * gain_ref[...]
+        grad_rows = inverse * (
+            grad_normed - normed * jnp.mean(grad_normed * normed, -1, keepdims=True)
+        )
+        grad_mid = cot_ref[chunk_rows(chunk), :].astype(F32) + grad_rows
+        grad_mid_ref[chunk_rows(chunk), :] = grad_mid
+        branch[chunk] = grad_mid.astype(BF)
+
+    def write_output(chunk):
+        output_ref[chunk_rows(chunk), :] = (middle[chunk_rows(chunk), :] + total[...]).astype(BF)
+
+    span = (line - 1) * SEND
+    ready_ffn = ready_back = 0.0
+    starts = []
+    steps.append((0.0, loads[0].wait))
+    for chunk in range(chunks):
+        cot_done = traveller(
+            0, chunk, cot_ref.at[chunk_rows(chunk)], lambda c, z, k=chunk: cots_ref.at[k, c, z], chunk * span
+        )
+        begin = 1.0 + chunk * span
+        steps.append((begin - 0.5, functools.partial(product, chunk)))
+        more, finish = reducer(0, chunk).plan(begin, total, functools.partial(norm_rows, chunk))
+        steps += more
+        arrived = traveller(1, chunk, None, lambda c, z, k=chunk: entry_ref.at[k, c, z], finish)
+        begin = max(arrived, cot_done, ready_ffn) + 0.1
+        if chunk == 0:
+            steps.append((begin, loads[1].wait))
+        count = 4
+        for index in range(count):
+            steps.append((begin + index, functools.partial(units_part, chunk, index, count)))
+        for index in range(count):
+            steps.append((begin + 4 + 0.8 * index, functools.partial(back_part, chunk, index, count)))
+        for index in range(count):
+            steps.append((begin + 7.3 + 0.5 * index, functools.partial(down_part, chunk, index, count)))
+        ready_ffn = begin + 9.5
+        begin = max(begin + 7.25, ready_back)
+        ready_back = begin + span
+        more, finish = reducer(1, chunk).plan(begin, total, functools.partial(norm_rows_back, chunk))
+        steps += more
+        traveller(
+            2,
+            chunk,
+            branch.at[chunk],
+            lambda c, z, k=chunk: branch_ref.at[c, z, pl.ds(k * rows, rows)],
+            finish,
+        )
+    for chunk in range(chunks):
+        begin = ready_back + chunk * span
+        steps += reducer(2, chunk).plan(begin, total, functools.partial(write_output, chunk))[0]
+    run_steps(steps)
+    for one in sums:
+        one.drain()
+
+
+def middle_rows(sizes, collective_id, heads, low, high, hidden, cot, gain):
+    line, pair = sizes["ctx"], sizes["core"]
+    rows, width = hidden.shape
+    chunks = 4
+    step = rows // chunks
+    tokens = pair * line * step
+    units = high.shape[1] // 3
+    query_cols = heads.shape[1]
+    any_spec = pl.BlockSpec(memory_space=pl.ANY)
+    vmem = pl.BlockSpec(memory_space=pltpu.VMEM)
+    shape = jax.ShapeDtypeStruct
+    dma = pltpu.SemaphoreType.DMA
+    outs = pl.pallas_call(
+        functools.partial(middle_kernel, line, pair, chunks),
+        out_shape=[
+            shape((rows, width), BF),
+            shape((rows, width), F32),
+            shape((1, width), F32),
+            shape((pair, line, rows, width), BF),
+            shape((chunks, pair, line, step, width), BF),
+            shape((chunks, pair, line, step, width), BF),
+            shape((chunks, tokens, units), BF),
+            shape((chunks, tokens, 2 * units), BF),
+        ],
+        in_specs=[vmem, any_spec, any_spec, vmem, vmem, vmem],
+        out_specs=[vmem, vmem, vmem, any_spec, vmem, vmem, vmem, vmem],
+        scratch_shapes=[
+            pltpu.VMEM((width, query_cols), BF),
+            pltpu.VMEM(high.shape, BF),
+            *Reduce.room(line, pair, step, width, 3, chunks),
+            pltpu.VMEM((step, width), F32),
+            pltpu.VMEM((rows, width), F32),
+            pltpu.VMEM((chunks, step, width), BF),
+            dma((2,)),
+            *Reduce.sems(3, chunks)(line),
+            dma((3, chunks, 1)),
+            *[dma((3, chunks, 1, 2, line))] * 4,
+        ],
+        compiler_params=pltpu.CompilerParams(
+            collective_id=collective_id, has_side_effects=True, vmem_limit_bytes=63 * 2**20
+        ),
+    )(heads.reshape(pair, line, rows, query_cols), low, high, hidden, cot, gain)
+    return list(outs[:3]) + [out.reshape(-1, out.shape[-1]) for out in outs[3:]]
 
 
 def blocks_in_order(line, pair):
@@ -408,7 +633,7 @@
     greet_all(sizes)
     order = blocks_in_order(line, pair)
     me = at["ctx"] * pair + at["core"]
-    travel = Travel(line, pair, [hidden_ref], [hidden_out], *travel_sems)
+    travel = Travel(line, pair, [hidden_ref], [lambda c, z: hidden_out.at[c, z]], *travel_sems)
     travel.begin()
 
     def first(kind, index):
@@ -875,8 +1100,6 @@
     out_c = low[:, qkv_width : qkv_width + query_cols]
     gains = low[:, qkv_width + query_cols :].astype(F32)[:, :2].T
     gain_one, gain_two = gains[0], gains[1]
-    gate_up_c = high[:, : 2 * unit_cols]
-    down_c = high[:, 2 * unit_cols :]
 
     def normed(rows):
         inverse = lax.rsqrt(jnp.mean(rows * rows, -1, keepdims=True) + EPS_NORM)
@@ -885,7 +1108,6 @@
     row_in = hidden[0].astype(F32)
     normed_one, inv_one = normed(row_in)
     entry_one = (normed(hidden_all.astype(F32))[0] * gain_one).astype(BF)
-    (cot,) = gather_tokens(sizes, 1, cotangent[0])
 
     projected = dot(entry_one, qkv_c).reshape(pair, total_rows, qkv_width)
     queries = projected[..., :query_cols].reshape(pair, total_rows, heads, HD)
@@ -910,27 +1132,10 @@
     attended = product("skgtu,sukd->stkgd", prob_low, value_rows).astype(BF)
     attended = attended.reshape(pair * total_rows, query_cols)
 
-    middle = row_in + scatter_tokens(sizes, 2, contract_cols(attended, out_c).astype(BF))
-    normed_two, inv_two = normed(middle)
-    (entry_two,) = gather_tokens(sizes, 3, (normed_two * gain_two).astype(BF))
-
-    gate_up = dot(entry_two, gate_up_c)
-    gate_part = gate_up[:, :unit_cols]
-    up_part = gate_up[:, unit_cols:]
-    sigmoid_gate = jax.nn.sigmoid(gate_part)
-    silu_gate = gate_part * sigmoid_gate
-    activated = (silu_gate * up_part).astype(BF)
-    summed = scatter_tokens(sizes, 4, contract_cols(activated, down_c).astype(BF))
-    output = (middle + summed).astype(BF)[None]
-    grad_act = dot(cot, down_c)
-    grad_gate = grad_act * up_part * sigmoid_gate * (1.0 + gate_part * (1.0 - sigmoid_gate))
-    grad_up = grad_act * silu_gate
-    grad_gu = jnp.concatenate([grad_gate, grad_up], 1).astype(BF)
-    grad_entry_two = scatter_tokens(sizes, 5, contract_cols(grad_gu, gate_up_c).astype(BF))
-    grad_top = cotangent[0].astype(F32)
-    grad_mid_norm, grad_gain_two = norm_back(grad_entry_two, normed_two, inv_two, gain_two)
-    grad_middle = grad_top + grad_mid_norm
-    (grad_branch,) = gather_tokens(sizes, 6, grad_middle.astype(BF))
+    output, grad_middle, grad_gain_two, grad_branch, entry_two, cot, activated, grad_gu = middle_rows(
+        sizes, 1, attended, low, high, hidden[0], cotangent[0], gain_two[None]
+    )
+    output = output[None]
 
     grad_attended = dot(grad_branch, out_c).astype(BF)
     grad_heads = grad_attended.reshape(pair, total_rows, kv_heads, ratio, HD)
@@ -951,15 +1156,15 @@
         ],
         1,
     ).astype(BF)
-    grad_entry_one = scatter_tokens(sizes, 7, contract_cols(grad_projected, qkv_c).astype(BF))
+    grad_entry_one = scatter_tokens(sizes, 2, contract_cols(grad_projected, qkv_c).astype(BF))
     grad_row_norm, grad_gain_one = norm_back(grad_entry_one, normed_one, inv_one, gain_one)
     grad_hidden = (grad_middle + grad_row_norm).astype(BF)[None]
 
     grad_gate, grad_up, grad_down, grad_query, grad_key_value, grad_out = collect_grads(
-        sizes, 8, entry_two, grad_gu, cot, activated, entry_one, grad_projected, grad_branch, attended
+        sizes, 3, entry_two, grad_gu, cot, activated, entry_one, grad_projected, grad_branch, attended
     )
     grad_gains = lax.psum_scatter(
-        jnp.stack([grad_gain_one, grad_gain_two]), everyone, scatter_dimension=1, tiled=True
+        jnp.stack([grad_gain_one, grad_gain_two[0]]), everyone, scatter_dimension=1, tiled=True
     )
     rows = w_qkv.shape[0]
     grad_key_value = grad_key_value.reshape(rows, group, 2, kv_cols).transpose(0, 2, 1, 3)

time: 896 us -> 708 us (0.79)
  Pallas kernels: 710 us -> 584 us
  matrix products: 80.3 us -> 29.4 us
  other arithmetic: 39.8 us -> 30.2 us
    pallas_call x7 -> x2, Pallas kernels: 375 us -> 242 us  [the longest x1 199 us: middle_rows(): pl.pallas_call(functools.partial(middle_kernel, line, pair, chunks), out_...]
    dot_general x4 -> x1, matrix products: 29.8 us -> 2.37 us  [contract_cols(): lax.dot_general(left_arr, right_arr, (((1,), (1,)), ((), ())), preferred_...]
    dot_general x4 -> x2, matrix products: 28.7 us -> 5.62 us  [dot(): return jnp.dot(left, right, preferred_element_type=F32)]
    unnamed x75 -> x63, local copies, waits for them, and re-layouts: 18.2 us -> 17.3 us
  transfers between devices with their start and end apart: 1 -> 1, of which waited for: 0 -> 0; matrix products, arithmetic and copies ran while one was open for 3% -> 2% of each run, Pallas kernels for 28% -> 28%
where the time goes in v3:
time: 708 us; the launch traced here: 699 us
  Pallas kernels  584 us (82%)
  local copies, waits for them, and re-layouts  40.4 us (6%)
  other arithmetic  30.2 us (4%)
  matrix products  29.4 us (4%)
  between operations  14.7 us (2%)
    pallas_call x1, Pallas kernels, middle_rows(): pl.pallas_call(functools.partial(middle_kernel, line, pair, chunks), out_...  199 us
    pallas_call x1, Pallas kernels, collect_grads(): pl.pallas_call(functools.partial(collect_kernel, sizes, widths), out_shap...  158 us
    pallas_call x1, Pallas kernels, spread_weights(): pl.pallas_call(functools.partial(spread_kernel, sizes), out_shape=[jax.Sh...  150 us
    pallas_call x1, Pallas kernels, scatter_tokens(): pl.pallas_call(functools.partial(scatter_kernel, line, pair, chunks), out...  42.6 us
    pallas_call x4, Pallas kernels, adamw_columns(): pl.pallas_call(functools.partial(adamw_kernel, step_rate, decay_rate), gr...  34.1 us
    dot_general x6, matrix products, product(): return jnp.einsum(spec, left, right, preferred_element_type=F32)  21.4 us
    unnamed x63, local copies, waits for them, and re-layouts  17.3 us
  transfers between devices with their start and end apart: 1, of which 0 were waited for; matrix products, arithmetic and copies ran while one was open for 2% of the time, Pallas kernels for 28%

profile of v3, /device:TPU:0, one launch (start us, length us, event | category | flops | bytes accessed | tf_op | source)
XLA Modules:
  0.0 698.6 jit_solution(6779880761304033856)
XLA Ops:
  9.1 1.6 copy-done.4
  12.8 149.8 %shard_map.260 = (bf16[2,4,2,2,64,768]{5,4,3,2,1,0:T(8,128)(2,1)S(1)}, bf16[2,4,2,2,64,3072]{5,4,3,2,1,0:T(8,128)(2,1)}, bf16[2,4,128,2048]{3,2,1,0:T(8,128)(2,1)S(1)}) custom-call(f32[64,3072]{1,0:T(8,128)S(1)} %copy-done.7, f32[64,2048]{1,0:T(8,128)S(1)} %copy-done.8, f32[64,16384]{1,0:T(8,128)} %weight_ref.6, f32[64,8192]{1,0:T(8,128)S(1)} %copy-done.4, ...), custom_call_target="tpu_custom_call" | custom-call | tf_op jit(solution)/shard_map/pallas_call | solution.py:772
  162.7 2.0 copy-done
  165.8 1.8 copy.116
  168.3 3.4 multiply_reduce_fusion
  172.8 1.9 fusion.17
  181.9 1.8 fusion.9
  183.7 1.6 copy-done.9
  185.3 3.4 fusion.27
  190.7 199.1 %shard_map.261 = (bf16[128,2048]{1,0:T(8,128)(2,1)}, f32[128,2048]{1,0:T(8,128)}, f32[1,2048]{1,0:T(1,128)}, bf16[2,4,128,2048]{3,2,1,0:T(8,128)(2,1)}, bf16[4,2...) custom-call(bf16[2,4,128,256]{3,2,1,0:T(8,128)(2,1)} %copy.73.refs_0, ...), custom_call_target="tpu_custom_call" | custom-call | tf_op jit(solution)/shard_map/pallas_call | solution.py:548
  389.8 3.7 convolution_convert_fusion.1
  394.6 5.1 fusion.2
  399.7 5.5 fusion.36
  405.4 5.1 fusion.11
  410.5 2.3 bitcast_multiply_fusion.3
  413.0 1.7 copy.101
  414.8 2.5 reshape.317
  417.3 2.7 copy.99
  420.0 3.2 reshape.315
  424.9 3.2 reshape.316
  428.1 3.6 broadcast_multiply_fusion
  432.2 1.9 add_convert_fusion
  434.7 2.4 convolution_convert_fusion
  437.1 42.6 %shard_map.262 = f32[128,2048]{1,0:T(8,128)S(1)} custom-call(bf16[2,4,128,2048]{3,2,1,0:T(8,128)(2,1)S(1)} %bitcast.194), custom_call_target="tpu_custom_call" | custom-call | tf_op jit(solution)/shard_map/pallas_call | solution.py:375
  481.6 1.8 copy.102
  484.8 5.2 fusion.1.refs_4_
  490.0 158.3 %shard_map.263 = (bf16[64,8192]{1,0:T(8,128)(2,1)}, bf16[64,8192]{1,0:T(8,128)(2,1)}, bf16[64,8192]{1,0:T(8,128)(2,1)}, bf16[64,2048]{1,0:T(8,128)(2,1)}, bf16[6...) custom-call(bf16[1024,2048]{1,0:T(8,128)(2,1)} %bitcast.202, bf16[1024,2048]{1,0:T(8,128)(2,1)} %bitcast.204, ...), custom_call_target="tpu_custom_call" | custom-call | tf_op jit(solution)/shard_map/pallas_call | solution.py:990
  649.8 3.0 pad_maximum_fusion.grad_ref
  654.7 17.7 %shard_map.266 = (f32[64,16384]{1,0:T(8,128)}, f32[64,16384]{1,0:T(8,128)}, f32[2,64,16384]{2,1,0:T(8,128)}) custom-call(bf16[64,16384]{1,0:T(8,128)(2,1)} %pad_maximum_fusion.grad_ref, f32[64,16384]{1,0:T(8,128)} %weight_ref.6, f32[2,64,16384]{2,1,0:T(8,128)} %state_ref.6), custom_call_target="tpu_custom_call" | custom-call | tf_op jit(solution)/shard_map/pallas_call | solution.py:1028
  672.4 9.2 %shard_map.267 = (f32[64,8192]{1,0:T(8,128)}, f32[64,8192]{1,0:T(8,128)}, f32[2,64,8192]{2,1,0:T(8,128)}) custom-call(bf16[64,8192]{1,0:T(8,128)(2,1)} %get-tuple-element.65.grad_ref, f32[64,8192]{1,0:T(8,128)} %weight_ref.7, f32[2,64,8192]{2,1,0:T(8,128)} %state_ref.7), custom_call_target="tpu_custom_call" | custom-call | tf_op jit(solution)/shard_map/pallas_call | solution.py:1028
  681.6 4.5 shard_map.264
  686.1 2.7 shard_map.265
  (107 shorter events, 29.6 us)
Async XLA Ops:
  7.2 681.6 %reduce-scatter.4.cloned.1.call-start = ((), (), s32[]{:S(2)}) async-start(), calls=%async_computation.1 | async-start | bytes 1081344
  8.0 1.0 copy-start.2
  9.1 1.6 copy-start.4
  10.7 1.1 copy-start.7
  11.8 1.0 copy-start.8
  162.7 2.0 copy-start
  164.7 8.1 %copy-start.5 = (bf16[2,4,2,2,64,768]{5,4,3,2,1,0:T(8,128)(2,1)}, bf16[2,4,2,2,64,768]{5,4,3,2,1,0:T(8,128)(2,1)S(1)}, u32[]{:S(2)}) copy-start(bf16[2,4,2,2,64,768]{5,4,3,2,1,0:T(8,128)(2,1)S(1)} %get-tuple-element.47) | copy-start | bytes 9437188
  167.7 4.0 copy-start.1
  172.8 3.1 copy-start.27
  174.7 1.1 copy-start.13
  180.4 1.5 copy-start.14
  181.9 3.4 copy-start.9
  188.7 0.8 copy-start.12
  399.7 5.5 copy-start.3
  405.4 5.1 copy-start.15
  410.5 2.5 copy-start.10
  414.8 8.5 %copy-start.17 = (f32[512,64]{1,0:T(8,128)S(1)}, f32[512,64]{1,0:T(8,128)}, u32[]{:S(2)}) copy-start(f32[512,64]{1,0:T(8,128)} %copy.114) | copy-start | bytes 393220
  420.0 8.1 %copy-start.16 = (f32[512,64]{0,1:T(8,128)S(1)}, f32[512,64]{0,1:T(8,128)}, u32[]{:S(2)}) copy-start(f32[512,64]{0,1:T(8,128)} %get-tuple-element.87) | copy-start | bytes 393220
  424.9 6.9 copy-start.20
  428.1 3.9 copy-start.22
  432.2 2.5 copy-start.6
  434.7 2.4 copy-start.11
  437.1 43.0 %copy-start.23 = (f32[1,2048]{1,0:T(1,128)S(1)}, f32[1,2048]{1,0:T(1,128)}, u32[]{:S(2)}) copy-start(f32[1,2048]{1,0:T(1,128)} %get-tuple-element.52) | copy-start | bytes 24580
  648.3 4.5 copy-start.18
  649.6 4.4 copy-start.21
  672.4 17.2 %copy-start.24 = (f32[2,64]{1,0:T(2,128)S(1)}, f32[2,64]{1,0:T(2,128)}, u32[]{:S(2)}) copy-start(f32[2,64]{1,0:T(2,128)} %param.16) | copy-start | bytes 1540
  672.4 17.2 %copy-start.26 = (f32[2,2,64]{2,1,0:T(2,128)S(1)}, f32[2,2,64]{2,1,0:T(2,128)}, u32[]{:S(2)}) copy-start(f32[2,2,64]{2,1,0:T(2,128)} %param.21) | copy-start | bytes 3076
  672.4 18.4 %copy-start.19 = (bf16[128,2048]{1,0:T(8,128)(2,1)S(1)}, bf16[128,2048]{1,0:T(8,128)(2,1)}, u32[]{:S(2)}) copy-start(bf16[128,2048]{1,0:T(8,128)(2,1)} %get-tuple-element.49) | copy-start | bytes 1572868
  689.6 2.0 copy-start.25
Sparse Core Ops, SparseCore 0:
  481.7 135.7 reduce-scatter.3

commit v4 on v3

--- a/solution.py
+++ b/solution.py
@@ -339,54 +339,6 @@
 def run_steps(steps):
     for _, step in sorted(steps, key=lambda item: item[0]):
         step()
-
-
-def scatter_kernel(line, pair, chunks, terms_ref, out_ref, part, near, landed, total, load_sem, *sems):
-    rows = part.shape[-2]
-    loads = [
-        pltpu.make_async_copy(
-            terms_ref.at[:, :, pl.ds(chunk * rows, rows)], part.at[chunk], load_sem.at[chunk]
-        )
-        for chunk in range(chunks)
-    ]
-    for load in loads:
-        load.start()
-    greet_line(line, pair)
-    sums = [Reduce(line, pair, part, near, landed, *sems, (chunk,)) for chunk in range(chunks)]
-    steps = []
-    for chunk, one in enumerate(sums):
-
-        def after(chunk=chunk):
-            out_ref[chunk * rows : (chunk + 1) * rows, :] = total[...]
-
-        start = chunk * (line - 1) * SEND
-        steps.append((start, loads[chunk].wait))
-        steps += one.plan(start, total, after)[0]
-    run_steps(steps)
-    for one in sums:
-        one.drain()
-
-
-def scatter_tokens(sizes, collective_id, terms):
-    line, pair = sizes["ctx"], sizes["core"]
-    columns = terms.shape[1]
-    rows = terms.shape[0] // (line * pair)
-    chunks = 4
-    return pl.pallas_call(
-        functools.partial(scatter_kernel, line, pair, chunks),
-        out_shape=jax.ShapeDtypeStruct((rows, columns), F32),
-        in_specs=[pl.BlockSpec(memory_space=pl.ANY)],
-        out_specs=pl.BlockSpec(memory_space=pltpu.VMEM),
-        scratch_shapes=[
-            *Reduce.room(line, pair, rows // chunks, columns, chunks),
-            pltpu.VMEM((rows // chunks, columns), F32),
-            pltpu.SemaphoreType.DMA((chunks,)),
-            *Reduce.sems(chunks)(line),
-        ],
-        compiler_params=pltpu.CompilerParams(
-            collective_id=collective_id, has_side_effects=True, vmem_limit_bytes=40 * 2**20
-        ),
-    )(terms.reshape(pair, line, rows, columns))
 
 
 def middle_kernel(line, pair, chunks, *refs):
@@ -797,167 +749,628 @@
     return low.reshape(-1, tall), high.reshape(-1, wide), tokens.reshape(-1, hidden.shape[1])
 
 
-def collect_kernel(sizes, widths, *refs):
-    many = len(widths)
-    pieces = grad_pieces(sizes)
-    lefts, rights = refs[: 2 * many : 2], refs[1 : 2 * many : 2]
-    refs = refs[2 * many :]
-    outs, refs = refs[: len(pieces)], refs[len(pieces) :]
-    held, refs = refs[: 2 * many], refs[2 * many :]
-    terms, near, far_in = refs[:3]
-    load_sem, own_sem, a_send, a_recv, b_send, b_recv, f_send, f_recv = refs[3:]
-    line, pair = sizes["ctx"], sizes["core"]
-    rows = terms.shape[-2]
-    across = sizes["x"] * pair * rows
-    at = {name: lax.axis_index(name) for name in ("dp", "ctx", "x", "core")}
-    me = at["ctx"] * pair + at["core"]
-    loads = [
-        pltpu.make_async_copy(source, target, load_sem.at[i])
-        for i, (source, target) in enumerate(zip((r for two in zip(lefts, rights) for r in two), held))
-    ]
-    for load in loads:
-        load.start()
-    greet_all(sizes)
-    away = sorted(range(line), key=lambda d: -min(d, line - d))
-    order = [(dz, dc) for dz in away for dc in range(pair)]
-
-    def spot_of(index):
-        dz, dc = order[index]
-        return wrap(at["ctx"] + dz, line), wrap(at["core"] + dc, pair)
-
-    def axes(index):
-        dz, dc = order[index]
-        return ("dp", "x") if (dz + dc) % 2 == 0 else ("x", "dp")
-
-    def multiply(tick):
-        z = wrap(at["ctx"] + away[tick], line)
+class Collect:
+    AXES = (("dp", "x"), ("x", "dp"))
+
+    @staticmethod
+    def room(sizes, rows, width):
+        room = [pltpu.VMEM((sizes["ctx"], sizes["dp"], sizes["x"], sizes["core"], rows, width), BF)]
+        for parity, (name, other) in enumerate(Collect.AXES):
+            count = sum((dz + dc) % 2 == parity for dz, dc in blocks_in_order(sizes["ctx"], sizes["core"]))
+            room.append(pltpu.VMEM((max(1, count), (sizes[name] - 1) * sizes[other], rows, width), BF))
+            room.append(pltpu.VMEM((max(1, count), sizes[other] - 1, rows, width), BF))
+        return room
+
+    @staticmethod
+    def sems(sizes, pieces):
+        dma = pltpu.SemaphoreType.DMA
+        group, steps = sizes["ctx"] * sizes["core"], max(sizes["dp"], sizes["x"])
+        return (
+            [dma((pieces,))]
+            + [dma((group, steps, steps))] * 2
+            + [dma((group, steps))] * 2
+            + [dma((group, pieces))] * 2
+        )
+
+    def __init__(self, sizes, widths, pieces, room, sems):
+        self.sizes, self.widths, self.pieces = sizes, widths, pieces
+        self.terms = room[0]
+        self.near, self.far_in = room[1::2], room[2::2]
+        self.own_sem, *rest = sems
+        self.a_sems, self.b_sems, self.f_sems = rest[0:2], rest[2:4], rest[4:6]
+        self.line, self.pair = sizes["ctx"], sizes["core"]
+        self.rows = self.terms.shape[-2]
+        self.at = {name: lax.axis_index(name) for name in ("dp", "ctx", "x", "core")}
+        self.me = self.at["ctx"] * self.pair + self.at["core"]
+        self.away = sorted(range(self.line), key=lambda d: -min(d, self.line - d))
+        self.order = [(dz, dc) for dz in self.away for dc in range(self.pair)]
+
+    def spot_of(self, index, sign=1):
+        dz, dc = self.order[index]
+        return wrap(self.at["ctx"] + sign * dz, self.line), wrap(self.at["core"] + sign * dc, self.pair)
+
+    def parity(self, index):
+        return sum(self.order[index]) % 2
+
+    def axes(self, index):
+        return self.AXES[self.parity(index)]
+
+    def slot(self, index):
+        return sum(self.parity(before) == self.parity(index) for before in range(index))
+
+    def indices(self, tick):
+        return range(tick * self.pair, (tick + 1) * self.pair)
+
+    def lanes(self, tick, dp):
+        across = self.sizes["x"] * self.pair * self.rows
+        z = wrap(self.at["ctx"] + self.away[tick], self.line)
+        return pl.ds(pl.multiple_of((dp * self.line + z) * across, 128), across)
+
+    def multiply(self, tick, lefts, rights):
         start = 0
-        for item, width in enumerate(widths):
-            left, right = held[2 * item], held[2 * item + 1]
+        for left, right, width in zip(lefts, rights, self.widths):
             step = math.gcd(width, 512)
 
-            @pl.loop(0, sizes["dp"])
+            @pl.loop(0, self.sizes["dp"])
             def _(dp, left=left, right=right, start=start, width=width, step=step):
-                lanes = pl.ds(pl.multiple_of((dp * line + z) * across, 128), across)
-                left_t = left[:, lanes].T
+                left_t = left[dp].T
 
                 @pl.loop(0, width // step)
                 def _(part):
                     columns = pl.ds(pl.multiple_of(part * step, 128), step)
                     into = pl.ds(pl.multiple_of(start + part * step, 128), step)
                     product = dot(left_t, right[:, columns]).astype(BF)
-                    for x in range(sizes["x"]):
-                        for core in range(pair):
-                            low = (x * pair + core) * rows
-                            terms[tick, dp, x, core, :, into] = product[low : low + rows]
+                    for x in range(self.sizes["x"]):
+                        for core in range(self.pair):
+                            low = (x * self.pair + core) * self.rows
+                            self.terms[tick, dp, x, core, :, into] = product[low : low + self.rows]
 
             start += width
 
-    def block_terms(index, first_at, other_at):
-        spot = {axes(index)[0]: first_at, axes(index)[1]: other_at}
-        return terms.at[index // pair, spot["dp"], spot["x"], spot_of(index)[1]]
-
-    def hop_one(index, step, place):
-        name = axes(index)[0]
-        to = wrap(at[name] + step, sizes[name])
+    def block_terms(self, index, first_at, other_at):
+        name, other = self.axes(index)
+        spot = {name: first_at, other: other_at}
+        return self.terms.at[index // self.pair, spot["dp"], spot["x"], self.spot_of(index)[1]]
+
+    def landing(self, index, step, place):
+        at = (step - 1) * self.sizes[self.axes(index)[1]] + place
+        return self.near[self.parity(index)].at[self.slot(index), at]
+
+    def far_landing(self, index, far):
+        return self.far_in[self.parity(index)].at[self.slot(index), far - 1]
+
+    def hop_one(self, index, step, place):
+        name = self.axes(index)[0]
+        to = wrap(self.at[name] + step, self.sizes[name])
+        sems = [sem.at[index, step, place] for sem in self.a_sems]
         return remote(
-            block_terms(index, to, place),
-            near.at[index, (step - 1) * sizes[axes(index)[1]] + place],
-            a_send.at[index, step, place],
-            a_recv.at[index, step, place],
-            **{name: to},
-        )
-
-    def hop_two(index, far):
-        name, other = axes(index)
-        to = wrap(at[other] + far, sizes[other])
+            self.block_terms(index, to, place), self.landing(index, step, place), *sems, **{name: to}
+        )
+
+    def hop_two(self, index, far):
+        name, other = self.axes(index)
+        to = wrap(self.at[other] + far, self.sizes[other])
+        sems = [sem.at[index, far] for sem in self.b_sems]
         return remote(
-            block_terms(index, at[name], to),
-            far_in.at[index, far - 1],
-            b_send.at[index, far],
-            b_recv.at[index, far],
-            **{other: to},
-        )
-
-    def done(index):
-        name, other = axes(index)
-        return block_terms(index, at[name], at[other])
-
-    def piece_at(piece, member):
-        _, width, offset = pieces[piece]
-        return outs[piece].at[:, pl.ds(pl.multiple_of(member * width, 128), width)]
-
-    def last(index, piece):
-        z, c = spot_of(index)
-        _, width, offset = pieces[piece]
-        source = done(index).at[:, pl.ds(offset, width)]
-        target = piece_at(piece, me)
-        if index == len(order) - pair:
-            return pltpu.make_async_copy(source, target, own_sem.at[piece])
-        return remote(
-            source, target, f_send.at[index, piece], f_recv.at[index, piece], ctx=z, core=c
-        )
-
-    def last_came(index, piece):
-        dz, dc = order[index]
-        z, c = wrap(at["ctx"] - dz, line), wrap(at["core"] - dc, pair)
-        spot = piece_at(piece, z * pair + c)
-        return remote(
-            spot, spot, f_send.at[index, piece], f_recv.at[index, piece], core=at["core"]
-        )
-
-    def sum_one(index):
-        name, other = axes(index)
-        for far in list(range(1, sizes[other])) + [0]:
-            place = wrap(at[other] + far, sizes[other])
-            for step in range(1, sizes[name]):
-                hop_one(index, step, place).wait_recv()
-            kept = block_terms(index, at[name], place)
-            add_rows(rows, kept, kept, *[near.at[index, (step - 1) * sizes[other] + place] for step in range(1, sizes[name])])
-            if far:
-                hop_two(index, far).start()
-
-    def sum_two(index):
-        other = axes(index)[1]
-        for far in range(1, sizes[other]):
-            hop_two(index, far).wait_recv()
-        add_rows(
-            rows, done(index), done(index), *[far_in.at[index, far - 1] for far in range(1, sizes[other])]
-        )
-        for piece in range(len(pieces)):
-            last(index, piece).start()
-
-    late, later = 1, 2
-    for tick in range(line + later):
-        if tick < line:
-            if tick == 0:
-                for load in loads:
-                    load.wait()
-            multiply(tick)
-            for index in range(tick * pair, (tick + 1) * pair):
-                name, other = axes(index)
-                for far in list(range(1, sizes[other])) + [0]:
-                    for step in range(1, sizes[name]):
-                        hop_one(index, step, wrap(at[other] + far, sizes[other])).start()
-        if late <= tick < line + late:
-            for index in range((tick - late) * pair, (tick - late + 1) * pair):
-                sum_one(index)
-        if tick >= later:
-            for index in range((tick - later) * pair, (tick - later + 1) * pair):
-                sum_two(index)
-    for index in range(len(order)):
-        name, other = axes(index)
-        for step in range(1, sizes[name]):
-            for place in range(sizes[other]):
-                hop_one(index, step, place).wait_send()
-        for far in range(1, sizes[other]):
-            hop_two(index, far).wait_send()
-        for piece in range(len(pieces)):
-            if index == len(order) - pair:
-                last(index, piece).wait()
-            else:
-                last(index, piece).wait_send()
-                last_came(index, piece).wait_recv()
+            self.block_terms(index, self.at[name], to), self.far_landing(index, far), *sems, **{other: to}
+        )
+
+    def done(self, index):
+        name, other = self.axes(index)
+        return self.block_terms(index, self.at[name], self.at[other])
+
+    def stays(self, index):
+        return self.order[index] == (0, 0)
+
+    def piece_at(self, piece, member):
+        out, width, _ = self.pieces[piece]
+        return out.at[:, pl.ds(pl.multiple_of(member * width, 128), width)]
+
+    def last(self, index, piece):
+        z, c = self.spot_of(index)
+        _, width, offset = self.pieces[piece]
+        source = self.done(index).at[:, pl.ds(offset, width)]
+        target = self.piece_at(piece, self.me)
+        if self.stays(index):
+            return pltpu.make_async_copy(source, target, self.own_sem.at[piece])
+        return remote(source, target, *[sem.at[index, piece] for sem in self.f_sems], ctx=z, core=c)
+
+    def last_came(self, index, piece):
+        z, c = self.spot_of(index, -1)
+        spot = self.piece_at(piece, z * self.pair + c)
+        sems = [sem.at[index, piece] for sem in self.f_sems]
+        return remote(spot, spot, *sems, core=self.at["core"])
+
+    def places(self, index):
+        other = self.axes(index)[1]
+        size = self.sizes[other]
+        return [(far, wrap(self.at[other] + far, size)) for far in list(range(1, size)) + [0]]
+
+    def send_one(self, tick):
+        for index in self.indices(tick):
+            for _, place in self.places(index):
+                for step in range(1, self.sizes[self.axes(index)[0]]):
+                    self.hop_one(index, step, place).start()
+
+    def sum_one(self, tick):
+        for index in self.indices(tick):
+            name = self.axes(index)[0]
+            for far, place in self.places(index):
+                steps = range(1, self.sizes[name])
+                for step in steps:
+                    self.hop_one(index, step, place).wait_recv()
+                kept = self.block_terms(index, self.at[name], place)
+                add_rows(self.rows, kept, kept, *[self.landing(index, step, place) for step in steps])
+                if far:
+                    self.hop_two(index, far).start()
+
+    def sum_two(self, tick):
+        for index in self.indices(tick):
+            fars = range(1, self.sizes[self.axes(index)[1]])
+            for far in fars:
+                self.hop_two(index, far).wait_recv()
+            done = self.done(index)
+            add_rows(self.rows, done, done, *[self.far_landing(index, far) for far in fars])
+            for piece in range(len(self.pieces)):
+                self.last(index, piece).start()
+
+    def drain(self):
+        for index in range(len(self.order)):
+            name, other = self.axes(index)
+            for step in range(1, self.sizes[name]):
+                for place in range(self.sizes[other]):
+                    self.hop_one(index, step, place).wait_send()
+            for far in range(1, self.sizes[other]):
+                self.hop_two(index, far).wait_send()
+            for piece in range(len(self.pieces)):
+                if self.stays(index):
+                    self.last(index, piece).wait()
+                else:
+                    self.last(index, piece).wait_send()
+                    self.last_came(index, piece).wait_recv()
+
+
+def lane_index(shape):
+    return lax.broadcasted_iota(jnp.int32, shape, len(shape) - 1)
+
+
+def turned(values):
+    half, columns = HD // 2, values.shape[1]
+    ahead = pltpu.roll(values, columns - half, 1)
+    behind = pltpu.roll(values, half, 1)
+    return jnp.where(lane_index(values.shape) % HD < half, ahead, behind)
+
+
+def only_head(values, head):
+    return jnp.where(lane_index(values.shape) // HD == head, values, jnp.zeros_like(values))
+
+
+def both_halves(values, head):
+    wide = values.astype(F32)
+    return jnp.where(lane_index(wide.shape) // HD == head, wide, pltpu.roll(wide, HD, 1)).astype(BF)
+
+
+def softmax_rows(queries, keys, visible):
+    scores = contract_cols(queries, keys) * HD ** (-0.5)
+    scores = jnp.where(visible, scores, NEG_FILL)
+    exponent = jnp.exp(scores - jnp.max(scores, -1, keepdims=True))
+    return exponent / jnp.sum(exponent, -1, keepdims=True)
+
+
+def query_rows(total_rows):
+    return min(total_rows, 2**18 // total_rows)
+
+
+def each_query_block(total_rows, heads, pos_col, pos_row):
+    size = query_rows(total_rows)
+    for low in range(0, total_rows, size):
+        visible = pos_row[...] <= pos_col[low : low + size, :]
+        for lane in range(0, heads * HD, 2 * HD):
+            yield low, size, visible, lane
+
+
+def attend_kernel(
+    hidden_ref, low_ref, gain_ref, cos_ref, sin_ref, pos_col, pos_row, entry_ref, qkv_ref, heads_ref, qkv_w, load_sem
+):
+    load = pltpu.make_async_copy(low_ref.at[:, pl.ds(0, qkv_w.shape[1])], qkv_w, load_sem)
+    load.start()
+    tokens, total_rows = hidden_ref.shape[0], cos_ref.shape[0]
+    query_cols = heads_ref.shape[1]
+    step = 256
+    load.wait()
+
+    @pl.loop(0, tokens // step)
+    def _(index):
+        at = pl.ds(pl.multiple_of(index * step, step), step)
+        table_at = pl.ds(pl.multiple_of(lax.rem(index * step, total_rows), step), step)
+        rows = hidden_ref[at, :].astype(F32)
+        inverse = lax.rsqrt(jnp.mean(rows * rows, -1, keepdims=True) + EPS_NORM)
+        entry = (rows * inverse * gain_ref[...]).astype(BF)
+        entry_ref[at, :] = entry
+        projected = dot(entry, qkv_w[...])
+        rotated = projected * cos_ref[table_at, :] + turned(projected) * sin_ref[table_at, :]
+        qkv_ref[at, :] = rotated.astype(BF)
+
+    @pl.loop(0, tokens // total_rows)
+    def _(sequence):
+        start = sequence * total_rows
+        both = qkv_ref[pl.ds(pl.multiple_of(start, total_rows), total_rows), query_cols:]
+        keys, values = both_halves(both, 0), both_halves(both, 1)
+        for low, size, visible, lane in each_query_block(total_rows, query_cols // HD, pos_col, pos_row):
+            at = pl.ds(pl.multiple_of(start + low, 128), size)
+            queries = qkv_ref[at, lane : lane + 2 * HD]
+            pair = [
+                dot(softmax_rows(only_head(queries, head), keys, visible).astype(BF), values)
+                for head in range(2)
+            ]
+            heads_ref[at, lane : lane + 2 * HD] = jnp.where(
+                lane_index(pair[0].shape) < HD, pair[0], pair[1]
+            ).astype(BF)
+
+
+def attend(hidden_all, low, gain, tables):
+    tokens, width = hidden_all.shape
+    qkv_cols = tables[0].shape[1]
+    query_cols = qkv_cols - 2 * HD
+    vmem = pl.BlockSpec(memory_space=pltpu.VMEM)
+    return pl.pallas_call(
+        attend_kernel,
+        out_shape=[
+            jax.ShapeDtypeStruct((tokens, width), BF),
+            jax.ShapeDtypeStruct((tokens, qkv_cols), BF),
+            jax.ShapeDtypeStruct((tokens, query_cols), BF),
+        ],
+        in_specs=[vmem, pl.BlockSpec(memory_space=pl.ANY)] + [vmem] * 5,
+        out_specs=[vmem] * 3,
+        scratch_shapes=[pltpu.VMEM((width, qkv_cols), BF), pltpu.SemaphoreType.DMA],
+        compiler_params=pltpu.CompilerParams(vmem_limit_bytes=56 * 2**20),
+    )(hidden_all, low, gain, *tables)
+
+
+class GainSum:
+    @staticmethod
+    def room(sizes, width):
+        group = sizes["ctx"] * sizes["core"]
+        return [
+            pltpu.VMEM((8, width), F32),
+            pltpu.VMEM((sizes["x"] - 1, 8, width), F32),
+            pltpu.VMEM((sizes["dp"] - 1, 8, width), F32),
+            pltpu.VMEM((group, 8, 128), F32),
+        ]
+
+    @staticmethod
+    def sems(sizes):
+        group = sizes["ctx"] * sizes["core"]
+        counts = (sizes["x"], sizes["x"], sizes["dp"], sizes["dp"], group, group)
+        return [pltpu.SemaphoreType.DMA((count,)) for count in counts]
+
+    def __init__(self, sizes, own_rows, out_ref, room, sems):
+        self.sizes, self.own_rows, self.out_ref = sizes, own_rows, out_ref
+        self.mine, self.over_x, self.over_dp, self.tiles = room
+        self.sems_of = {"x": sems[0:2], "dp": sems[2:4], "group": sems[4:6]}
+        self.at = {name: lax.axis_index(name) for name in ("dp", "ctx", "x", "core")}
+        self.order = blocks_in_order(sizes["ctx"], sizes["core"])
+
+    def hop(self, name, step):
+        into = (self.over_x if name == "x" else self.over_dp).at[step - 1]
+        sems = [sem.at[step] for sem in self.sems_of[name]]
+        return remote(self.mine, into, *sems, **{name: wrap(self.at[name] + step, self.sizes[name])})
+
+    def tile(self, index):
+        dz, dc = self.order[index]
+        z, c = wrap(self.at["ctx"] + dz, self.sizes["ctx"]), wrap(self.at["core"] + dc, self.sizes["core"])
+        place = (self.at["dp"] * self.sizes["ctx"] + z) * self.sizes["x"] + self.at["x"]
+        first = (place * self.sizes["core"] + c) * self.own_rows
+        source = self.mine.at[:, pl.ds(pl.multiple_of(first // 128 * 128, 128), 128)]
+        sems = [sem.at[index] for sem in self.sems_of["group"]]
+        if index == 0:
+            return source
+        return remote(source, self.tiles.at[index], *sems, ctx=z, core=c)
+
+    def begin(self, first, second):
+        self.mine[...] = jnp.zeros_like(self.mine)
+        self.mine[0:1, :] = first[...]
+        self.mine[1:2, :] = second[...]
+        self.send("x")
+
+    def send(self, name):
+        for step in range(1, self.sizes[name]):
+            self.hop(name, step).start()
+
+    def add(self, name):
+        for step in range(1, self.sizes[name]):
+            self.hop(name, step).wait()
+        for step in range(1, self.sizes[name]):
+            self.mine[...] += (self.over_x if name == "x" else self.over_dp)[step - 1]
+
+    def second(self):
+        self.add("x")
+        self.send("dp")
+
+    def third(self):
+        self.add("dp")
+        for index in range(1, len(self.order)):
+            self.tile(index).start()
+
+    def end(self):
+        total = self.tile(0)[...]
+        for index in range(1, len(self.order)):
+            self.tile(index).wait()
+            total = total + self.tiles[index]
+        self.out_ref[...] = total
+
+
+def closing_kernel(sizes, chunks, *refs):
+    (entry_two, dgu_ref, cot_ref, act_ref, entry_one, branch_ref, qkv_ref, heads_ref, low_ref) = refs[:9]
+    hidden_ref, grad_mid_ref, gain_ref, gain_two_ref, cos_ref, sin_ref, pos_col, pos_row = refs[9:17]
+    piece_refs, (grad_hidden_ref, gain_sum_ref) = refs[17:23], refs[23:25]
+    refs = refs[1:]
+    (left_slots, part, act, dqkv, heads, branch_slots, low_w, grad_heads, grad_proj, key_acc, value_acc) = refs[24:35]
+    near, landed, total, load_sem, left_sem, branch_sem = refs[35:41]
+    ffn_room, att_room = refs[41:46], refs[46:51]
+    ffn_sems, att_sems, reduce_sems = refs[51:58], refs[58:65], refs[65:69]
+    gain_grad_ref, gain_room, gain_sems = refs[69], refs[70:74], refs[74:80]
+    line, pair = sizes["ctx"], sizes["core"]
+    rows = part.shape[-2]
+    block_rows, width = hidden_ref.shape
+    tokens, total_rows = qkv_ref.shape[0], cos_ref.shape[0]
+    query_cols = heads.shape[1]
+    qkv_cols = dqkv.shape[1]
+    loads = {
+        "dgu": pltpu.make_async_copy(dgu_ref, part, load_sem.at[0]),
+        "act": pltpu.make_async_copy(act_ref, act, load_sem.at[1]),
+        "heads": pltpu.make_async_copy(heads_ref, heads, load_sem.at[2]),
+        "low": pltpu.make_async_copy(low_ref.at[:, pl.ds(0, low_w.shape[1])], low_w, load_sem.at[3]),
+    }
+    names = grad_pieces(sizes)
+    shift = names[3][2]
+    ffn_pieces = [(ref, w, o) for ref, (_, w, o) in zip(piece_refs[:3], names[:3])]
+    att_pieces = [(ref, w, o - shift) for ref, (_, w, o) in zip(piece_refs[3:], names[3:])]
+    ffn = Collect(sizes, (2 * act.shape[1], act.shape[1]), ffn_pieces, ffn_room, ffn_sems)
+    att = Collect(sizes, (qkv_cols, query_cols), att_pieces, att_room, att_sems)
+    sums = [
+        Reduce(line, pair, part, near, landed, *reduce_sems, (chunk,)) for chunk in range(chunks)
+    ]
+    gain_sum = GainSum(sizes, ffn.rows, gain_sum_ref, gain_room, gain_sems)
+
+    def left_loads(turn):
+        tick, slot = turn % line, turn % 2
+        one, sources = (ffn, (entry_two, cot_ref)) if turn < line else (att, (entry_one, branch_ref))
+        return [
+            pltpu.make_async_copy(
+                source.at[:, one.lanes(tick, dp)], left_slots.at[slot, item, dp], left_sem.at[slot, item, dp]
+            )
+            for item, source in enumerate(sources)
+            for dp in range(sizes["dp"])
+        ]
+
+    def branch_load(index):
+        size = branch_slots.shape[1]
+        return pltpu.make_async_copy(
+            branch_ref.at[pl.ds(index * size, size)], branch_slots.at[index % 2], branch_sem.at[index % 2]
+        )
+
+    for load in left_loads(0):
+        load.start()
+    for load in loads.values():
+        load.start()
+    for load in left_loads(1):
+        load.start()
+    greet_all(sizes)
+
+    def multiply(turn):
+        for load in left_loads(turn):
+            load.wait()
+        lefts = [left_slots.at[turn % 2, item] for item in range(2)]
+        if turn < line:
+            ffn.multiply(turn, lefts, (part_rows, act))
+        else:
+            att.multiply(turn - line, lefts, (dqkv, heads))
+        if turn + 2 < 2 * line:
+            for load in left_loads(turn + 2):
+                load.start()
+
+    class PartRows:
+        def __getitem__(self, at):
+            return part[:, :, :, :, at[1]].reshape(tokens, -1)
+
+    part_rows = PartRows()
+
+    def back_to_heads():
+        loads["low"].wait()
+        size = branch_slots.shape[1]
+        branch_load(0).start()
+        for index in range(tokens // size):
+            if index + 1 < tokens // size:
+                branch_load(index + 1).start()
+            branch_load(index).wait()
+            grad_heads[index * size : (index + 1) * size, :] = dot(
+                branch_slots[index % 2], low_w[:, qkv_cols:]
+            ).astype(BF)
+
+    def attention_part(sequence, low, size, lane):
+        start = sequence * total_rows
+        span = slice(start, start + total_rows)
+        at = slice(start + low, start + low + size)
+        both = qkv_ref[span, query_cols:]
+        keys, values = both_halves(both, 0), both_halves(both, 1)
+        visible = pos_row[...] <= pos_col[low : low + size, :]
+        queries = qkv_ref[at, lane : lane + 2 * HD]
+        grads = grad_heads[at, lane : lane + 2 * HD]
+        grad_queries = []
+        key_term = value_term = None
+        for head in range(2):
+            query, grad = only_head(queries, head), only_head(grads, head)
+            probability = softmax_rows(query, keys, visible)
+            grad_prob = contract_cols(grad, values)
+            delta = jnp.sum(probability * grad_prob, -1, keepdims=True)
+            grad_scores = jnp.where(visible, probability * (grad_prob - delta), 0.0).astype(BF)
+            grad_queries.append(dot(grad_scores, keys))
+            key_more = contract_rows(grad_scores, query)
+            value_more = contract_rows(probability.astype(BF), grad)
+            key_term = key_more if key_term is None else key_term + key_more
+            value_term = value_more if value_term is None else value_term + value_more
+        scale = HD ** (-0.5)
+        grad_proj[low : low + size, lane : lane + 2 * HD] = scale * jnp.where(
+            lane_index(grad_queries[0].shape) < HD, grad_queries[0], grad_queries[1]
+        )
+        if low == 0 and lane == 0:
+            key_acc[...] = key_term * scale
+            value_acc[...] = value_term
+        else:
+            key_acc[...] += key_term * scale
+            value_acc[...] += value_term
+
+    def rotate_back(sequence):
+        keys, values = key_acc[...], value_acc[...]
+        grad_proj[:, query_cols:] = jnp.where(
+            lane_index(keys.shape) < HD, keys + pltpu.roll(keys, HD, 1), values + pltpu.roll(values, HD, 1)
+        )
+        for low in range(0, total_rows, 256):
+            size = min(256, total_rows - low)
+            grads = grad_proj[low : low + size, :]
+            back = grads * cos_ref[low : low + size, :] + turned(grads * sin_ref[low : low + size, :])
+            at = sequence * total_rows + low
+            dqkv[at : at + size, :] = back.astype(BF)
+
+    def entry_terms(chunk):
+        mine = jnp.concatenate(
+            [
+                dqkv[(c * line + z) * block_rows + chunk * rows : (c * line + z) * block_rows + (chunk + 1) * rows, :]
+                for c in range(pair)
+                for z in range(line)
+            ],
+            0,
+        )
+        for low in range(0, width, 512):
+            term = contract_cols(mine, low_w[low : low + 512, :qkv_cols]).astype(BF)
+            part[chunk, :, :, :, low : low + 512] = term.reshape(pair, line, rows, 512)
+
+    def norm_rows_back(chunk):
+        at = slice(chunk * rows, (chunk + 1) * rows)
+        values = hidden_ref[at, :].astype(F32)
+        inverse = lax.rsqrt(jnp.mean(values * values, -1, keepdims=True) + EPS_NORM)
+        normed = values * inverse
+        grad_entry = total[...]
+        gain_term = jnp.sum(grad_entry * normed, 0, keepdims=True)
+        if chunk == 0:
+            gain_grad_ref[...] = gain_term
+        else:
+            gain_grad_ref[...] += gain_term
+        grad_normed = grad_entry * gain_ref[...]
+        grad_rows = inverse * (
+            grad_normed - normed * jnp.mean(grad_normed * normed, -1, keepdims=True)
+        )
+        grad_hidden_ref[at, :] = (grad_mid_ref[at, :] + grad_rows).astype(BF)
+
+    steps = []
+
+    def step(time, function, *values):
+        steps.append((time, functools.partial(function, *values)))
+
+    step(0.0, loads["dgu"].wait)
+    step(0.0, loads["act"].wait)
+    period, before = 26.0, 24.0
+    for tick in range(line):
+        arrived = before + period * tick
+        issued = 5.0 * (tick + 1) if tick < 2 else before + period * (tick - 2) + 0.5
+        step(issued - 5.0 if tick < 2 else issued - 5.5, multiply, tick)
+        step(issued, ffn.send_one, tick)
+        step(arrived, ffn.sum_one, tick)
+        step(arrived + 12.0, ffn.sum_two, tick)
+    now = 10.5
+    step(now, back_to_heads)
+    now += 3.0
+    for sequence in range(tokens // total_rows):
+        size = query_rows(total_rows)
+        for low in range(0, total_rows, size):
+            for lane in range(0, query_cols, 2 * HD):
+                step(now, attention_part, sequence, low, size, lane)
+                now += 6.0
+        step(now, rotate_back, sequence)
+        now += 0.5
+    now = max(now, before + period * (line - 3) + 0.6)
+    step(now, loads["heads"].wait)
+    for chunk in range(chunks):
+        step(now + 0.5 + chunk, entry_terms, chunk)
+    begin = now + 1.0
+    for chunk, one in enumerate(sums):
+        start = begin + chunk * (line - 1) * SEND
+        more, finish = one.plan(start, total, functools.partial(norm_rows_back, chunk))
+        steps += more
+    step(finish + 0.2, gain_sum.begin, gain_grad_ref, gain_two_ref)
+    step(finish + 4.0, gain_sum.second)
+    step(finish + 8.0, gain_sum.third)
+    step(finish + 12.0, gain_sum.end)
+    now += 1.0 + chunks
+    for tick in range(line):
+        step(now + tick, multiply, line + tick)
+        step(now + tick + 0.5, att.send_one, tick)
+        arrived = max(now + 30.0 + 2.0 * tick, before + period * (line - 2) + 1.0 + 2.0 * tick)
+        step(arrived, att.sum_one, tick)
+        step(arrived + 12.5, att.sum_two, tick)
+    run_steps(steps)
+    for one in sums + [ffn, att]:
+        one.drain()
+
+
+def closing(sizes, collective_id, factors, low, hidden, grad_mid, gain, grad_gain_two, tables):
+    line, pair = sizes["ctx"], sizes["core"]
+    group = line * pair
+    block_rows, width = hidden.shape
+    tokens = block_rows * group
+    chunks = 4
+    rows = block_rows // chunks
+    own_rows = width // (group * sizes["dp"] * sizes["x"])
+    units = factors[3].shape[1]
+    qkv_cols, query_cols = factors[6].shape[1], factors[7].shape[1]
+    total_rows = tables[0].shape[0]
+    pieces = grad_pieces(sizes)
+    any_spec = pl.BlockSpec(memory_space=pl.ANY)
+    vmem = pl.BlockSpec(memory_space=pltpu.VMEM)
+    dma = pltpu.SemaphoreType.DMA
+    shape = jax.ShapeDtypeStruct
+    across = sizes["x"] * pair * own_rows
+    branch_rows = 128
+    part_shape = (chunks, pair, line, rows, width)
+    factors = list(factors)
+    factors[1] = factors[1].reshape(part_shape)
+    return pl.pallas_call(
+        functools.partial(closing_kernel, sizes, chunks),
+        out_shape=[shape((own_rows, group * w), BF) for _, w, _ in pieces]
+        + [shape((block_rows, width), BF), shape((8, 128), F32)],
+        in_specs=[any_spec] * 6 + [vmem] + [any_spec] * 2 + [vmem] * 8,
+        out_specs=[any_spec] * len(pieces) + [vmem] * 2,
+        scratch_shapes=[
+            pltpu.VMEM((2, 2, sizes["dp"], tokens, across), BF),
+            pltpu.VMEM(part_shape, BF),
+            pltpu.VMEM((tokens, units), BF),
+            pltpu.VMEM((tokens, qkv_cols), BF),
+            pltpu.VMEM((tokens, query_cols), BF),
+            pltpu.VMEM((2, branch_rows, width), BF),
+            pltpu.VMEM((width, qkv_cols + query_cols), BF),
+            pltpu.VMEM((tokens, query_cols), BF),
+            pltpu.VMEM((total_rows, qkv_cols), F32),
+            pltpu.VMEM((total_rows, 2 * HD), F32),
+            pltpu.VMEM((total_rows, 2 * HD), F32),
+            *Reduce.room(line, pair, rows, width, chunks)[1:],
+            pltpu.VMEM((rows, width), F32),
+            dma((4,)),
+            dma((2, 2, sizes["dp"])),
+            dma((2,)),
+            *Collect.room(sizes, own_rows, 3 * units),
+            *Collect.room(sizes, own_rows, qkv_cols + query_cols),
+            *Collect.sems(sizes, 3),
+            *Collect.sems(sizes, 3),
+            *Reduce.sems(chunks)(line),
+            pltpu.VMEM((1, width), F32),
+            *GainSum.room(sizes, width),
+            *GainSum.sems(sizes),
+        ],
+        compiler_params=pltpu.CompilerParams(
+            collective_id=collective_id, has_side_effects=True, vmem_limit_bytes=63 * 2**20
+        ),
+    )(*factors, low, hidden, grad_mid, gain, grad_gain_two, *tables)
 
 
 def grad_pieces(sizes):
@@ -975,41 +1388,6 @@
         pieces.append((name, width, offset))
         offset += width
     return pieces
-
-
-def collect_grads(sizes, collective_id, *factors):
-    line, pair = sizes["ctx"], sizes["core"]
-    group = line * pair
-    rows = factors[0].shape[1] // (group * sizes["dp"] * sizes["x"])
-    widths = [right.shape[1] for right in factors[1::2]]
-    total = sum(widths)
-    pieces = grad_pieces(sizes)
-    steps = max(sizes["dp"], sizes["x"])
-    any_spec = pl.BlockSpec(memory_space=pl.ANY)
-    dma = pltpu.SemaphoreType.DMA
-    return pl.pallas_call(
-        functools.partial(collect_kernel, sizes, widths),
-        out_shape=[jax.ShapeDtypeStruct((rows, group * width), BF) for _, width, _ in pieces],
-        in_specs=[any_spec] * len(factors),
-        out_specs=[any_spec] * len(pieces),
-        scratch_shapes=[
-            *[pltpu.VMEM(factor.shape, factor.dtype) for factor in factors],
-            pltpu.VMEM((line, sizes["dp"], sizes["x"], pair, rows, total), BF),
-            pltpu.VMEM((group, sizes["dp"] * sizes["x"] - min(sizes["dp"], sizes["x"]), rows, total), BF),
-            pltpu.VMEM((group, steps - 1, rows, total), BF),
-            dma((len(factors),)),
-            dma((len(pieces),)),
-            dma((group, steps, steps)),
-            dma((group, steps, steps)),
-            dma((group, steps)),
-            dma((group, steps)),
-            dma((group, len(pieces))),
-            dma((group, len(pieces))),
-        ],
-        compiler_params=pltpu.CompilerParams(
-            collective_id=collective_id, has_side_effects=True, vmem_limit_bytes=62 * 2**20
-        ),
-    )(*factors)
 
 
 def adamw_kernel(step_rate, decay_rate, grad_ref, weight_ref, state_ref, grad_out, weight_out, state_out):
@@ -1036,23 +1414,6 @@
         in_specs=[flat, flat, deep],
         out_specs=[flat, flat, deep],
     )(gradient, weight, states)
-
-
-def turned(values):
-    half_dim = values.shape[-1] // 2
-    return jnp.concatenate([-values[..., half_dim:], values[..., :half_dim]], -1)
-
-
-def turned_back(values):
-    half_dim = values.shape[-1] // 2
-    return jnp.concatenate([values[..., half_dim:], -values[..., :half_dim]], -1)
-
-
-def norm_back(grad_entry, normed, inverse, gain):
-    grad_gain = jnp.sum(grad_entry * normed, 0)
-    grad_normed = grad_entry * gain
-    grad_rows = inverse * (grad_normed - normed * jnp.mean(grad_normed * normed, -1, keepdims=True))
-    return (grad_rows, grad_gain)
 
 
 def dot(left, right):
@@ -1082,91 +1443,35 @@
     total_rows = block_rows * line
     span_rows = total_rows // span_order.shape[0]
     heads, kv_heads = H // group, KV // group
-    ratio = heads // kv_heads
-    query_cols, kv_cols, unit_cols = heads * HD, kv_heads * HD, FF // group
-    scale = HD ** (-0.5)
+    query_cols, kv_cols = heads * HD, kv_heads * HD
     key_pos = (
         span_order[:, None] * span_rows + jnp.arange(span_rows, dtype=jnp.int32)[None, :]
     ).reshape(-1)
-    visible = key_pos[None, :] <= key_pos[:, None]
     cos_tab, sin_tab = rope_table(key_pos)
-    cos_tab, sin_tab = cos_tab[None, :, None, :], sin_tab[None, :, None, :]
-
-    qkv_width = query_cols + 2 * kv_cols
+    signs = jnp.where(jnp.arange(HD) < HD // 2, -1.0, 1.0)
+    cosines = jnp.concatenate([cos_tab] * (heads + kv_heads) + [jnp.ones_like(cos_tab)] * kv_heads, 1)
+    sines = jnp.concatenate(
+        [sin_tab * signs] * (heads + kv_heads) + [jnp.zeros_like(sin_tab)] * kv_heads, 1
+    )
+    tables = (cosines, sines, key_pos[:, None], key_pos[None, :])
     low, high, hidden_all = spread_weights(
         sizes, 0, hidden[0], norm_gains, w_qkv, w_out, w_gate_up, w_down
     )
-    qkv_c = low[:, :qkv_width]
-    out_c = low[:, qkv_width : qkv_width + query_cols]
-    gains = low[:, qkv_width + query_cols :].astype(F32)[:, :2].T
-    gain_one, gain_two = gains[0], gains[1]
-
-    def normed(rows):
-        inverse = lax.rsqrt(jnp.mean(rows * rows, -1, keepdims=True) + EPS_NORM)
-        return rows * inverse, inverse
-
-    row_in = hidden[0].astype(F32)
-    normed_one, inv_one = normed(row_in)
-    entry_one = (normed(hidden_all.astype(F32))[0] * gain_one).astype(BF)
-
-    projected = dot(entry_one, qkv_c).reshape(pair, total_rows, qkv_width)
-    queries = projected[..., :query_cols].reshape(pair, total_rows, heads, HD)
-    key_rows = projected[..., query_cols : query_cols + kv_cols].reshape(
-        pair, total_rows, kv_heads, HD
+    gains = low[:, 2 * query_cols + 2 * kv_cols :].astype(F32)[:, :2].T
+    gain_one, gain_two = gains[:1], gains[1:]
+    entry_one, qkv, attended = attend(hidden_all, low, gain_one, tables)
+    output, grad_middle, grad_gain_two, grad_branch, entry_two, cot, activated, grad_gu = middle_rows(
+        sizes, 1, attended, low, high, hidden[0], cotangent[0], gain_two
     )
-    value_rows = projected[..., query_cols + kv_cols :].reshape(pair, total_rows, kv_heads, HD)
-    queries = (queries * cos_tab + turned(queries) * sin_tab).astype(BF)
-    key_rows = (key_rows * cos_tab + turned(key_rows) * sin_tab).astype(BF)
-    value_rows = value_rows.astype(BF)
-    queries = queries.reshape(pair, total_rows, kv_heads, ratio, HD)
-
-    def product(spec, left, right):
-        return jnp.einsum(spec, left, right, preferred_element_type=F32)
-
-    scores = product("stkgd,sukd->skgtu", queries, key_rows) * scale
-    scores = jnp.where(visible, scores, NEG_FILL)
-    top_score = jnp.max(scores, -1, keepdims=True)
-    exponent = jnp.exp(scores - top_score)
-    probability = exponent / jnp.sum(exponent, -1, keepdims=True)
-    prob_low = probability.astype(BF)
-    attended = product("skgtu,sukd->stkgd", prob_low, value_rows).astype(BF)
-    attended = attended.reshape(pair * total_rows, query_cols)
-
-    output, grad_middle, grad_gain_two, grad_branch, entry_two, cot, activated, grad_gu = middle_rows(
-        sizes, 1, attended, low, high, hidden[0], cotangent[0], gain_two[None]
+    factors = (entry_two, grad_gu, cot, activated, entry_one, grad_branch, qkv, attended)
+    *pieces, grad_hidden, gain_sums = closing(
+        sizes, 2, factors, low, hidden[0], grad_middle, gain_one, grad_gain_two, tables
     )
-    output = output[None]
-
-    grad_attended = dot(grad_branch, out_c).astype(BF)
-    grad_heads = grad_attended.reshape(pair, total_rows, kv_heads, ratio, HD)
-    grad_prob = product("stkgd,sukd->skgtu", grad_heads, value_rows)
-    delta_row = jnp.sum(probability * grad_prob, -1, keepdims=True)
-    grad_scores = jnp.where(visible, probability * (grad_prob - delta_row), 0.0).astype(BF)
-    grad_queries = product("skgtu,sukd->stkgd", grad_scores, key_rows) * scale
-    grad_keys = product("skgtu,stkgd->sukd", grad_scores, queries) * scale
-    grad_values = product("skgtu,stkgd->sukd", prob_low, grad_heads)
-    grad_queries = grad_queries.reshape(pair, total_rows, heads, HD)
-    grad_queries = grad_queries * cos_tab + turned_back(grad_queries * sin_tab)
-    grad_keys = grad_keys * cos_tab + turned_back(grad_keys * sin_tab)
-    grad_projected = jnp.concatenate(
-        [
-            grad_queries.reshape(-1, query_cols),
-            grad_keys.reshape(-1, kv_cols),
-            grad_values.reshape(-1, kv_cols),
-        ],
-        1,
-    ).astype(BF)
-    grad_entry_one = scatter_tokens(sizes, 2, contract_cols(grad_projected, qkv_c).astype(BF))
-    grad_row_norm, grad_gain_one = norm_back(grad_entry_one, normed_one, inv_one, gain_one)
-    grad_hidden = (grad_middle + grad_row_norm).astype(BF)[None]
-
-    grad_gate, grad_up, grad_down, grad_query, grad_key_value, grad_out = collect_grads(
-        sizes, 3, entry_two, grad_gu, cot, activated, entry_one, grad_projected, grad_branch, attended
-    )
-    grad_gains = lax.psum_scatter(
-        jnp.stack([grad_gain_one, grad_gain_two[0]]), everyone, scatter_dimension=1, tiled=True
-    )
+    grad_gate, grad_up, grad_down, grad_query, grad_key_value, grad_out = pieces
+    output, grad_hidden = output[None], grad_hidden[None]
     rows = w_qkv.shape[0]
+    place = lax.axis_index(everyone) * rows
+    grad_gains = lax.dynamic_slice(gain_sums, (0, lax.rem(place, 128)), (2, rows))
     grad_key_value = grad_key_value.reshape(rows, group, 2, kv_cols).transpose(0, 2, 1, 3)
     grad_qkv = jnp.concatenate([grad_query, grad_key_value.reshape(rows, -1)], 1)
     grad_gate_up = jnp.concatenate([grad_gate, grad_up], 1)

time: 708 us -> 614 us (0.87)
  matrix products: 29.4 us -> 0 us
  other arithmetic: 30.2 us -> 8.75 us
  local copies, waits for them, and re-layouts: 40.4 us -> 20.4 us
  between operations: 14.7 us -> 1.26 us
  Pallas kernels: 584 us -> 574 us
    dot_general x9 -> x0, matrix products: 29.4 us -> none  [the longest x6 21.4 us: product(): return jnp.einsum(spec, left, right, preferred_element_type=F32)]
    pallas_call x2, Pallas kernels: 201 us -> 190 us  [the longest x1 176 us: closing(): pl.pallas_call(functools.partial(closing_kernel, sizes, chunks), out_shap...]
    reshape x5 -> x0, local copies, waits for them, and re-layouts: 9.2 us -> none  [the longest x2 5.94 us: shards(): grad_queries = grad_queries.reshape(pair, total_rows, heads, HD)]
    convert_element_type x5 -> x0, other arithmetic: 7.71 us -> none  [the longest x2 6.25 us: shards(): entry_one = (normed(hidden_all.astype(F32))[0] * gain_one).astype(BF)]
    unnamed x63 -> x32, local copies, waits for them, and re-layouts: 17.3 us -> 11.1 us
  transfers between devices with their start and end apart: 1 -> 0, of which waited for: 0 -> 0; matrix products, arithmetic and copies ran while one was open for 2% -> 0% of each run, Pallas kernels for 28% -> 0%
where the time goes in v4:
time: 614 us; the launch traced here: 604 us
  Pallas kernels  574 us (93%)
  local copies, waits for them, and re-layouts  20.4 us (3%)
  other arithmetic  8.75 us (1%)
    pallas_call x1, Pallas kernels, middle_rows(): pl.pallas_call(functools.partial(middle_kernel, line, pair, chunks), out_...  200 us
    pallas_call x1, Pallas kernels, closing(): pl.pallas_call(functools.partial(closing_kernel, sizes, chunks), out_shap...  176 us
    pallas_call x1, Pallas kernels, spread_weights(): pl.pallas_call(functools.partial(spread_kernel, sizes), out_shape=[jax.Sh...  150 us
    pallas_call x4, Pallas kernels, adamw_columns(): pl.pallas_call(functools.partial(adamw_kernel, step_rate, decay_rate), gr...  34.1 us
    pallas_call x1, Pallas kernels, attend(): pl.pallas_call(attend_kernel, out_shape=[jax.ShapeDtypeStruct((tokens, wi...  14 us

profile of v4, /device:TPU:0, one launch (start us, length us, event | category | flops | bytes accessed | tf_op | source)
XLA Modules:
  0.0 604.4 jit_solution(18280469544598907712)
XLA Ops:
  0.7 0.8 copy.36
  1.4 1.6 copy-done.1
  3.0 1.0 copy-done.2
  4.1 1.1 copy-done.4
  5.2 1.0 copy-done.5
  6.2 149.8 %shard_map.260 = (bf16[2,4,2,2,64,768]{5,4,3,2,1,0:T(8,128)(2,1)S(1)}, bf16[2,4,2,2,64,3072]{5,4,3,2,1,0:T(8,128)(2,1)}, bf16[2,4,128,2048]{3,2,1,0:T(8,128)(2,1)S(1)}) custom-call(f32[64,3072]{1,0:T(8,128)S(1)} %copy-done.4, f32[64,2048]{1,0:T(8,128)S(1)} %copy-done.5, f32[64,16384]{1,0:T(8,128)} %weight_ref.6, f32[64,8192]{1,0:T(8,128)S(1)} %copy-done.1, ...), custom_call_target="tpu_custom_call" | custom-call | tf_op jit(solution)/shard_map/pallas_call | solution.py:724
  156.1 2.0 copy-done.3
  158.1 1.1 slice_convert_fusion
  159.2 1.9 copy.42
  161.1 0.6 fusion.5
  161.9 1.0 multiply_sine_fusion
  162.9 0.8 maximum_multiply_fusion
  163.7 0.7 broadcast_in_dim.28
  164.5 2.9 concatenate.19.sin_ref.refs_14_
  167.3 0.7 broadcast_in_dim.25
  168.0 2.4 concatenate.17.cos_ref.refs_13_
  170.4 0.9 add.94.pos_col.refs_15_
  171.4 0.7 add.84.pos_row.refs_16_
  172.0 14.0 %shard_map.261 = (bf16[1024,2048]{1,0:T(8,128)(2,1)}, bf16[1024,384]{1,0:T(8,128)(2,1)}, bf16[1024,256]{1,0:T(8,128)(2,1)}) custom-call(bf16[1024,2048]{1,0:T(8,128)(2,1)} %bitcast.43, bf16[2048,768]{1,0:T(8,128)(2,1)} %bitcast.37, f32[1,2048]{1,0:T(1,128)} %get-tuple-element.88.gain_ref.refs_11_, f32[512,384]{1,0:T(8,128)} %concatenate.17.cos_ref.refs_13_, ...), custom_call_target="tpu_custom_call" | custom-call | tf_op jit(solution)/shard_map/pallas_call | solution.py:1016
  186.0 199.9 %shard_map.262 = (bf16[128,2048]{1,0:T(8,128)(2,1)}, f32[128,2048]{1,0:T(8,128)}, f32[1,2048]{1,0:T(1,128)}, bf16[2,4,128,2048]{3,2,1,0:T(8,128)(2,1)}, bf16[4,2...) custom-call(bf16[2,4,128,256]{3,2,1,0:T(8,128)(2,1)} %bitcast.49, ...), custom_call_target="tpu_custom_call" | custom-call | tf_op jit(solution)/shard_map/pallas_call | solution.py:500
  386.0 176.1 %shard_map.263 = (bf16[64,8192]{1,0:T(8,128)(2,1)}, bf16[64,8192]{1,0:T(8,128)(2,1)}, bf16[64,8192]{1,0:T(8,128)(2,1)}, bf16[64,2048]{1,0:T(8,128)(2,1)}, bf16[6...) custom-call(bf16[1024,2048]{1,0:T(8,128)(2,1)} %bitcast.46, ...), custom_call_target="tpu_custom_call" | custom-call | tf_op jit(solution)/shard_map/pallas_call | solution.py:1338
  562.1 0.8 fusion.3
  562.8 0.6 fusion.4
  563.4 0.6 pad_maximum_fusion.2
  564.0 3.0 pad_maximum_fusion.grad_ref
  567.0 17.7 %shard_map.266 = (f32[64,16384]{1,0:T(8,128)}, f32[64,16384]{1,0:T(8,128)}, f32[2,64,16384]{2,1,0:T(8,128)}) custom-call(bf16[64,16384]{1,0:T(8,128)(2,1)} %pad_maximum_fusion.grad_ref, f32[64,16384]{1,0:T(8,128)} %weight_ref.6, f32[2,64,16384]{2,1,0:T(8,128)} %state_ref.6), custom_call_target="tpu_custom_call" | custom-call | tf_op jit(solution)/shard_map/pallas_call | solution.py:1406
  584.7 9.2 %shard_map.267 = (f32[64,8192]{1,0:T(8,128)}, f32[64,8192]{1,0:T(8,128)}, f32[2,64,8192]{2,1,0:T(8,128)}) custom-call(bf16[64,8192]{1,0:T(8,128)(2,1)} %get-tuple-element.75.grad_ref, f32[64,8192]{1,0:T(8,128)} %weight_ref.7, f32[2,64,8192]{2,1,0:T(8,128)} %state_ref.7), custom_call_target="tpu_custom_call" | custom-call | tf_op jit(solution)/shard_map/pallas_call | solution.py:1406
  594.4 0.8 pad_maximum_fusion.1.grad_ref
  595.1 4.5 shard_map.264
  599.6 2.7 shard_map.265
  602.3 0.8 copy.47
  603.1 0.8 copy.48
  (32 shorter events, 0.7 us)
Async XLA Ops:
  1.4 1.6 copy-start.1
  3.0 1.0 copy-start.2
  4.1 1.1 copy-start.4
  5.2 1.0 copy-start.5
  6.2 155.5 %copy-start.13 = (s32[8]{0:T(128)S(1)}, s32[8]{0:T(128)}, u32[]{:S(2)}) copy-start(s32[8]{0:T(128)} %param.15) | copy-start | bytes 100
  156.1 2.0 copy-start.3
  158.1 12.4 %copy-start = (bf16[2,4,2,2,64,768]{5,4,3,2,1,0:T(8,128)(2,1)}, bf16[2,4,2,2,64,768]{5,4,3,2,1,0:T(8,128)(2,1)S(1)}, u32[]{:S(2)}) copy-start(bf16[2,4,2,2,64,768]{5,4,3,2,1,0:T(8,128)(2,1)S(1)} %get-tuple-element.52) | copy-start | bytes 9437188
  385.9 176.1 %copy-start.10 = (f32[2,2,64]{2,1,0:T(2,128)S(1)}, f32[2,2,64]{2,1,0:T(2,128)}, u32[]{:S(2)}) copy-start(f32[2,2,64]{2,1,0:T(2,128)} %param.21) | copy-start | bytes 3076
  385.9 176.9 %copy-start.11 = (f32[2,64]{1,0:T(2,128)S(1)}, f32[2,64]{1,0:T(2,128)}, u32[]{:S(2)}) copy-start(f32[2,64]{1,0:T(2,128)} %param.16) | copy-start | bytes 1540
  562.8 21.8 %copy-start.12 = (f32[2,64]{1,0:T(2,128)}, f32[2,64]{1,0:T(2,128)S(1)}, u32[]{:S(2)}) copy-start(f32[2,64]{1,0:T(2,128)S(1)} %get-tuple-element.114) | copy-start | bytes 1540
  584.7 9.2 %copy-start.9 = (bf16[64,1024]{1,0:T(8,128)(2,1)S(1)}, bf16[64,1024]{1,0:T(8,128)(2,1)}, u32[]{:S(2)}) copy-start(bf16[64,1024]{1,0:T(8,128)(2,1)} %get-tuple-element.68) | copy-start | bytes 393220
  584.7 9.7 %copy-start.8 = (bf16[64,2048]{1,0:T(8,128)(2,1)S(1)}, bf16[64,2048]{1,0:T(8,128)(2,1)}, u32[]{:S(2)}) copy-start(bf16[64,2048]{1,0:T(8,128)(2,1)} %get-tuple-element.67) | copy-start | bytes 786436
  593.9 8.4 %copy-start.6 = (bf16[128,2048]{1,0:T(8,128)(2,1)S(1)}, bf16[128,2048]{1,0:T(8,128)(2,1)}, u32[]{:S(2)}) copy-start(bf16[128,2048]{1,0:T(8,128)(2,1)} %get-tuple-element.55) | copy-start | bytes 1572868
  593.9 9.2 %copy-start.7 = (bf16[128,2048]{1,0:T(8,128)(2,1)S(1)}, bf16[128,2048]{1,0:T(8,128)(2,1)}, u32[]{:S(2)}) copy-start(bf16[128,2048]{1,0:T(8,128)(2,1)} %get-tuple-element.65) | copy-start | bytes 1572868

commit v5 on v4

--- a/solution.py
+++ b/solution.py
@@ -241,8 +241,9 @@
             pltpu.VMEM(outer + (line + 1, rows, columns), BF),
         ]
 
-    def __init__(self, line, pair, part, near, landed, core_send, core_recv, line_send, line_recv, at):
+    def __init__(self, line, pair, part, near, landed, core_send, core_recv, line_send, line_recv, at, kind=None):
         self.line, self.pair, self.at = line, pair, at
+        self.sem_at = at if kind is None else (kind,) + at[1:]
         self.part, self.near, self.landed = part, near, landed
         self.core_sems, self.line_sems = (core_send, core_recv), (line_send, line_recv)
         self.here, self.core = lax.axis_index("ctx"), lax.axis_index("core")
@@ -255,8 +256,8 @@
         return remote(
             self.part.at[self.at + (1 - self.core,)],
             self.near.at[self.at],
-            self.core_sems[0].at[self.at],
-            self.core_sems[1].at[self.at],
+            self.core_sems[0].at[self.sem_at],
+            self.core_sems[1].at[self.sem_at],
             core=1 - self.core,
         )
 
@@ -264,7 +265,7 @@
         return self.landed.at[self.at + (block + 1 if way == 0 else block,)]
 
     def onward(self, way, block, here):
-        index = self.at + (way, block)
+        index = self.sem_at + (way, block)
         return remote(
             self.mine(block),
             self.slot(way, block),
@@ -341,195 +342,6 @@
         step()
 
 
-def middle_kernel(line, pair, chunks, *refs):
-    heads_ref, low_ref, high_ref, hidden_ref, cot_ref, gain_ref = refs[:6]
-    output_ref, grad_mid_ref, gain_grad_ref, branch_ref, entry_ref, cots_ref, act_ref, dgu_ref = refs[6:14]
-    out_w, ffn_w, part, near, landed, total, middle, branch, load_sem = refs[14:23]
-    reduce_sems, travel_sems = refs[23:27], refs[27:]
-    width = hidden_ref.shape[1]
-    rows = part.shape[-2]
-    tokens = pair * line * rows
-    query_cols = out_w.shape[1]
-    units = ffn_w.shape[1] // 3
-    core, here = lax.axis_index("core"), lax.axis_index("ctx")
-    first_col = low_ref.shape[1] - 128 - query_cols
-    loads = [
-        pltpu.make_async_copy(low_ref.at[:, pl.ds(first_col, query_cols)], out_w, load_sem.at[0]),
-        pltpu.make_async_copy(high_ref, ffn_w, load_sem.at[1]),
-    ]
-    for load in loads:
-        load.start()
-    greet_line(line, pair)
-    steps = []
-    sums, travels = [], []
-
-    def chunk_rows(chunk):
-        return slice(chunk * rows, (chunk + 1) * rows)
-
-    def reducer(kind, chunk):
-        one = Reduce(line, pair, part, near, landed, *reduce_sems, (kind, chunk))
-        sums.append(one)
-        return one
-
-    def traveller(kind, chunk, source, place, start):
-        one = Travel(line, pair, [source], [place], *[sem.at[kind, chunk] for sem in travel_sems])
-        travels.append(one)
-        steps.append((start, one.begin))
-        for step in range(line - 1):
-            steps.append((start + (step + 1) * HOP, functools.partial(one.step, step)))
-        finish = start + line * HOP - 1.0
-        steps.append((finish, one.end))
-        return finish
-
-    def product(chunk):
-        mine = heads_ref[:, :, chunk_rows(chunk), :].reshape(tokens, query_cols)
-
-        @pl.loop(0, width // 512)
-        def _(index):
-            at = pl.ds(pl.multiple_of(index * 512, 512), 512)
-            term = contract_cols(mine, out_w[at, :]).astype(BF)
-            part[0, chunk, :, :, :, at] = term.reshape(pair, line, rows, 512)
-
-    def norm_rows(chunk):
-        mid = hidden_ref[chunk_rows(chunk), :].astype(F32) + total[...]
-        middle[chunk_rows(chunk), :] = mid
-        inverse = lax.rsqrt(jnp.mean(mid * mid, -1, keepdims=True) + EPS_NORM)
-        entry_ref[chunk, core, here] = (mid * inverse * gain_ref[...]).astype(BF)
-
-    def units_part(chunk, index, count):
-        size = units // count
-        entry = entry_ref[chunk].reshape(tokens, width)
-        low, high = index * size, (index + 1) * size
-        gate = dot(entry, ffn_w[:, low:high])
-        up = dot(entry, ffn_w[:, units + low : units + high])
-        grad_act = dot(cots_ref[chunk].reshape(tokens, width), ffn_w[:, 2 * units + low : 2 * units + high])
-        sigmoid = 1.0 / (1.0 + jnp.exp(-gate))
-        silu = gate * sigmoid
-        act_ref[chunk, :, low:high] = (silu * up).astype(BF)
-        dgu_ref[chunk, :, low:high] = (grad_act * up * sigmoid * (1.0 + gate * (1.0 - sigmoid))).astype(BF)
-        dgu_ref[chunk, :, units + low : units + high] = (grad_act * silu).astype(BF)
-
-    def back_part(chunk, index, count):
-        size = width // count
-        at = slice(index * size, (index + 1) * size)
-        term = contract_cols(dgu_ref[chunk], ffn_w[at, : 2 * units]).astype(BF)
-        part[1, chunk, :, :, :, at] = term.reshape(pair, line, rows, size)
-
-    def down_part(chunk, index, count):
-        size = width // count
-        at = slice(index * size, (index + 1) * size)
-        term = contract_cols(act_ref[chunk], ffn_w[at, 2 * units :]).astype(BF)
-        part[2, chunk, :, :, :, at] = term.reshape(pair, line, rows, size)
-
-    def norm_rows_back(chunk):
-        mid = middle[chunk_rows(chunk), :]
-        inverse = lax.rsqrt(jnp.mean(mid * mid, -1, keepdims=True) + EPS_NORM)
-        normed = mid * inverse
-        grad_entry = total[...]
-        gain_term = jnp.sum(grad_entry * normed, 0, keepdims=True)
-        if chunk == 0:
-            gain_grad_ref[...] = gain_term
-        else:
-            gain_grad_ref[...] += gain_term
-        grad_normed = grad_entry * gain_ref[...]
-        grad_rows = inverse * (
-            grad_normed - normed * jnp.mean(grad_normed * normed, -1, keepdims=True)
-        )
-        grad_mid = cot_ref[chunk_rows(chunk), :].astype(F32) + grad_rows
-        grad_mid_ref[chunk_rows(chunk), :] = grad_mid
-        branch[chunk] = grad_mid.astype(BF)
-
-    def write_output(chunk):
-        output_ref[chunk_rows(chunk), :] = (middle[chunk_rows(chunk), :] + total[...]).astype(BF)
-
-    span = (line - 1) * SEND
-    ready_ffn = ready_back = 0.0
-    starts = []
-    steps.append((0.0, loads[0].wait))
-    for chunk in range(chunks):
-        cot_done = traveller(
-            0, chunk, cot_ref.at[chunk_rows(chunk)], lambda c, z, k=chunk: cots_ref.at[k, c, z], chunk * span
-        )
-        begin = 1.0 + chunk * span
-        steps.append((begin - 0.5, functools.partial(product, chunk)))
-        more, finish = reducer(0, chunk).plan(begin, total, functools.partial(norm_rows, chunk))
-        steps += more
-        arrived = traveller(1, chunk, None, lambda c, z, k=chunk: entry_ref.at[k, c, z], finish)
-        begin = max(arrived, cot_done, ready_ffn) + 0.1
-        if chunk == 0:
-            steps.append((begin, loads[1].wait))
-        count = 4
-        for index in range(count):
-            steps.append((begin + index, functools.partial(units_part, chunk, index, count)))
-        for index in range(count):
-            steps.append((begin + 4 + 0.8 * index, functools.partial(back_part, chunk, index, count)))
-        for index in range(count):
-            steps.append((begin + 7.3 + 0.5 * index, functools.partial(down_part, chunk, index, count)))
-        ready_ffn = begin + 9.5
-        begin = max(begin + 7.25, ready_back)
-        ready_back = begin + span
-        more, finish = reducer(1, chunk).plan(begin, total, functools.partial(norm_rows_back, chunk))
-        steps += more
-        traveller(
-            2,
-            chunk,
-            branch.at[chunk],
-            lambda c, z, k=chunk: branch_ref.at[c, z, pl.ds(k * rows, rows)],
-            finish,
-        )
-    for chunk in range(chunks):
-        begin = ready_back + chunk * span
-        steps += reducer(2, chunk).plan(begin, total, functools.partial(write_output, chunk))[0]
-    run_steps(steps)
-    for one in sums:
-        one.drain()
-
-
-def middle_rows(sizes, collective_id, heads, low, high, hidden, cot, gain):
-    line, pair = sizes["ctx"], sizes["core"]
-    rows, width = hidden.shape
-    chunks = 4
-    step = rows // chunks
-    tokens = pair * line * step
-    units = high.shape[1] // 3
-    query_cols = heads.shape[1]
-    any_spec = pl.BlockSpec(memory_space=pl.ANY)
-    vmem = pl.BlockSpec(memory_space=pltpu.VMEM)
-    shape = jax.ShapeDtypeStruct
-    dma = pltpu.SemaphoreType.DMA
-    outs = pl.pallas_call(
-        functools.partial(middle_kernel, line, pair, chunks),
-        out_shape=[
-            shape((rows, width), BF),
-            shape((rows, width), F32),
-            shape((1, width), F32),
-            shape((pair, line, rows, width), BF),
-            shape((chunks, pair, line, step, width), BF),
-            shape((chunks, pair, line, step, width), BF),
-            shape((chunks, tokens, units), BF),
-            shape((chunks, tokens, 2 * units), BF),
-        ],
-        in_specs=[vmem, any_spec, any_spec, vmem, vmem, vmem],
-        out_specs=[vmem, vmem, vmem, any_spec, vmem, vmem, vmem, vmem],
-        scratch_shapes=[
-            pltpu.VMEM((width, query_cols), BF),
-            pltpu.VMEM(high.shape, BF),
-            *Reduce.room(line, pair, step, width, 3, chunks),
-            pltpu.VMEM((step, width), F32),
-            pltpu.VMEM((rows, width), F32),
-            pltpu.VMEM((chunks, step, width), BF),
-            dma((2,)),
-            *Reduce.sems(3, chunks)(line),
-            dma((3, chunks, 1)),
-            *[dma((3, chunks, 1, 2, line))] * 4,
-        ],
-        compiler_params=pltpu.CompilerParams(
-            collective_id=collective_id, has_side_effects=True, vmem_limit_bytes=63 * 2**20
-        ),
-    )(heads.reshape(pair, line, rows, query_cols), low, high, hidden, cot, gain)
-    return list(outs[:3]) + [out.reshape(-1, out.shape[-1]) for out in outs[3:]]
-
-
 def blocks_in_order(line, pair):
     away = sorted(range(line), key=lambda d: min(d, line - d))
     return [(dz, dc) for dz in away for dc in range(pair)]
@@ -550,203 +362,116 @@
     greet(places)
 
 
-def pack_member(refs, member, rows, group, tall, wide):
-    qkv_ref, out_ref, gate_up_ref, down_ref, gain_ref = refs
-    heads, keys, units = H * HD // group, KV * HD // group, FF // group
-    low = lambda values: values.astype(BF)
-    tall[member, :, :heads] = low(qkv_ref[:, member * heads : (member + 1) * heads])
-    key_at, value_at = H * HD + member * keys, (H + KV) * HD + member * keys
-    tall[member, :, heads : heads + 2 * keys] = low(
-        jnp.concatenate(
-            [qkv_ref[:, key_at : key_at + keys], qkv_ref[:, value_at : value_at + keys]], 1
-        )
-    )
-    tall[member, :, heads + 2 * keys : 2 * heads + 2 * keys] = low(
-        out_ref[:, member * heads : (member + 1) * heads]
-    )
-    tall[member, :, 2 * heads + 2 * keys :] = low(gain_ref[...])
-    wide[member, :, :units] = low(gate_up_ref[:, member * units : (member + 1) * units])
-    wide[member, :, units : 2 * units] = low(
-        gate_up_ref[:, FF + member * units : FF + (member + 1) * units]
-    )
-    wide[member, :, 2 * units :] = low(down_ref[:, member * units : (member + 1) * units])
-
-
-def spread_kernel(sizes, *refs):
-    weight_refs, hidden_ref = refs[:5], refs[5]
-    outs, hidden_out = refs[6:8], refs[8]
-    packs = refs[9:11]
-    own_sem, f_send, f_recv, a_send, a_recv, b_send, b_recv = refs[11:18]
-    travel_sems = refs[18:]
-    line, pair = sizes["ctx"], sizes["core"]
-    group = line * pair
-    rows = packs[0].shape[1]
-    at = {name: lax.axis_index(name) for name in ("dp", "ctx", "x", "core")}
-    greet_all(sizes)
-    order = blocks_in_order(line, pair)
-    me = at["ctx"] * pair + at["core"]
-    travel = Travel(line, pair, [hidden_ref], [lambda c, z: hidden_out.at[c, z]], *travel_sems)
-    travel.begin()
-
-    def first(kind, index):
-        dz, dc = order[index]
-        z, c = wrap(at["ctx"] + dz, line), wrap(at["core"] + dc, pair)
-        return remote(
-            packs[kind].at[z * pair + c],
-            outs[kind].at[at["dp"], at["ctx"], at["x"], at["core"]],
-            f_send.at[kind, index],
-            f_recv.at[kind, index],
-            ctx=z,
-            core=c,
-        )
-
-    def place(kind, index, moved):
-        dz, dc = order[index]
-        z, c = wrap(at["ctx"] - dz, line), wrap(at["core"] - dc, pair)
-        spot = {name: wrap(at[name] - moved.get(name, 0), sizes[name]) for name in ("dp", "x")}
-        return outs[kind].at[spot["dp"], z, spot["x"], c]
-
-    def came(kind, index):
-        spot = place(kind, index, {})
-        return remote(spot, spot, f_send.at[kind, index], f_recv.at[kind, index], core=at["core"])
-
-    def axes(index):
-        dz, dc = order[index]
-        return ("x", "dp") if (dz + dc) % 2 == 0 else ("dp", "x")
-
-    def hop_one(kind, index, step):
-        name = axes(index)[0]
-        spot = place(kind, index, {})
-        return remote(
-            spot,
-            spot,
-            a_send.at[kind, index, step],
-            a_recv.at[kind, index, step],
-            **{name: wrap(at[name] + step, sizes[name])},
-        )
-
-    def one_came(kind, index, step):
-        name = axes(index)[0]
-        spot = place(kind, index, {name: step})
-        return remote(
-            spot, spot, a_send.at[kind, index, step], a_recv.at[kind, index, step], core=at["core"]
-        )
-
-    def hop_two(kind, index, step, far):
-        name, other = axes(index)
-        spot = place(kind, index, {name: step})
-        return remote(
-            spot,
-            spot,
-            b_send.at[kind, index, step, far],
-            b_recv.at[kind, index, step, far],
-            **{other: wrap(at[other] + far, sizes[other])},
-        )
-
-    def two_came(kind, index, step, far):
-        name, other = axes(index)
-        spot = place(kind, index, {name: step, other: far})
-        return remote(
-            spot,
-            spot,
-            b_send.at[kind, index, step, far],
-            b_recv.at[kind, index, step, far],
-            core=at["core"],
-        )
-
-    def own(kind):
-        return pltpu.make_async_copy(
-            packs[kind].at[me],
-            outs[kind].at[at["dp"], at["ctx"], at["x"], at["core"]],
-            own_sem.at[kind],
-        )
-
-    def onward(kind, index):
-        name, other = axes(index)
-        for step in range(1, sizes[name]):
-            hop_one(kind, index, step).start()
-        for far in range(1, sizes[other]):
-            hop_two(kind, index, 0, far).start()
-
-    def onward_two(kind, index):
-        name, other = axes(index)
-        for step in range(1, sizes[name]):
-            one_came(kind, index, step).wait_recv()
-            for far in range(1, sizes[other]):
-                hop_two(kind, index, step, far).start()
-
-    for member in range(group):
-        pack_member(weight_refs, member, rows, group, *packs)
-    ahead, late = 3, 1
-    for kind in range(2):
-        own(kind).start()
-        for index in range(1, 1 + ahead):
-            first(kind, index).start()
-    for tick in range(group + late):
-        if tick < group:
-            for kind in range(2):
-                if tick == 0:
-                    own(kind).wait()
-                else:
-                    came(kind, tick).wait_recv()
-                onward(kind, tick)
-                if 1 + ahead <= tick + ahead < group and tick:
-                    first(kind, tick + ahead).start()
-        if tick % 2 == 1 and tick // 2 < line - 1:
-            travel.step(tick // 2)
-        if tick >= late:
-            for kind in range(2):
-                onward_two(kind, tick - late)
-    travel.end()
-    for kind in range(2):
-        for index in range(group):
+class Spread:
+    @staticmethod
+    def sems(sizes):
+        dma = pltpu.SemaphoreType.DMA
+        group, steps = sizes["ctx"] * sizes["core"], max(sizes["dp"], sizes["x"])
+        return [dma((1,))] + [dma((group,))] * 2 + [dma((group, steps))] * 2 + [dma((group, steps, steps))] * 2
+
+    def __init__(self, sizes, pack, out, sems):
+        self.sizes, self.pack, self.out = sizes, pack, out
+        self.own_sem, *rest = sems
+        self.f_sems, self.a_sems, self.b_sems = rest[0:2], rest[2:4], rest[4:6]
+        self.line, self.pair = sizes["ctx"], sizes["core"]
+        self.at = {name: lax.axis_index(name) for name in ("dp", "ctx", "x", "core")}
+        self.order = blocks_in_order(self.line, self.pair)
+
+    def spot(self, dp, z, x, c):
+        return self.out.at[dp * self.line + z, x * self.pair + c]
+
+    def mine(self):
+        return self.spot(*[self.at[name] for name in ("dp", "ctx", "x", "core")])
+
+    def copy(self, sems, at, source, target, **where):
+        return remote(source, target, *[sem.at[at] for sem in sems], **where)
+
+    def first(self, index):
+        dz, dc = self.order[index]
+        z, c = wrap(self.at["ctx"] + dz, self.line), wrap(self.at["core"] + dc, self.pair)
+        return self.copy(self.f_sems, index, self.pack.at[z * self.pair + c], self.mine(), ctx=z, core=c)
+
+    def place(self, index, moved):
+        dz, dc = self.order[index]
+        z, c = wrap(self.at["ctx"] - dz, self.line), wrap(self.at["core"] - dc, self.pair)
+        dp, x = [wrap(self.at[name] - moved.get(name, 0), self.sizes[name]) for name in ("dp", "x")]
+        return self.spot(dp, z, x, c)
+
+    def axes(self, index):
+        return ("x", "dp") if sum(self.order[index]) % 2 == 0 else ("dp", "x")
+
+    def ahead(self, name, step):
+        return {name: wrap(self.at[name] + step, self.sizes[name])}
+
+    def came(self, index):
+        spot = self.place(index, {})
+        return self.copy(self.f_sems, index, spot, spot, core=self.at["core"])
+
+    def hop_one(self, index, step):
+        spot = self.place(index, {})
+        return self.copy(self.a_sems, (index, step), spot, spot, **self.ahead(self.axes(index)[0], step))
+
+    def one_came(self, index, step):
+        spot = self.place(index, {self.axes(index)[0]: step})
+        return self.copy(self.a_sems, (index, step), spot, spot, core=self.at["core"])
+
+    def hop_two(self, index, step, far):
+        name, other = self.axes(index)
+        spot = self.place(index, {name: step})
+        return self.copy(self.b_sems, (index, step, far), spot, spot, **self.ahead(other, far))
+
+    def two_came(self, index, step, far):
+        name, other = self.axes(index)
+        spot = self.place(index, {name: step, other: far})
+        return self.copy(self.b_sems, (index, step, far), spot, spot, core=self.at["core"])
+
+    def own(self):
+        source = self.pack.at[self.at["ctx"] * self.pair + self.at["core"]]
+        return pltpu.make_async_copy(source, self.mine(), self.own_sem.at[0])
+
+    def begin(self, *indices):
+        for index in indices:
+            if index == 0:
+                self.own().start()
+            elif index < len(self.order):
+                self.first(index).start()
+
+    def onward(self, index, *more):
+        if index == 0:
+            self.own().wait()
+        else:
+            self.came(index).wait_recv()
+        self.begin(*more)
+        name, other = self.axes(index)
+        for step in range(1, self.sizes[name]):
+            self.hop_one(index, step).start()
+        for far in range(1, self.sizes[other]):
+            self.hop_two(index, 0, far).start()
+
+    def onward_two(self, index):
+        name, other = self.axes(index)
+        for step in range(1, self.sizes[name]):
+            self.one_came(index, step).wait_recv()
+            for far in range(1, self.sizes[other]):
+                self.hop_two(index, step, far).start()
+
+    def complete(self, *indices):
+        for index in indices:
+            name, other = self.axes(index)
+            for step in range(self.sizes[name]):
+                for far in range(1, self.sizes[other]):
+                    self.two_came(index, step, far).wait_recv()
+
+    def drain(self):
+        for index in range(len(self.order)):
+            name, other = self.axes(index)
             if index:
-                first(kind, index).wait_send()
-            name, other = axes(index)
-            for step in range(sizes[name]):
+                self.first(index).wait_send()
+            for step in range(self.sizes[name]):
                 if step:
-                    hop_one(kind, index, step).wait_send()
-                for far in range(1, sizes[other]):
-                    hop_two(kind, index, step, far).wait_send()
-                    two_came(kind, index, step, far).wait_recv()
-
-
-def spread_weights(sizes, collective_id, hidden, gains, *weights):
-    line, pair = sizes["ctx"], sizes["core"]
-    group = line * pair
-    rows = weights[0].shape[0]
-    steps = max(sizes["dp"], sizes["x"])
-    tall, wide = (2 * H * HD + 2 * KV * HD) // group + 128, 3 * FF // group
-    gain_tile = jnp.pad(gains.T, ((0, 0), (0, 126)))
-    any_spec = pl.BlockSpec(memory_space=pl.ANY)
-    vmem = pl.BlockSpec(memory_space=pltpu.VMEM)
-    everyone = (sizes["dp"], line, sizes["x"], pair, rows)
-    low, high, tokens = pl.pallas_call(
-        functools.partial(spread_kernel, sizes),
-        out_shape=[
-            jax.ShapeDtypeStruct(everyone + (tall,), BF),
-            jax.ShapeDtypeStruct(everyone + (wide,), BF),
-            jax.ShapeDtypeStruct((pair, line) + hidden.shape, BF),
-        ],
-        in_specs=[vmem] * 5 + [any_spec],
-        out_specs=[any_spec] * 3,
-        scratch_shapes=[
-            pltpu.VMEM((group, rows, tall), BF),
-            pltpu.VMEM((group, rows, wide), BF),
-            pltpu.SemaphoreType.DMA((2,)),
-            pltpu.SemaphoreType.DMA((2, group)),
-            pltpu.SemaphoreType.DMA((2, group)),
-            pltpu.SemaphoreType.DMA((2, group, steps)),
-            pltpu.SemaphoreType.DMA((2, group, steps)),
-            pltpu.SemaphoreType.DMA((2, group, steps, steps)),
-            pltpu.SemaphoreType.DMA((2, group, steps, steps)),
-            *Travel.sems(1, line),
-        ],
-        compiler_params=pltpu.CompilerParams(
-            collective_id=collective_id, has_side_effects=True, vmem_limit_bytes=40 * 2**20
-        ),
-    )(*weights, gain_tile, hidden)
-    return low.reshape(-1, tall), high.reshape(-1, wide), tokens.reshape(-1, hidden.shape[1])
+                    self.hop_one(index, step).wait_send()
+                for far in range(1, self.sizes[other]):
+                    self.hop_two(index, step, far).wait_send()
 
 
 class Collect:
@@ -961,70 +686,402 @@
     return min(total_rows, 2**18 // total_rows)
 
 
-def each_query_block(total_rows, heads, pos_col, pos_row):
-    size = query_rows(total_rows)
-    for low in range(0, total_rows, size):
-        visible = pos_row[...] <= pos_col[low : low + size, :]
-        for lane in range(0, heads * HD, 2 * HD):
-            yield low, size, visible, lane
-
-
-def attend_kernel(
-    hidden_ref, low_ref, gain_ref, cos_ref, sin_ref, pos_col, pos_row, entry_ref, qkv_ref, heads_ref, qkv_w, load_sem
-):
-    load = pltpu.make_async_copy(low_ref.at[:, pl.ds(0, qkv_w.shape[1])], qkv_w, load_sem)
-    load.start()
-    tokens, total_rows = hidden_ref.shape[0], cos_ref.shape[0]
-    query_cols = heads_ref.shape[1]
-    step = 256
-    load.wait()
-
-    @pl.loop(0, tokens // step)
-    def _(index):
-        at = pl.ds(pl.multiple_of(index * step, step), step)
-        table_at = pl.ds(pl.multiple_of(lax.rem(index * step, total_rows), step), step)
-        rows = hidden_ref[at, :].astype(F32)
-        inverse = lax.rsqrt(jnp.mean(rows * rows, -1, keepdims=True) + EPS_NORM)
-        entry = (rows * inverse * gain_ref[...]).astype(BF)
-        entry_ref[at, :] = entry
-        projected = dot(entry, qkv_w[...])
-        rotated = projected * cos_ref[table_at, :] + turned(projected) * sin_ref[table_at, :]
-        qkv_ref[at, :] = rotated.astype(BF)
-
-    @pl.loop(0, tokens // total_rows)
-    def _(sequence):
+def opening_kernel(sizes, chunks, *refs):
+    line, pair = sizes["ctx"], sizes["core"]
+    group = line * pair
+    refs = list(refs)
+
+    def take(count):
+        taken, refs[:count] = refs[:count], []
+        return taken
+
+    qkv_in, out_in, gate_up_in, down_in, gain_in, hidden_ref, cot_ref, cos_ref, sin_ref, pos_col, pos_row = take(11)
+    output_ref, grad_mid_ref, gain_grad_ref, gains_ref = take(4)
+    low_out, entry_one_out, qkv_out, heads_out, branch_ref, entry_two_out, cots_out, act_out, dgu_out = take(9)
+    stage, tall, wide, low_w, ffn_w, rows_in, cots, qkv, heads, act, dgu = take(11)
+    part, near, landed, total, middle, branch = take(6)
+    stage_sem, out_sem, slot_sem = take(3)
+    tall_sems, wide_sems, reduce_sems, hidden_sems, travel_sems = take(7), take(7), take(4), take(5), take(5)
+
+    rows, width = part.shape[-2:]
+    own_rows = tall.shape[1]
+    block_rows = rows * chunks
+    tokens = group * rows
+    total_rows = cos_ref.shape[0]
+    qkv_cols, query_cols = qkv.shape[1], heads.shape[-1]
+    units = ffn_w.shape[-1] // 3
+    groups = ffn_w.shape[0]
+    core, here = lax.axis_index("core"), lax.axis_index("ctx")
+    steps, travels, sums = [], [], []
+    low, high = Spread(sizes, tall, low_w, tall_sems), Spread(sizes, wide, ffn_w, wide_sems)
+    gain_rows = [gains_ref.at[pl.ds(0, 1)], gains_ref.at[pl.ds(1, 1)]]
+
+    def step(time, function, *values):
+        steps.append((time, functools.partial(function, *values)))
+
+    def chunk_rows(chunk):
+        return slice(chunk * rows, (chunk + 1) * rows)
+
+    def staged(member):
+        slot = member % 2
+        sources = (
+            gate_up_in.at[:, pl.ds(member * units, units)],
+            gate_up_in.at[:, pl.ds(FF + member * units, units)],
+            down_in.at[:, pl.ds(member * units, units)],
+        )
+        return [
+            pltpu.make_async_copy(
+                source, stage.at[slot, :, pl.ds(index * units, units)], stage_sem.at[slot, index]
+            )
+            for index, source in enumerate(sources)
+        ]
+
+    def pack_low():
+        keys = KV * HD // group
+        heads_of = H * HD // group
+        for member in range(group):
+            key_at, value_at = H * HD + member * keys, (H + KV) * HD + member * keys
+            tall[member, :, :heads_of] = qkv_in[:, member * heads_of : (member + 1) * heads_of].astype(BF)
+            both = jnp.concatenate(
+                [qkv_in[:, key_at : key_at + keys], qkv_in[:, value_at : value_at + keys]], 1
+            )
+            tall[member, :, heads_of:qkv_cols] = both.astype(BF)
+            tall[member, :, qkv_cols : qkv_cols + heads_of] = out_in[
+                :, member * heads_of : (member + 1) * heads_of
+            ].astype(BF)
+            tall[member, :, qkv_cols + heads_of :] = gain_in[...].astype(BF)
+
+    def pack_high():
+        for member in range(group):
+            for load in staged(member):
+                load.wait()
+            wide[member] = stage[member % 2].astype(BF)
+            if member + 2 < group:
+                for load in staged(member + 2):
+                    load.start()
+
+    def columns_of(weight, first, size):
+        return weight[:, :, :, first : first + size].reshape(width, size)
+
+    def rows_of(weight, index, count, first, size):
+        each = groups // count
+        return weight[index * each : (index + 1) * each, :, :, first : first + size].reshape(-1, size)
+
+    def gains_to_rows():
+        columns = columns_of(low_w, qkv_cols + query_cols, 128).astype(F32)
+        gains_ref[...] = columns.T[:8, :]
+
+    def project(sequence):
+        weight = columns_of(low_w, 0, qkv_cols)
+
+        @pl.loop(0, line)
+        def _(z):
+            values = rows_in[:, sequence, z].reshape(block_rows, width).astype(F32)
+            inverse = lax.rsqrt(jnp.mean(values * values, -1, keepdims=True) + EPS_NORM)
+            entry = (values * inverse * gain_rows[0][...]).astype(BF)
+            rows_in[:, sequence, z] = entry.reshape(chunks, rows, width)
+            projected = dot(entry, weight)
+            table_at = pl.ds(pl.multiple_of(z * block_rows, block_rows), block_rows)
+            rotated = projected * cos_ref[table_at, :] + turned(projected) * sin_ref[table_at, :]
+            at = pl.ds(pl.multiple_of((sequence * line + z) * block_rows, block_rows), block_rows)
+            qkv[at, :] = rotated.astype(BF)
+
+    def attention(sequence, first, size, lane):
         start = sequence * total_rows
-        both = qkv_ref[pl.ds(pl.multiple_of(start, total_rows), total_rows), query_cols:]
+        both = qkv[start : start + total_rows, query_cols:]
         keys, values = both_halves(both, 0), both_halves(both, 1)
-        for low, size, visible, lane in each_query_block(total_rows, query_cols // HD, pos_col, pos_row):
-            at = pl.ds(pl.multiple_of(start + low, 128), size)
-            queries = qkv_ref[at, lane : lane + 2 * HD]
-            pair = [
-                dot(softmax_rows(only_head(queries, head), keys, visible).astype(BF), values)
-                for head in range(2)
-            ]
-            heads_ref[at, lane : lane + 2 * HD] = jnp.where(
-                lane_index(pair[0].shape) < HD, pair[0], pair[1]
-            ).astype(BF)
-
-
-def attend(hidden_all, low, gain, tables):
-    tokens, width = hidden_all.shape
-    qkv_cols = tables[0].shape[1]
-    query_cols = qkv_cols - 2 * HD
+        visible = pos_row[...] <= pos_col[first : first + size, :]
+        queries = qkv[start + first : start + first + size, lane : lane + 2 * HD]
+        two = [
+            dot(softmax_rows(only_head(queries, head), keys, visible).astype(BF), values)
+            for head in range(2)
+        ]
+        merged = jnp.where(lane_index(two[0].shape) < HD, two[0], two[1]).astype(BF)
+        from_z, to_z = first // block_rows, (first + size) // block_rows
+        heads[sequence, from_z:to_z, :, lane : lane + 2 * HD] = merged.reshape(-1, block_rows, 2 * HD)
+
+    def entry_one_copies():
+        return [
+            pltpu.make_async_copy(rows_in.at[:, c, z], entry_one_out.at[c, z], out_sem.at[3 + c * line + z])
+            for c in range(pair)
+            for z in range(line)
+        ]
+
+    whole_copies = [
+        pltpu.make_async_copy(low_w, low_out, out_sem.at[0]),
+        pltpu.make_async_copy(qkv, qkv_out, out_sem.at[1]),
+        pltpu.make_async_copy(heads, heads_out, out_sem.at[2]),
+    ]
+
+    def chunk_copies(chunk):
+        return [
+            pltpu.make_async_copy(source, target.at[chunk], slot_sem.at[chunk, index])
+            for index, (source, target) in enumerate(
+                (
+                    (act.at[chunk % 2], act_out),
+                    (dgu.at[chunk % 2], dgu_out),
+                    (rows_in.at[chunk], entry_two_out),
+                    (cots.at[chunk], cots_out),
+                )
+            )
+        ]
+
+    def start_all(copies):
+        for copy in copies:
+            copy.start()
+
+    def wait_all(copies):
+        for copy in copies:
+            copy.wait()
+
+    def reducer(kind, chunk):
+        one = Reduce(line, pair, part, near, landed, *reduce_sems, (kind // 2, chunk), kind)
+        sums.append(one)
+        return one
+
+    def traveller(sems, source, place, start, hop):
+        one = Travel(line, pair, [source], [place], *sems)
+        steps.append((start, one.begin))
+        for index in range(line - 1):
+            steps.append((start + (index + 1) * hop, functools.partial(one.step, index)))
+        finish = start + line * hop - 1.0
+        steps.append((finish, one.end))
+        return finish
+
+    def product(chunk):
+        mine = heads[:, :, chunk_rows(chunk), :].reshape(tokens, query_cols)
+        for index in range(4):
+            at = slice(index * (width // 4), (index + 1) * (width // 4))
+            term = contract_cols(mine, rows_of(low_w, index, 4, qkv_cols, query_cols)).astype(BF)
+            part[0, chunk, :, :, :, at] = term.reshape(pair, line, rows, -1)
+
+    def norm_rows(chunk):
+        mid = hidden_ref[chunk].astype(F32) + total[...]
+        middle[chunk_rows(chunk), :] = mid
+        inverse = lax.rsqrt(jnp.mean(mid * mid, -1, keepdims=True) + EPS_NORM)
+        rows_in[chunk, core, here] = (mid * inverse * gain_rows[1][...]).astype(BF)
+
+    def units_part(chunk, index, count):
+        size = units // count
+        slot = chunk % 2
+        entry = rows_in[chunk].reshape(tokens, width)
+        first, last = index * size, (index + 1) * size
+        gate = dot(entry, columns_of(ffn_w, first, size))
+        up = dot(entry, columns_of(ffn_w, units + first, size))
+        grad_act = dot(cots[chunk].reshape(tokens, width), columns_of(ffn_w, 2 * units + first, size))
+        sigmoid = 1.0 / (1.0 + jnp.exp(-gate))
+        silu = gate * sigmoid
+        act[slot, :, first:last] = (silu * up).astype(BF)
+        dgu[slot, :, first:last] = (grad_act * up * sigmoid * (1.0 + gate * (1.0 - sigmoid))).astype(BF)
+        dgu[slot, :, units + first : units + last] = (grad_act * silu).astype(BF)
+
+    def back_part(chunk, index, count):
+        size = width // count
+        at = slice(index * size, (index + 1) * size)
+        term = contract_cols(dgu[chunk % 2], rows_of(ffn_w, index, count, 0, 2 * units)).astype(BF)
+        part[0, chunk, :, :, :, at] = term.reshape(pair, line, rows, size)
+
+    def down_part(chunk, index, count):
+        size = width // count
+        at = slice(index * size, (index + 1) * size)
+        term = contract_cols(act[chunk % 2], rows_of(ffn_w, index, count, 2 * units, units)).astype(BF)
+        part[1, chunk, :, :, :, at] = term.reshape(pair, line, rows, size)
+
+    def norm_rows_back(chunk):
+        mid = middle[chunk_rows(chunk), :]
+        inverse = lax.rsqrt(jnp.mean(mid * mid, -1, keepdims=True) + EPS_NORM)
+        normed = mid * inverse
+        grad_entry = total[...]
+        gain_term = jnp.sum(grad_entry * normed, 0, keepdims=True)
+        if chunk == 0:
+            gain_grad_ref[...] = gain_term
+        else:
+            gain_grad_ref[...] += gain_term
+        grad_normed = grad_entry * gain_rows[1][...]
+        grad_rows = inverse * (
+            grad_normed - normed * jnp.mean(grad_normed * normed, -1, keepdims=True)
+        )
+        grad_mid = cot_ref[chunk].astype(F32) + grad_rows
+        grad_mid_ref[chunk_rows(chunk), :] = grad_mid
+        branch[chunk] = grad_mid.astype(BF)
+
+    def write_output(chunk):
+        output_ref[chunk_rows(chunk), :] = (middle[chunk_rows(chunk), :] + total[...]).astype(BF)
+
+    for member in range(2):
+        start_all(staged(member))
+    greet_all(sizes)
+
+    step(0.0, pack_low)
+    hidden_done = traveller(
+        hidden_sems, hidden_ref, lambda c, z: rows_in.at[:, c, z], 0.0, T_HIDDEN
+    )
+    step(0.1, low.begin, *range(group))
+    step(0.2, pack_high)
+    step(0.3, high.begin, *range(min(group, 4)))
+    for index in range(group):
+        when = 1.0 + T_LOW * (index // 2)
+        step(when, low.onward, index)
+        step(when + T_LOW + 1.0, low.onward_two, index)
+        when = 1.0 + T_HIGH * (index // 2)
+        step(when, high.onward, index, *([index + 2] if index >= 2 else []))
+        step(when + T_HIGH * 0.6, high.onward_two, index)
+    weights_there = 1.0 + T_HIGH * (group // 2) + 8.0
+
+    now = max(hidden_done + 0.2, 1.0 + T_LOW * (group // 2) + 6.0)
+    step(now, low.complete, *range(group))
+    step(now, gains_to_rows)
+    step(now, whole_copies[0].start)
+    for sequence in range(pair * line * block_rows // total_rows):
+        step(now + 0.1, project, sequence)
+        now += 2.5
+    step(now, start_all, entry_one_copies())
+    step(now, whole_copies[1].start)
+    size = query_rows(total_rows) // 2
+    for sequence in range(pair * line * block_rows // total_rows):
+        for first in range(0, total_rows, size):
+            for lane in range(0, query_cols, 2 * HD):
+                step(now + 0.1, attention, sequence, first, size, lane)
+                now += 1.0
+    step(now, whole_copies[2].start)
+    step(now, wait_all, entry_one_copies())
+
+    span = (line - 1) * SEND
+    ready_ffn, ready_back, base = weights_there, 0.0, now + 0.5
+    count = 4
+    for chunk in range(chunks):
+        cot_done = traveller(
+            [sem.at[0, chunk] for sem in travel_sems],
+            cot_ref.at[chunk],
+            lambda c, z, k=chunk: cots.at[k, c, z],
+            base + chunk * span,
+            HOP,
+        )
+        begin = base + 1.0 + chunk * span
+        step(begin - 0.5, product, chunk)
+        first_sum = reducer(0, chunk)
+        more, finish = first_sum.plan(begin, total, functools.partial(norm_rows, chunk))
+        steps.extend(more)
+        arrived = traveller(
+            [sem.at[1, chunk] for sem in travel_sems],
+            None,
+            lambda c, z, k=chunk: rows_in.at[k, c, z],
+            finish,
+            HOP,
+        )
+        begin = max(arrived, cot_done, ready_ffn) + 0.1
+        if chunk == 0:
+            step(begin, high.complete, *range(group))
+        if chunk >= 2:
+            step(begin, wait_all, chunk_copies(chunk - 2))
+        step(begin, first_sum.drain)
+        for index in range(count):
+            step(begin + index, units_part, chunk, index, count)
+        for index in range(count):
+            step(begin + 4 + 0.8 * index, back_part, chunk, index, count)
+        for index in range(count):
+            step(begin + 7.3 + 0.5 * index, down_part, chunk, index, count)
+        step(begin + 4.0, start_all, chunk_copies(chunk))
+        ready_ffn = begin + 9.5
+        begin = max(begin + 7.25, ready_back)
+        ready_back = begin + span
+        more, finish = reducer(1, chunk).plan(begin, total, functools.partial(norm_rows_back, chunk))
+        steps.extend(more)
+        traveller(
+            [sem.at[2, chunk] for sem in travel_sems],
+            branch.at[chunk],
+            lambda c, z, k=chunk: branch_ref.at[c, z, pl.ds(k * rows, rows)],
+            finish,
+            HOP,
+        )
+    for chunk in range(chunks):
+        begin = ready_back + chunk * span
+        steps.extend(reducer(2, chunk).plan(begin, total, functools.partial(write_output, chunk))[0])
+    run_steps(steps)
+    for one in sums:
+        if one.sem_at[0]:
+            one.drain()
+    low.drain()
+    high.drain()
+    wait_all(whole_copies)
+    for chunk in range(max(0, chunks - 2), chunks):
+        wait_all(chunk_copies(chunk))
+
+
+T_HIDDEN, T_LOW, T_HIGH = 14.0, 7.0, 28.0
+
+
+def opening(sizes, collective_id, weights, gains, hidden, cot, tables):
+    line, pair = sizes["ctx"], sizes["core"]
+    group = line * pair
+    block_rows, width = hidden.shape
+    chunks = 4
+    rows = block_rows // chunks
+    tokens = group * rows
+    own_rows = weights[0].shape[0]
+    heads, keys, units = H * HD // group, KV * HD // group, FF // group
+    qkv_cols = heads + 2 * keys
+    tall, wide = qkv_cols + heads + 128, 3 * units
+    blocks = (sizes["dp"] * line, sizes["x"] * pair, own_rows)
+    gain_tile = jnp.pad(gains.T, ((0, 0), (0, 126)))
+    any_spec = pl.BlockSpec(memory_space=pl.ANY)
     vmem = pl.BlockSpec(memory_space=pltpu.VMEM)
-    return pl.pallas_call(
-        attend_kernel,
+    shape = jax.ShapeDtypeStruct
+    dma = pltpu.SemaphoreType.DMA
+    by_chunk = (chunks, pair, line, rows, width)
+    outs = pl.pallas_call(
+        functools.partial(opening_kernel, sizes, chunks),
         out_shape=[
-            jax.ShapeDtypeStruct((tokens, width), BF),
-            jax.ShapeDtypeStruct((tokens, qkv_cols), BF),
-            jax.ShapeDtypeStruct((tokens, query_cols), BF),
+            shape((block_rows, width), BF),
+            shape((block_rows, width), F32),
+            shape((1, width), F32),
+            shape((8, width), F32),
+            shape(blocks + (tall,), BF),
+            shape((pair, line, chunks, rows, width), BF),
+            shape((group * block_rows, qkv_cols), BF),
+            shape((pair, line, block_rows, heads), BF),
+            shape((pair, line, block_rows, width), BF),
+            shape(by_chunk, BF),
+            shape(by_chunk, BF),
+            shape((chunks, tokens, units), BF),
+            shape((chunks, tokens, 2 * units), BF),
         ],
-        in_specs=[vmem, pl.BlockSpec(memory_space=pl.ANY)] + [vmem] * 5,
-        out_specs=[vmem] * 3,
-        scratch_shapes=[pltpu.VMEM((width, qkv_cols), BF), pltpu.SemaphoreType.DMA],
-        compiler_params=pltpu.CompilerParams(vmem_limit_bytes=56 * 2**20),
-    )(hidden_all, low, gain, *tables)
+        in_specs=[vmem, vmem, any_spec, any_spec] + [vmem] * 7,
+        out_specs=[vmem] * 4 + [any_spec] * 9,
+        scratch_shapes=[
+            pltpu.VMEM((2, own_rows, wide), F32),
+            pltpu.VMEM((group, own_rows, tall), BF),
+            pltpu.VMEM((group, own_rows, wide), BF),
+            pltpu.VMEM(blocks + (tall,), BF),
+            pltpu.VMEM(blocks + (wide,), BF),
+            pltpu.VMEM(by_chunk, BF),
+            pltpu.VMEM(by_chunk, BF),
+            pltpu.VMEM((group * block_rows, qkv_cols), BF),
+            pltpu.VMEM((pair, line, block_rows, heads), BF),
+            pltpu.VMEM((2, tokens, units), BF),
+            pltpu.VMEM((2, tokens, 2 * units), BF),
+            *Reduce.room(line, pair, rows, width, 2, chunks),
+            pltpu.VMEM((rows, width), F32),
+            pltpu.VMEM((block_rows, width), F32),
+            pltpu.VMEM((chunks, rows, width), BF),
+            dma((2, 3)),
+            dma((3 + group,)),
+            dma((chunks, 4)),
+            *Spread.sems(sizes),
+            *Spread.sems(sizes),
+            *Reduce.sems(3, chunks)(line),
+            *Travel.sems(1, line),
+            dma((3, chunks, 1)),
+            *[dma((3, chunks, 1, 2, line))] * 4,
+        ],
+        compiler_params=pltpu.CompilerParams(
+            collective_id=collective_id, has_side_effects=True, vmem_limit_bytes=63 * 2**20
+        ),
+    )(*weights, gain_tile, hidden.reshape(chunks, rows, width), cot.reshape(chunks, rows, width), *tables)
+    output, grad_mid, gain_grad, gain_rows, low, *rest = outs
+    return output, grad_mid, gain_grad, gain_rows, low.reshape(width, tall), [
+        array.reshape(-1, array.shape[-1]) for array in rest
+    ]
 
 
 class GainSum:
@@ -1454,18 +1511,15 @@
         [sin_tab * signs] * (heads + kv_heads) + [jnp.zeros_like(sin_tab)] * kv_heads, 1
     )
     tables = (cosines, sines, key_pos[:, None], key_pos[None, :])
-    low, high, hidden_all = spread_weights(
-        sizes, 0, hidden[0], norm_gains, w_qkv, w_out, w_gate_up, w_down
+    weights = (w_qkv, w_out, w_gate_up, w_down)
+    output, grad_middle, grad_gain_two, gains, low, rest = opening(
+        sizes, 0, weights, norm_gains, hidden[0], cotangent[0], tables
     )
-    gains = low[:, 2 * query_cols + 2 * kv_cols :].astype(F32)[:, :2].T
-    gain_one, gain_two = gains[:1], gains[1:]
-    entry_one, qkv, attended = attend(hidden_all, low, gain_one, tables)
-    output, grad_middle, grad_gain_two, grad_branch, entry_two, cot, activated, grad_gu = middle_rows(
-        sizes, 1, attended, low, high, hidden[0], cotangent[0], gain_two
-    )
+    entry_one, qkv, attended, grad_branch, entry_two, cot, activated, grad_gu = rest
+    gain_one = gains[:1]
     factors = (entry_two, grad_gu, cot, activated, entry_one, grad_branch, qkv, attended)
     *pieces, grad_hidden, gain_sums = closing(
-        sizes, 2, factors, low, hidden[0], grad_middle, gain_one, grad_gain_two, tables
+        sizes, 1, factors, low, hidden[0], grad_middle, gain_one, grad_gain_two, tables
     )
     grad_gate, grad_up, grad_down, grad_query, grad_key_value, grad_out = pieces
     output, grad_hidden = output[None], grad_hidden[None]

time: 614 us -> 561 us (0.914)
  Pallas kernels: 574 us -> 533 us
  local copies, waits for them, and re-layouts: 20.4 us -> 10.3 us
    pallas_call x3 -> x1, Pallas kernels: 364 us -> 322 us  [opening(): pl.pallas_call(functools.partial(opening_kernel, sizes, chunks), out_shap...]
    unnamed x32 -> x17, local copies, waits for them, and re-layouts: 11.1 us -> 2.38 us
where the time goes in v5:
time: 561 us; the launch traced here: 551 us
  Pallas kernels  533 us (95%)
  local copies, waits for them, and re-layouts  10.3 us (2%)
  other arithmetic  7.12 us (1%)
    pallas_call x1, Pallas kernels, opening(): pl.pallas_call(functools.partial(opening_kernel, sizes, chunks), out_shap...  322 us
    pallas_call x1, Pallas kernels, closing(): pl.pallas_call(functools.partial(closing_kernel, sizes, chunks), out_shap...  177 us
    pallas_call x4, Pallas kernels, adamw_columns(): pl.pallas_call(functools.partial(adamw_kernel, step_rate, decay_rate), gr...  34.1 us

profile of v5, /device:TPU:0, one launch (start us, length us, event | category | flops | bytes accessed | tf_op | source)
XLA Modules:
  0.0 551.3 jit_solution(5119882846795808025)
XLA Ops:
  0.7 0.8 copy.32
  1.4 0.6 pad.4.refs_4_
  2.1 0.7 broadcast_multiply_fusion
  2.7 0.1 iota_add_fusion
  2.8 0.1 convert_element_type.13
  2.9 1.0 multiply_sine_fusion
  3.9 1.6 concatenate.17.refs_7_.refs_13_
  5.5 0.1 maximum_multiply_fusion
  5.7 1.2 concatenate.19.refs_8_.refs_14_
  6.9 0.9 add.94.refs_9_.refs_15_
  7.8 0.7 add.84.refs_10_.refs_16_
  8.5 321.8 %shard_map.260 = (bf16[128,2048]{1,0:T(8,128)(2,1)}, f32[128,2048]{1,0:T(8,128)}, f32[1,2048]{1,0:T(1,128)}, f32[8,2048]{1,0:T(8,128)}, bf16[8,4,64,768]{3,2,1,0...) custom-call(f32[64,3072]{1,0:T(8,128)} %weight_ref.4, ...), custom_call_target="tpu_custom_call" | custom-call | tf_op jit(solution)/shard_map/pallas_call | solution.py:1032
  330.3 1.4 slice.10.refs_11_
  331.8 176.9 %shard_map.261 = (bf16[64,8192]{1,0:T(8,128)(2,1)}, bf16[64,8192]{1,0:T(8,128)(2,1)}, bf16[64,8192]{1,0:T(8,128)(2,1)}, bf16[64,2048]{1,0:T(8,128)(2,1)}, bf16[6...) custom-call(bf16[1024,2048]{1,0:T(8,128)(2,1)} %bitcast.37, ...), custom_call_target="tpu_custom_call" | custom-call | tf_op jit(solution)/shard_map/pallas_call | solution.py:1395
  508.7 0.0 copy-start
  508.7 0.0 copy-start.1
  508.7 0.0 copy-done.4
  508.7 0.9 fusion.3
  509.6 1.1 reshape.155
  510.8 0.2 reshape.156
  511.0 1.7 pad_maximum_fusion.1.grad_ref
  512.7 4.5 shard_map.262
  517.2 2.7 shard_map.263
  519.9 0.0 copy-done
  519.9 0.0 copy-done.1
  519.9 1.5 pad_maximum_fusion.grad_ref
  521.4 17.7 %shard_map.264 = (f32[64,16384]{1,0:T(8,128)}, f32[64,16384]{1,0:T(8,128)}, f32[2,64,16384]{2,1,0:T(8,128)}) custom-call(bf16[64,16384]{1,0:T(8,128)(2,1)} %pad_maximum_fusion.grad_ref, f32[64,16384]{1,0:T(8,128)} %weight_ref.6, f32[2,64,16384]{2,1,0:T(8,128)} %state_ref.6), custom_call_target="tpu_custom_call" | custom-call | tf_op jit(solution)/shard_map/pallas_call | solution.py:1463
  539.1 9.2 %shard_map.265 = (f32[64,8192]{1,0:T(8,128)}, f32[64,8192]{1,0:T(8,128)}, f32[2,64,8192]{2,1,0:T(8,128)}) custom-call(bf16[64,8192]{1,0:T(8,128)(2,1)} %get-tuple-element.73.grad_ref, f32[64,8192]{1,0:T(8,128)} %weight_ref.7, f32[2,64,8192]{2,1,0:T(8,128)} %state_ref.7), custom_call_target="tpu_custom_call" | custom-call | tf_op jit(solution)/shard_map/pallas_call | solution.py:1463
  548.3 0.6 fusion.4
  548.9 0.6 pad_maximum_fusion.2
  549.4 0.8 copy.40
  550.2 0.8 copy.41
  (14 shorter events, 0.1 us)
Async XLA Ops:
  331.8 176.9 %copy-start.4 = (f32[2,2,64]{2,1,0:T(2,128)S(1)}, f32[2,2,64]{2,1,0:T(2,128)}, u32[]{:S(2)}) copy-start(f32[2,2,64]{2,1,0:T(2,128)} %param.21) | copy-start | bytes 3076
  508.7 11.2 %copy-start = (bf16[64,8192]{1,0:T(8,128)(2,1)S(1)}, bf16[64,8192]{1,0:T(8,128)(2,1)}, u32[]{:S(2)}) copy-start(bf16[64,8192]{1,0:T(8,128)(2,1)} %get-tuple-element.70) | copy-start | bytes 3145732
  508.7 11.2 %copy-start.1 = (bf16[64,8192]{1,0:T(8,128)(2,1)S(1)}, bf16[64,8192]{1,0:T(8,128)(2,1)}, u32[]{:S(2)}) copy-start(bf16[64,8192]{1,0:T(8,128)(2,1)} %get-tuple-element.71) | copy-start | bytes 3145732
  509.6 38.6 %copy-start.6 = (f32[2,64]{1,0:T(2,128)}, f32[2,64]{1,0:T(2,128)S(1)}, u32[]{:S(2)}) copy-start(f32[2,64]{1,0:T(2,128)S(1)} %get-tuple-element.110) | copy-start | bytes 1540
  539.0 9.2 %copy-start.5 = (f32[2,64]{1,0:T(2,128)S(1)}, f32[2,64]{1,0:T(2,128)}, u32[]{:S(2)}) copy-start(f32[2,64]{1,0:T(2,128)} %param.16) | copy-start | bytes 1540
  539.0 10.4 %copy-start.2 = (bf16[128,2048]{1,0:T(8,128)(2,1)S(1)}, bf16[128,2048]{1,0:T(8,128)(2,1)}, u32[]{:S(2)}) copy-start(bf16[128,2048]{1,0:T(8,128)(2,1)} %get-tuple-element.50) | copy-start | bytes 1572868
  539.1 11.2 %copy-start.3 = (bf16[128,2048]{1,0:T(8,128)(2,1)S(1)}, bf16[128,2048]{1,0:T(8,128)(2,1)}, u32[]{:S(2)}) copy-start(bf16[128,2048]{1,0:T(8,128)(2,1)} %get-tuple-element.63) | copy-start | bytes 1572868

commit v6 on v5

--- a/solution.py
+++ b/solution.py
@@ -243,7 +243,7 @@
 
     def __init__(self, line, pair, part, near, landed, core_send, core_recv, line_send, line_recv, at, kind=None):
         self.line, self.pair, self.at = line, pair, at
-        self.sem_at = at if kind is None else (kind,) + at[1:]
+        self.sem_at = at if kind is None else (kind, at[-1])
         self.part, self.near, self.landed = part, near, landed
         self.core_sems, self.line_sems = (core_send, core_recv), (line_send, line_recv)
         self.here, self.core = lax.axis_index("ctx"), lax.axis_index("core")
@@ -334,7 +334,7 @@
         return steps, finish
 
 
-SEND, HOP, LAG = 3.0, 4.5, 2.5
+SEND, HOP, LAG = 4.0, 7.0, 5.0
 
 
 def run_steps(steps):
@@ -507,7 +507,7 @@
         self.rows = self.terms.shape[-2]
         self.at = {name: lax.axis_index(name) for name in ("dp", "ctx", "x", "core")}
         self.me = self.at["ctx"] * self.pair + self.at["core"]
-        self.away = sorted(range(self.line), key=lambda d: -min(d, self.line - d))
+        self.away = sorted(range(self.line), key=lambda d: (d != 0, -min(d, self.line - d)))
         self.order = [(dz, dc) for dz in self.away for dc in range(self.pair)]
 
     def spot_of(self, index, sign=1):
@@ -531,26 +531,23 @@
         z = wrap(self.at["ctx"] + self.away[tick], self.line)
         return pl.ds(pl.multiple_of((dp * self.line + z) * across, 128), across)
 
-    def multiply(self, tick, lefts, rights):
-        start = 0
-        for left, right, width in zip(lefts, rights, self.widths):
-            step = math.gcd(width, 512)
-
-            @pl.loop(0, self.sizes["dp"])
-            def _(dp, left=left, right=right, start=start, width=width, step=step):
-                left_t = left[dp].T
-
-                @pl.loop(0, width // step)
-                def _(part):
-                    columns = pl.ds(pl.multiple_of(part * step, 128), step)
-                    into = pl.ds(pl.multiple_of(start + part * step, 128), step)
-                    product = dot(left_t, right[:, columns]).astype(BF)
-                    for x in range(self.sizes["x"]):
-                        for core in range(self.pair):
-                            low = (x * self.pair + core) * self.rows
-                            self.terms[tick, dp, x, core, :, into] = product[low : low + self.rows]
-
-            start += width
+    def multiply(self, tick, item, left, right):
+        start, width = sum(self.widths[:item]), self.widths[item]
+        step = math.gcd(width, 512)
+
+        @pl.loop(0, self.sizes["dp"])
+        def _(dp):
+            left_t = left[dp].T
+
+            @pl.loop(0, width // step)
+            def _(part):
+                columns = pl.ds(pl.multiple_of(part * step, 128), step)
+                into = pl.ds(pl.multiple_of(start + part * step, 128), step)
+                product = dot(left_t, right[:, columns]).astype(BF)
+                for x in range(self.sizes["x"]):
+                    for core in range(self.pair):
+                        low = (x * self.pair + core) * self.rows
+                        self.terms[tick, dp, x, core, :, into] = product[low : low + self.rows]
 
     def block_terms(self, index, first_at, other_at):
         name, other = self.axes(index)
@@ -666,6 +663,11 @@
     return jnp.where(lane_index(values.shape) % HD < half, ahead, behind)
 
 
+def for_heads(table, columns):
+    pair = 2 * HD
+    return jnp.concatenate([table[:, :pair]] * ((columns - pair) // pair) + [table[:, pair:]], 1)
+
+
 def only_head(values, head):
     return jnp.where(lane_index(values.shape) // HD == head, values, jnp.zeros_like(values))
 
@@ -683,7 +685,7 @@
 
 
 def query_rows(total_rows):
-    return min(total_rows, 2**18 // total_rows)
+    return min(total_rows, 2**17 // total_rows)
 
 
 def opening_kernel(sizes, chunks, *refs):
@@ -696,11 +698,11 @@
         return taken
 
     qkv_in, out_in, gate_up_in, down_in, gain_in, hidden_ref, cot_ref, cos_ref, sin_ref, pos_col, pos_row = take(11)
-    output_ref, grad_mid_ref, gain_grad_ref, gains_ref = take(4)
-    low_out, entry_one_out, qkv_out, heads_out, branch_ref, entry_two_out, cots_out, act_out, dgu_out = take(9)
+    output_ref, middle, gains_ref = take(3)
+    low_out, entry_one_out, qkv_out, heads_out, terms_out, entry_two_out, cots_out, act_out, dgu_out = take(9)
     stage, tall, wide, low_w, ffn_w, rows_in, cots, qkv, heads, act, dgu = take(11)
-    part, near, landed, total, middle, branch = take(6)
-    stage_sem, out_sem, slot_sem = take(3)
+    part, near, landed, total = take(4)
+    stage_sem, out_sem, slot_sem, terms_sem = take(4)
     tall_sems, wide_sems, reduce_sems, hidden_sems, travel_sems = take(7), take(7), take(4), take(5), take(5)
 
     rows, width = part.shape[-2:]
@@ -782,7 +784,8 @@
             rows_in[:, sequence, z] = entry.reshape(chunks, rows, width)
             projected = dot(entry, weight)
             table_at = pl.ds(pl.multiple_of(z * block_rows, block_rows), block_rows)
-            rotated = projected * cos_ref[table_at, :] + turned(projected) * sin_ref[table_at, :]
+            cosine, sine = for_heads(cos_ref[table_at, :], qkv_cols), for_heads(sin_ref[table_at, :], qkv_cols)
+            rotated = projected * cosine + turned(projected) * sine
             at = pl.ds(pl.multiple_of((sequence * line + z) * block_rows, block_rows), block_rows)
             qkv[at, :] = rotated.astype(BF)
 
@@ -887,23 +890,8 @@
         term = contract_cols(act[chunk % 2], rows_of(ffn_w, index, count, 2 * units, units)).astype(BF)
         part[1, chunk, :, :, :, at] = term.reshape(pair, line, rows, size)
 
-    def norm_rows_back(chunk):
-        mid = middle[chunk_rows(chunk), :]
-        inverse = lax.rsqrt(jnp.mean(mid * mid, -1, keepdims=True) + EPS_NORM)
-        normed = mid * inverse
-        grad_entry = total[...]
-        gain_term = jnp.sum(grad_entry * normed, 0, keepdims=True)
-        if chunk == 0:
-            gain_grad_ref[...] = gain_term
-        else:
-            gain_grad_ref[...] += gain_term
-        grad_normed = grad_entry * gain_rows[1][...]
-        grad_rows = inverse * (
-            grad_normed - normed * jnp.mean(grad_normed * normed, -1, keepdims=True)
-        )
-        grad_mid = cot_ref[chunk].astype(F32) + grad_rows
-        grad_mid_ref[chunk_rows(chunk), :] = grad_mid
-        branch[chunk] = grad_mid.astype(BF)
+    def terms_copy(chunk):
+        return pltpu.make_async_copy(part.at[0, chunk], terms_out.at[chunk], terms_sem.at[chunk])
 
     def write_output(chunk):
         output_ref[chunk_rows(chunk), :] = (middle[chunk_rows(chunk), :] + total[...]).astype(BF)
@@ -937,7 +925,7 @@
         now += 2.5
     step(now, start_all, entry_one_copies())
     step(now, whole_copies[1].start)
-    size = query_rows(total_rows) // 2
+    size = query_rows(total_rows)
     for sequence in range(pair * line * block_rows // total_rows):
         for first in range(0, total_rows, size):
             for lane in range(0, query_cols, 2 * HD):
@@ -978,24 +966,14 @@
         for index in range(count):
             step(begin + index, units_part, chunk, index, count)
         for index in range(count):
-            step(begin + 4 + 0.8 * index, back_part, chunk, index, count)
+            step(begin + 4 + 0.5 * index, down_part, chunk, index, count)
         for index in range(count):
-            step(begin + 7.3 + 0.5 * index, down_part, chunk, index, count)
+            step(begin + 6.3 + 0.8 * index, back_part, chunk, index, count)
         step(begin + 4.0, start_all, chunk_copies(chunk))
+        step(begin + 9.4, terms_copy(chunk).start)
         ready_ffn = begin + 9.5
-        begin = max(begin + 7.25, ready_back)
+        begin = max(begin + 6.2, ready_back)
         ready_back = begin + span
-        more, finish = reducer(1, chunk).plan(begin, total, functools.partial(norm_rows_back, chunk))
-        steps.extend(more)
-        traveller(
-            [sem.at[2, chunk] for sem in travel_sems],
-            branch.at[chunk],
-            lambda c, z, k=chunk: branch_ref.at[c, z, pl.ds(k * rows, rows)],
-            finish,
-            HOP,
-        )
-    for chunk in range(chunks):
-        begin = ready_back + chunk * span
         steps.extend(reducer(2, chunk).plan(begin, total, functools.partial(write_output, chunk))[0])
     run_steps(steps)
     for one in sums:
@@ -1004,6 +982,7 @@
     low.drain()
     high.drain()
     wait_all(whole_copies)
+    wait_all([terms_copy(chunk) for chunk in range(chunks)])
     for chunk in range(max(0, chunks - 2), chunks):
         wait_all(chunk_copies(chunk))
 
@@ -1034,20 +1013,19 @@
         out_shape=[
             shape((block_rows, width), BF),
             shape((block_rows, width), F32),
-            shape((1, width), F32),
             shape((8, width), F32),
             shape(blocks + (tall,), BF),
             shape((pair, line, chunks, rows, width), BF),
             shape((group * block_rows, qkv_cols), BF),
             shape((pair, line, block_rows, heads), BF),
-            shape((pair, line, block_rows, width), BF),
+            shape(by_chunk, BF),
             shape(by_chunk, BF),
             shape(by_chunk, BF),
             shape((chunks, tokens, units), BF),
             shape((chunks, tokens, 2 * units), BF),
         ],
         in_specs=[vmem, vmem, any_spec, any_spec] + [vmem] * 7,
-        out_specs=[vmem] * 4 + [any_spec] * 9,
+        out_specs=[vmem] * 3 + [any_spec] * 9,
         scratch_shapes=[
             pltpu.VMEM((2, own_rows, wide), F32),
             pltpu.VMEM((group, own_rows, tall), BF),
@@ -1062,26 +1040,24 @@
             pltpu.VMEM((2, tokens, 2 * units), BF),
             *Reduce.room(line, pair, rows, width, 2, chunks),
             pltpu.VMEM((rows, width), F32),
-            pltpu.VMEM((block_rows, width), F32),
-            pltpu.VMEM((chunks, rows, width), BF),
             dma((2, 3)),
             dma((3 + group,)),
             dma((chunks, 4)),
+            dma((chunks,)),
             *Spread.sems(sizes),
             *Spread.sems(sizes),
             *Reduce.sems(3, chunks)(line),
             *Travel.sems(1, line),
-            dma((3, chunks, 1)),
-            *[dma((3, chunks, 1, 2, line))] * 4,
+            dma((2, chunks, 1)),
+            *[dma((2, chunks, 1, 2, line))] * 4,
         ],
         compiler_params=pltpu.CompilerParams(
             collective_id=collective_id, has_side_effects=True, vmem_limit_bytes=63 * 2**20
         ),
     )(*weights, gain_tile, hidden.reshape(chunks, rows, width), cot.reshape(chunks, rows, width), *tables)
-    output, grad_mid, gain_grad, gain_rows, low, *rest = outs
-    return output, grad_mid, gain_grad, gain_rows, low.reshape(width, tall), [
-        array.reshape(-1, array.shape[-1]) for array in rest
-    ]
+    output, middle, gain_rows, low, entry_one, qkv, attended, terms, *rest = outs
+    flat = [array.reshape(-1, array.shape[-1]) for array in (entry_one, qkv, attended, *rest)]
+    return output, middle, gain_rows, low.reshape(width, tall), terms, flat
 
 
 class GainSum:
@@ -1158,15 +1134,21 @@
 
 
 def closing_kernel(sizes, chunks, *refs):
-    (entry_two, dgu_ref, cot_ref, act_ref, entry_one, branch_ref, qkv_ref, heads_ref, low_ref) = refs[:9]
-    hidden_ref, grad_mid_ref, gain_ref, gain_two_ref, cos_ref, sin_ref, pos_col, pos_row = refs[9:17]
-    piece_refs, (grad_hidden_ref, gain_sum_ref) = refs[17:23], refs[23:25]
-    refs = refs[1:]
-    (left_slots, part, act, dqkv, heads, branch_slots, low_w, grad_heads, grad_proj, key_acc, value_acc) = refs[24:35]
-    near, landed, total, load_sem, left_sem, branch_sem = refs[35:41]
-    ffn_room, att_room = refs[41:46], refs[46:51]
-    ffn_sems, att_sems, reduce_sems = refs[51:58], refs[58:65], refs[65:69]
-    gain_grad_ref, gain_room, gain_sems = refs[69], refs[70:74], refs[74:80]
+    refs = list(refs)
+
+    def take(count):
+        taken, refs[:count] = refs[:count], []
+        return taken
+
+    entry_two, dgu_ref, cots_ref, act_ref, entry_one, heads_ref, low_ref, terms_ref = take(8)
+    qkv_ref, hidden_ref, cot_ref, middle_ref, gains_ref, cos_ref, sin_ref, pos_col, pos_row = take(9)
+    piece_refs, (branch_ref, grad_hidden_ref, gain_sum_ref) = take(6), take(3)
+    left_slots, dgu, part, act, dqkv, heads, branch_slots, low_w, grad_heads, grad_proj, key_acc, value_acc = take(12)
+    near, landed, total, grad_mid, branch, load_sem, left_sem, branch_sem = take(8)
+    ffn_room, att_room = take(5), take(5)
+    ffn_sems, att_sems, reduce_sems = take(7), take(7), take(4)
+    gain_grad, gain_room, gain_sems = take(2), take(4), take(6)
+    travel_sems = take(5)
     line, pair = sizes["ctx"], sizes["core"]
     rows = part.shape[-2]
     block_rows, width = hidden_ref.shape
@@ -1174,7 +1156,7 @@
     query_cols = heads.shape[1]
     qkv_cols = dqkv.shape[1]
     loads = {
-        "dgu": pltpu.make_async_copy(dgu_ref, part, load_sem.at[0]),
+        "dgu": pltpu.make_async_copy(dgu_ref, dgu, load_sem.at[0]),
         "act": pltpu.make_async_copy(act_ref, act, load_sem.at[1]),
         "heads": pltpu.make_async_copy(heads_ref, heads, load_sem.at[2]),
         "low": pltpu.make_async_copy(low_ref.at[:, pl.ds(0, low_w.shape[1])], low_w, load_sem.at[3]),
@@ -1185,19 +1167,22 @@
     att_pieces = [(ref, w, o - shift) for ref, (_, w, o) in zip(piece_refs[3:], names[3:])]
     ffn = Collect(sizes, (2 * act.shape[1], act.shape[1]), ffn_pieces, ffn_room, ffn_sems)
     att = Collect(sizes, (qkv_cols, query_cols), att_pieces, att_room, att_sems)
-    sums = [
-        Reduce(line, pair, part, near, landed, *reduce_sems, (chunk,)) for chunk in range(chunks)
+    entry_sums, sums = [
+        [Reduce(line, pair, part, near, landed, *reduce_sems, (chunk,), kind) for chunk in range(chunks)]
+        for kind in range(2)
+    ]
+    term_loads = [
+        pltpu.make_async_copy(terms_ref.at[chunk], part.at[chunk], load_sem.at[4 + chunk])
+        for chunk in range(chunks)
     ]
     gain_sum = GainSum(sizes, ffn.rows, gain_sum_ref, gain_room, gain_sems)
 
-    def left_loads(turn):
-        tick, slot = turn % line, turn % 2
-        one, sources = (ffn, (entry_two, cot_ref)) if turn < line else (att, (entry_one, branch_ref))
+    def left_loads(turn, item):
+        one, sources = (ffn, (entry_two, cots_ref)) if turn < line else (att, (entry_one, branch_ref))
         return [
             pltpu.make_async_copy(
-                source.at[:, one.lanes(tick, dp)], left_slots.at[slot, item, dp], left_sem.at[slot, item, dp]
+                sources[item].at[:, one.lanes(turn % line, dp)], left_slots.at[item, dp], left_sem.at[item, dp]
             )
-            for item, source in enumerate(sources)
             for dp in range(sizes["dp"])
         ]
 
@@ -1207,31 +1192,23 @@
             branch_ref.at[pl.ds(index * size, size)], branch_slots.at[index % 2], branch_sem.at[index % 2]
         )
 
-    for load in left_loads(0):
-        load.start()
-    for load in loads.values():
-        load.start()
-    for load in left_loads(1):
+    for load in term_loads + left_loads(0, 0) + list(loads.values()) + left_loads(0, 1):
         load.start()
     greet_all(sizes)
 
     def multiply(turn):
-        for load in left_loads(turn):
-            load.wait()
-        lefts = [left_slots.at[turn % 2, item] for item in range(2)]
-        if turn < line:
-            ffn.multiply(turn, lefts, (part_rows, act))
-        else:
-            att.multiply(turn - line, lefts, (dqkv, heads))
-        if turn + 2 < 2 * line:
-            for load in left_loads(turn + 2):
-                load.start()
-
-    class PartRows:
-        def __getitem__(self, at):
-            return part[:, :, :, :, at[1]].reshape(tokens, -1)
-
-    part_rows = PartRows()
+        one, rights = (ffn, (dgu, act)) if turn < line else (att, (dqkv, heads))
+        for item in range(2):
+            for load in left_loads(turn, item):
+                load.wait()
+            one.multiply(turn % line, item, left_slots.at[item], rights[item])
+            if turn % line < line - 1:
+                for load in left_loads(turn + 1, item):
+                    load.start()
+
+    def later_loads():
+        for load in left_loads(line, 0) + left_loads(line, 1):
+            load.start()
 
     def back_to_heads():
         loads["low"].wait()
@@ -1286,7 +1263,9 @@
         for low in range(0, total_rows, 256):
             size = min(256, total_rows - low)
             grads = grad_proj[low : low + size, :]
-            back = grads * cos_ref[low : low + size, :] + turned(grads * sin_ref[low : low + size, :])
+            cosine = for_heads(cos_ref[low : low + size, :], qkv_cols)
+            sine = for_heads(sin_ref[low : low + size, :], qkv_cols)
+            back = grads * cosine + turned(grads * sine)
             at = sequence * total_rows + low
             dqkv[at : at + size, :] = back.astype(BF)
 
@@ -1303,22 +1282,28 @@
             term = contract_cols(mine, low_w[low : low + 512, :qkv_cols]).astype(BF)
             part[chunk, :, :, :, low : low + 512] = term.reshape(pair, line, rows, 512)
 
-    def norm_rows_back(chunk):
-        at = slice(chunk * rows, (chunk + 1) * rows)
-        values = hidden_ref[at, :].astype(F32)
+    def norm_back(values, which, chunk):
         inverse = lax.rsqrt(jnp.mean(values * values, -1, keepdims=True) + EPS_NORM)
         normed = values * inverse
         grad_entry = total[...]
         gain_term = jnp.sum(grad_entry * normed, 0, keepdims=True)
         if chunk == 0:
-            gain_grad_ref[...] = gain_term
+            gain_grad[which][...] = gain_term
         else:
-            gain_grad_ref[...] += gain_term
-        grad_normed = grad_entry * gain_ref[...]
-        grad_rows = inverse * (
-            grad_normed - normed * jnp.mean(grad_normed * normed, -1, keepdims=True)
-        )
-        grad_hidden_ref[at, :] = (grad_mid_ref[at, :] + grad_rows).astype(BF)
+            gain_grad[which][...] += gain_term
+        grad_normed = grad_entry * gains_ref[which : which + 1, :]
+        return inverse * (grad_normed - normed * jnp.mean(grad_normed * normed, -1, keepdims=True))
+
+    def middle_back(chunk):
+        at = slice(chunk * rows, (chunk + 1) * rows)
+        grad = cot_ref[at, :].astype(F32) + norm_back(middle_ref[at, :], 1, chunk)
+        grad_mid[at, :] = grad
+        branch[chunk] = grad.astype(BF)
+
+    def hidden_back(chunk):
+        at = slice(chunk * rows, (chunk + 1) * rows)
+        grad = grad_mid[at, :] + norm_back(hidden_ref[at, :].astype(F32), 0, chunk)
+        grad_hidden_ref[at, :] = grad.astype(BF)
 
     steps = []
 
@@ -1327,43 +1312,63 @@
 
     step(0.0, loads["dgu"].wait)
     step(0.0, loads["act"].wait)
-    period, before = 26.0, 24.0
+    span = (line - 1) * SEND
+    gathered = 0.0
+    for chunk, one in enumerate(entry_sums):
+        start = 1.0 + chunk * span
+        step(start - 0.1, term_loads[chunk].wait)
+        more, finish = one.plan(start, total, functools.partial(middle_back, chunk))
+        steps += more
+        travel = Travel(
+            line,
+            pair,
+            [branch.at[chunk]],
+            [lambda c, z, k=chunk: branch_ref.at[pl.ds(((c * line + z) * chunks + k) * rows, rows)]],
+            *[sem.at[chunk] for sem in travel_sems],
+        )
+        step(finish, travel.begin)
+        for index in range(line - 1):
+            step(finish + (index + 1) * HOP, travel.step, index)
+        gathered = finish + line * HOP - 1.0
+        step(gathered, travel.end)
+    period, before = PERIOD, BEFORE
     for tick in range(line):
         arrived = before + period * tick
-        issued = 5.0 * (tick + 1) if tick < 2 else before + period * (tick - 2) + 0.5
+        issued = 5.5 * (tick + 1) if tick < 2 else before + period * (tick - 2) + 0.5
         step(issued - 5.0 if tick < 2 else issued - 5.5, multiply, tick)
         step(issued, ffn.send_one, tick)
         step(arrived, ffn.sum_one, tick)
-        step(arrived + 12.0, ffn.sum_two, tick)
-    now = 10.5
+        step(arrived + 18.0, ffn.sum_two, tick)
+    now = gathered + 0.1
     step(now, back_to_heads)
+    last_multiply = max(5.5 * 2, before + period * (line - 3)) + 0.6
+    step(max(now, last_multiply), later_loads)
     now += 3.0
     for sequence in range(tokens // total_rows):
         size = query_rows(total_rows)
         for low in range(0, total_rows, size):
             for lane in range(0, query_cols, 2 * HD):
                 step(now, attention_part, sequence, low, size, lane)
-                now += 6.0
+                now += 3.0
         step(now, rotate_back, sequence)
         now += 0.5
-    now = max(now, before + period * (line - 3) + 0.6)
     step(now, loads["heads"].wait)
-    for chunk in range(chunks):
-        step(now + 0.5 + chunk, entry_terms, chunk)
     begin = now + 1.0
     for chunk, one in enumerate(sums):
-        start = begin + chunk * (line - 1) * SEND
-        more, finish = one.plan(start, total, functools.partial(norm_rows_back, chunk))
+        step(now + 0.5 + chunk, entry_sums[chunk].drain)
+        step(now + 0.5 + chunk, entry_terms, chunk)
+        start = begin + chunk * span
+        more, finish = one.plan(start, total, functools.partial(hidden_back, chunk))
         steps += more
-    step(finish + 0.2, gain_sum.begin, gain_grad_ref, gain_two_ref)
+    step(finish + 0.2, gain_sum.begin, *gain_grad)
     step(finish + 4.0, gain_sum.second)
     step(finish + 8.0, gain_sum.third)
     step(finish + 12.0, gain_sum.end)
-    now += 1.0 + chunks
+    now = max(now + 1.0 + chunks, last_multiply + 1.0)
     for tick in range(line):
         step(now + tick, multiply, line + tick)
         step(now + tick + 0.5, att.send_one, tick)
-        arrived = max(now + 30.0 + 2.0 * tick, before + period * (line - 2) + 1.0 + 2.0 * tick)
+        arrived = now + ATT_WAIT + 2.0 * tick
         step(arrived, att.sum_one, tick)
         step(arrived + 12.5, att.sum_two, tick)
     run_steps(steps)
@@ -1371,7 +1376,10 @@
         one.drain()
 
 
-def closing(sizes, collective_id, factors, low, hidden, grad_mid, gain, grad_gain_two, tables):
+PERIOD, BEFORE, ATT_WAIT = 26.0, 40.0, 40.0
+
+
+def closing(sizes, collective_id, factors, low, terms, hidden, cot, middle, gains, tables):
     line, pair = sizes["ctx"], sizes["core"]
     group = line * pair
     block_rows, width = hidden.shape
@@ -1380,7 +1388,7 @@
     rows = block_rows // chunks
     own_rows = width // (group * sizes["dp"] * sizes["x"])
     units = factors[3].shape[1]
-    qkv_cols, query_cols = factors[6].shape[1], factors[7].shape[1]
+    qkv_cols, query_cols = factors[6].shape[1], factors[5].shape[1]
     total_rows = tables[0].shape[0]
     pieces = grad_pieces(sizes)
     any_spec = pl.BlockSpec(memory_space=pl.ANY)
@@ -1390,16 +1398,15 @@
     across = sizes["x"] * pair * own_rows
     branch_rows = 128
     part_shape = (chunks, pair, line, rows, width)
-    factors = list(factors)
-    factors[1] = factors[1].reshape(part_shape)
     return pl.pallas_call(
         functools.partial(closing_kernel, sizes, chunks),
         out_shape=[shape((own_rows, group * w), BF) for _, w, _ in pieces]
-        + [shape((block_rows, width), BF), shape((8, 128), F32)],
-        in_specs=[any_spec] * 6 + [vmem] + [any_spec] * 2 + [vmem] * 8,
-        out_specs=[any_spec] * len(pieces) + [vmem] * 2,
+        + [shape((tokens, width), BF), shape((block_rows, width), BF), shape((8, 128), F32)],
+        in_specs=[any_spec] * 8 + [vmem] * 9,
+        out_specs=[any_spec] * (len(pieces) + 1) + [vmem] * 2,
         scratch_shapes=[
-            pltpu.VMEM((2, 2, sizes["dp"], tokens, across), BF),
+            pltpu.VMEM((2, sizes["dp"], tokens, across), BF),
+            pltpu.VMEM((tokens, 2 * units), BF),
             pltpu.VMEM(part_shape, BF),
             pltpu.VMEM((tokens, units), BF),
             pltpu.VMEM((tokens, qkv_cols), BF),
@@ -1412,22 +1419,27 @@
             pltpu.VMEM((total_rows, 2 * HD), F32),
             *Reduce.room(line, pair, rows, width, chunks)[1:],
             pltpu.VMEM((rows, width), F32),
-            dma((4,)),
-            dma((2, 2, sizes["dp"])),
+            pltpu.VMEM((block_rows, width), F32),
+            pltpu.VMEM((chunks, rows, width), BF),
+            dma((4 + chunks,)),
+            dma((2, sizes["dp"])),
             dma((2,)),
             *Collect.room(sizes, own_rows, 3 * units),
             *Collect.room(sizes, own_rows, qkv_cols + query_cols),
             *Collect.sems(sizes, 3),
             *Collect.sems(sizes, 3),
-            *Reduce.sems(chunks)(line),
+            *Reduce.sems(2, chunks)(line),
+            pltpu.VMEM((1, width), F32),
             pltpu.VMEM((1, width), F32),
             *GainSum.room(sizes, width),
             *GainSum.sems(sizes),
+            dma((chunks, 1)),
+            *[dma((chunks, 1, 2, line))] * 4,
         ],
         compiler_params=pltpu.CompilerParams(
             collective_id=collective_id, has_side_effects=True, vmem_limit_bytes=63 * 2**20
         ),
-    )(*factors, low, hidden, grad_mid, gain, grad_gain_two, *tables)
+    )(*factors[:6], low, terms, factors[6], hidden, cot, middle, gains, *tables)
 
 
 def grad_pieces(sizes):
@@ -1457,7 +1469,9 @@
 
 def adamw_columns(gradient, weight, states, step_rate, decay_rate):
     rows, columns = weight.shape
-    step = math.gcd(columns, 1024)
+    step = math.gcd(columns, 4096)
+    while rows * step > 2**18 and step % 256 == 0:
+        step //= 2
     flat = pl.BlockSpec((rows, step), lambda i: (0, i))
     deep = pl.BlockSpec((2, rows, step), lambda i: (0, 0, i))
     return pl.pallas_call(
@@ -1470,6 +1484,7 @@
         ],
         in_specs=[flat, flat, deep],
         out_specs=[flat, flat, deep],
+        compiler_params=pltpu.CompilerParams(vmem_limit_bytes=40 * 2**20),
     )(gradient, weight, states)
 
 
@@ -1506,20 +1521,19 @@
     ).reshape(-1)
     cos_tab, sin_tab = rope_table(key_pos)
     signs = jnp.where(jnp.arange(HD) < HD // 2, -1.0, 1.0)
-    cosines = jnp.concatenate([cos_tab] * (heads + kv_heads) + [jnp.ones_like(cos_tab)] * kv_heads, 1)
+    cosines = jnp.concatenate([cos_tab] * 3 + [jnp.ones_like(cos_tab)], 1)
     sines = jnp.concatenate(
-        [sin_tab * signs] * (heads + kv_heads) + [jnp.zeros_like(sin_tab)] * kv_heads, 1
+        [sin_tab * signs] * 3 + [jnp.zeros_like(sin_tab)], 1
     )
     tables = (cosines, sines, key_pos[:, None], key_pos[None, :])
     weights = (w_qkv, w_out, w_gate_up, w_down)
-    output, grad_middle, grad_gain_two, gains, low, rest = opening(
+    output, middle, gains, low, terms, flat = opening(
         sizes, 0, weights, norm_gains, hidden[0], cotangent[0], tables
     )
-    entry_one, qkv, attended, grad_branch, entry_two, cot, activated, grad_gu = rest
-    gain_one = gains[:1]
-    factors = (entry_two, grad_gu, cot, activated, entry_one, grad_branch, qkv, attended)
-    *pieces, grad_hidden, gain_sums = closing(
-        sizes, 1, factors, low, hidden[0], grad_middle, gain_one, grad_gain_two, tables
+    entry_one, qkv, attended, entry_two, cot, activated, grad_gu = flat
+    factors = (entry_two, grad_gu, cot, activated, entry_one, attended, qkv)
+    *pieces, _, grad_hidden, gain_sums = closing(
+        sizes, 1, factors, low, terms, hidden[0], cotangent[0], middle, gains, tables
     )
     grad_gate, grad_up, grad_down, grad_query, grad_key_value, grad_out = pieces
     output, grad_hidden = output[None], grad_hidden[None]

time: 561 us -> 505 us (0.900)
  Pallas kernels: 533 us -> 476 us
    pallas_call x1, Pallas kernels: 322 us -> 254 us  [opening(): pl.pallas_call(functools.partial(opening_kernel, sizes, chunks), out_shap...]
    pallas_call x1, Pallas kernels: 177 us -> 201 us  [closing(): pl.pallas_call(functools.partial(closing_kernel, sizes, chunks), out_shap...]
    pallas_call x4, Pallas kernels: 34.1 us -> 20.8 us  [adamw_columns(): pl.pallas_call(functools.partial(adamw_kernel, step_rate, decay_rate), gr...]
where the time goes in v6:
time: 505 us; the launch traced here: 496 us
  Pallas kernels  476 us (94%)
  local copies, waits for them, and re-layouts  11 us (2%)
  other arithmetic  7.5 us (1%)
    pallas_call x1, Pallas kernels, opening(): pl.pallas_call(functools.partial(opening_kernel, sizes, chunks), out_shap...  254 us
    pallas_call x1, Pallas kernels, closing(): pl.pallas_call(functools.partial(closing_kernel, sizes, chunks), out_shap...  201 us
    pallas_call x4, Pallas kernels, adamw_columns(): pl.pallas_call(functools.partial(adamw_kernel, step_rate, decay_rate), gr...  20.8 us

profile of v6, /device:TPU:0, one launch (start us, length us, event | category | flops | bytes accessed | tf_op | source)
XLA Modules:
  0.0 495.7 jit_solution(5197347554445496665)
XLA Ops:
  0.7 0.8 copy.32
  1.4 0.6 pad.4.refs_4_
  2.1 0.7 broadcast_multiply_fusion
  2.7 0.1 iota_add_fusion
  2.8 0.1 convert_element_type.13
  2.9 1.0 multiply_sine_fusion
  3.9 1.3 concatenate.17.refs_7_.refs_13_
  5.2 0.1 maximum_multiply_fusion
  5.4 0.1 pad.14.clone
  5.5 1.0 maximum_maximum_fusion.refs_8_.refs_14_
  6.5 0.9 add.94.refs_9_.refs_15_
  7.4 0.7 add.84.refs_10_.refs_16_
  8.0 254.2 %shard_map.260 = (bf16[128,2048]{1,0:T(8,128)(2,1)}, f32[128,2048]{1,0:T(8,128)}, f32[8,2048]{1,0:T(8,128)}, bf16[8,4,64,768]{3,2,1,0:T(8,128)(2,1)}, bf16[2,4,4...) custom-call(f32[64,3072]{1,0:T(8,128)} %weight_ref.4, ...), custom_call_target="tpu_custom_call" | custom-call | tf_op jit(solution)/shard_map/pallas_call | solution.py:1011
  262.3 200.9 %shard_map.261 = (bf16[64,8192]{1,0:T(8,128)(2,1)}, bf16[64,8192]{1,0:T(8,128)(2,1)}, bf16[64,8192]{1,0:T(8,128)(2,1)}, bf16[64,2048]{1,0:T(8,128)(2,1)}, bf16[6...) custom-call(bf16[1024,2048]{1,0:T(8,128)(2,1)} %bitcast.36, ...), custom_call_target="tpu_custom_call" | custom-call | tf_op jit(solution)/shard_map/pallas_call | solution.py:1401
  463.2 0.0 copy-start.4
  463.2 0.8 fusion.3
  464.0 1.1 reshape.155
  465.2 0.2 reshape.156
  465.4 1.0 pad_maximum_fusion.1.grad_ref
  466.4 1.4 copy-done.5
  467.8 2.5 shard_map.262
  470.3 1.2 copy-done.7
  471.5 0.9 copy-done.8
  472.4 1.7 shard_map.263
  474.2 1.7 pad_maximum_fusion.grad_ref
  475.9 0.0 copy-start.1
  475.9 11.9 %shard_map.264 = (f32[64,16384]{1,0:T(8,128)}, f32[64,16384]{1,0:T(8,128)}, f32[2,64,16384]{2,1,0:T(8,128)}) custom-call(bf16[64,16384]{1,0:T(8,128)(2,1)S(1)} %pad_maximum_fusion.grad_ref, f32[64,16384]{1,0:T(8,128)S(1)} %copy-done, f32[2,64,16384]{2,1,0:T(8,128)} %state_ref.6), custom_call_target="tpu_custom_call" | custom-call | tf_op jit(solution)/shard_map/pallas_call | solution.py:1477
  487.8 4.7 shard_map.265
  492.5 0.6 fusion.4
  493.1 0.6 pad_maximum_fusion.2
  493.7 0.8 copy.40
  494.5 0.8 copy.41
  (28 shorter events, 0.1 us)
Async XLA Ops:
  262.3 200.9 %copy-start.11 = (f32[2,2,64]{2,1,0:T(2,128)S(1)}, f32[2,2,64]{2,1,0:T(2,128)}, u32[]{:S(2)}) copy-start(f32[2,2,64]{2,1,0:T(2,128)} %param.21) | copy-start | bytes 3076
  262.3 204.1 %copy-start.3 = (f32[64,3072]{1,0:T(8,128)S(1)}, f32[64,3072]{1,0:T(8,128)}, u32[]{:S(2)}) copy-start(f32[64,3072]{1,0:T(8,128)} %weight_ref.4) | copy-start | bytes 2359300
  463.2 7.1 %copy-start.4 = (f32[64,2048]{1,0:T(8,128)S(1)}, f32[64,2048]{1,0:T(8,128)}, u32[]{:S(2)}) copy-start(f32[64,2048]{1,0:T(8,128)} %weight_ref.5) | copy-start | bytes 1572868
  464.0 28.5 %copy-start.13 = (f32[2,64]{1,0:T(2,128)}, f32[2,64]{1,0:T(2,128)S(1)}, u32[]{:S(2)}) copy-start(f32[2,64]{1,0:T(2,128)S(1)} %get-tuple-element.108) | copy-start | bytes 1540
  466.4 1.4 copy-start.5
  467.8 8.1 %copy-start = (f32[64,16384]{1,0:T(8,128)S(1)}, f32[64,16384]{1,0:T(8,128)}, u32[]{:S(2)}) copy-start(f32[64,16384]{1,0:T(8,128)} %weight_ref.6) | copy-start | bytes 12582916
  470.3 1.2 copy-start.7
  471.5 0.9 copy-start.8
  475.9 11.9 %copy-start.1 = (f32[64,8192]{1,0:T(8,128)S(1)}, f32[64,8192]{1,0:T(8,128)}, u32[]{:S(2)}) copy-start(f32[64,8192]{1,0:T(8,128)} %weight_ref.7) | copy-start | bytes 6291460
  475.9 11.9 %copy-start.2 = (f32[2,64,8192]{2,1,0:T(8,128)S(1)}, f32[2,64,8192]{2,1,0:T(8,128)}, u32[]{:S(2)}) copy-start(f32[2,64,8192]{2,1,0:T(8,128)} %state_ref.7) | copy-start | bytes 12582916
  475.9 11.9 %copy-start.6 = (bf16[64,8192]{1,0:T(8,128)(2,1)S(1)}, bf16[64,8192]{1,0:T(8,128)(2,1)}, u32[]{:S(2)}) copy-start(bf16[64,8192]{1,0:T(8,128)(2,1)} %get-tuple-element.71.grad_ref) | copy-start | bytes 3145732
  487.8 4.7 copy-start.12
  487.8 5.9 %copy-start.9 = (bf16[128,2048]{1,0:T(8,128)(2,1)S(1)}, bf16[128,2048]{1,0:T(8,128)(2,1)}, u32[]{:S(2)}) copy-start(bf16[128,2048]{1,0:T(8,128)(2,1)} %get-tuple-element.49) | copy-start | bytes 1572868
  487.8 6.7 %copy-start.10 = (bf16[128,2048]{1,0:T(8,128)(2,1)S(1)}, bf16[128,2048]{1,0:T(8,128)(2,1)}, u32[]{:S(2)}) copy-start(bf16[128,2048]{1,0:T(8,128)(2,1)} %get-tuple-element.61) | copy-start | bytes 1572868

commit v7 on v6

--- a/solution.py
+++ b/solution.py
@@ -30,13 +30,13 @@
 LR_GAIN = 0.3
 
 
-def rope_table(positions):
+def rope_rates():
     half_dim = HD // 2
     index_row = jnp.arange(half_dim, dtype=jnp.float32)
     frequency = jnp.exp(-(2.0 * index_row / HD) * math.log(THETA))
     wavelen = 2.0 * math.pi / frequency
     smooth = (8192.0 / wavelen - 1.0) / 3.0
-    scaled = jnp.where(
+    return jnp.where(
         wavelen < 2048.0,
         frequency,
         jnp.where(
@@ -45,10 +45,6 @@
             (1.0 - smooth) * frequency / 32.0 + smooth * frequency,
         ),
     )
-    angles = positions.astype(jnp.float32)[:, None] * scaled[None, :]
-    cosine = jnp.cos(angles)
-    sine_part = jnp.sin(angles)
-    return (jnp.concatenate([cosine, cosine], 1), jnp.concatenate([sine_part, sine_part], 1))
 
 
 def adamw(weight, gradient, states, step_rate, decay_rate):
@@ -697,8 +693,8 @@
         taken, refs[:count] = refs[:count], []
         return taken
 
-    qkv_in, out_in, gate_up_in, down_in, gain_in, hidden_ref, cot_ref, cos_ref, sin_ref, pos_col, pos_row = take(11)
-    output_ref, middle, gains_ref = take(3)
+    qkv_in, out_in, gate_up_in, down_in, gain_in, hidden_ref, cot_ref, rate_ref, pos_col, pos_row = take(10)
+    output_ref, middle, gains_ref, cos_ref, sin_ref = take(5)
     low_out, entry_one_out, qkv_out, heads_out, terms_out, entry_two_out, cots_out, act_out, dgu_out = take(9)
     stage, tall, wide, low_w, ffn_w, rows_in, cots, qkv, heads, act, dgu = take(11)
     part, near, landed, total = take(4)
@@ -769,6 +765,15 @@
         each = groups // count
         return weight[index * each : (index + 1) * each, :, :, first : first + size].reshape(-1, size)
 
+    def rotary_tables():
+        @pl.loop(0, total_rows // block_rows)
+        def _(index):
+            at = pl.ds(pl.multiple_of(index * block_rows, block_rows), block_rows)
+            angle = pos_col[at, :].astype(F32) * rate_ref[...]
+            sine = jnp.sin(angle)
+            cos_ref[at, :] = jnp.cos(angle)
+            sin_ref[at, :] = jnp.where(lane_index(sine.shape) % HD < HD // 2, -sine, sine)
+
     def gains_to_rows():
         columns = columns_of(low_w, qkv_cols + query_cols, 128).astype(F32)
         gains_ref[...] = columns.T[:8, :]
@@ -907,6 +912,7 @@
     step(0.1, low.begin, *range(group))
     step(0.2, pack_high)
     step(0.3, high.begin, *range(min(group, 4)))
+    step(9.0, rotary_tables)
     for index in range(group):
         when = 1.0 + T_LOW * (index // 2)
         step(when, low.onward, index)
@@ -1014,6 +1020,8 @@
             shape((block_rows, width), BF),
             shape((block_rows, width), F32),
             shape((8, width), F32),
+            shape((tables[1].shape[0], 4 * HD), F32),
+            shape((tables[1].shape[0], 4 * HD), F32),
             shape(blocks + (tall,), BF),
             shape((pair, line, chunks, rows, width), BF),
             shape((group * block_rows, qkv_cols), BF),
@@ -1024,8 +1032,8 @@
             shape((chunks, tokens, units), BF),
             shape((chunks, tokens, 2 * units), BF),
         ],
-        in_specs=[vmem, vmem, any_spec, any_spec] + [vmem] * 7,
-        out_specs=[vmem] * 3 + [any_spec] * 9,
+        in_specs=[vmem, vmem, any_spec, any_spec] + [vmem] * 6,
+        out_specs=[vmem] * 5 + [any_spec] * 9,
         scratch_shapes=[
             pltpu.VMEM((2, own_rows, wide), F32),
             pltpu.VMEM((group, own_rows, tall), BF),
@@ -1055,9 +1063,9 @@
             collective_id=collective_id, has_side_effects=True, vmem_limit_bytes=63 * 2**20
         ),
     )(*weights, gain_tile, hidden.reshape(chunks, rows, width), cot.reshape(chunks, rows, width), *tables)
-    output, middle, gain_rows, low, entry_one, qkv, attended, terms, *rest = outs
+    output, middle, gain_rows, cosines, sines, low, entry_one, qkv, attended, terms, *rest = outs
     flat = [array.reshape(-1, array.shape[-1]) for array in (entry_one, qkv, attended, *rest)]
-    return output, middle, gain_rows, low.reshape(width, tall), terms, flat
+    return output, middle, gain_rows, (cosines, sines), low.reshape(width, tall), terms, flat
 
 
 class GainSum:
@@ -1519,21 +1527,16 @@
     key_pos = (
         span_order[:, None] * span_rows + jnp.arange(span_rows, dtype=jnp.int32)[None, :]
     ).reshape(-1)
-    cos_tab, sin_tab = rope_table(key_pos)
-    signs = jnp.where(jnp.arange(HD) < HD // 2, -1.0, 1.0)
-    cosines = jnp.concatenate([cos_tab] * 3 + [jnp.ones_like(cos_tab)], 1)
-    sines = jnp.concatenate(
-        [sin_tab * signs] * 3 + [jnp.zeros_like(sin_tab)], 1
-    )
-    tables = (cosines, sines, key_pos[:, None], key_pos[None, :])
+    positions = (key_pos[:, None], key_pos[None, :])
+    rates = jnp.concatenate([rope_rates()] * 6 + [jnp.zeros(HD, jnp.float32)])[None]
     weights = (w_qkv, w_out, w_gate_up, w_down)
-    output, middle, gains, low, terms, flat = opening(
-        sizes, 0, weights, norm_gains, hidden[0], cotangent[0], tables
+    output, middle, gains, turns, low, terms, flat = opening(
+        sizes, 0, weights, norm_gains, hidden[0], cotangent[0], (rates,) + positions
     )
     entry_one, qkv, attended, entry_two, cot, activated, grad_gu = flat
     factors = (entry_two, grad_gu, cot, activated, entry_one, attended, qkv)
     *pieces, _, grad_hidden, gain_sums = closing(
-        sizes, 1, factors, low, terms, hidden[0], cotangent[0], middle, gains, tables
+        sizes, 1, factors, low, terms, hidden[0], cotangent[0], middle, gains, turns + positions
     )
     grad_gate, grad_up, grad_down, grad_query, grad_key_value, grad_out = pieces
     output, grad_hidden = output[None], grad_hidden[None]

time: 505 us -> 501 us (level)
  no operation moved by 1% of the time
where the time goes in v7:
time: 501 us; the launch traced here: 492 us
  Pallas kernels  476 us (95%)
  local copies, waits for them, and re-layouts  10.2 us (2%)
  other arithmetic  5.39 us (1%)
    pallas_call x1, Pallas kernels, opening(): pl.pallas_call(functools.partial(opening_kernel, sizes, chunks), out_shap...  254 us
    pallas_call x1, Pallas kernels, closing(): pl.pallas_call(functools.partial(closing_kernel, sizes, chunks), out_shap...  201 us
    pallas_call x4, Pallas kernels, adamw_columns(): pl.pallas_call(functools.partial(adamw_kernel, step_rate, decay_rate), gr...  20.8 us

profile of v7, /device:TPU:0, one launch (start us, length us, event | category | flops | bytes accessed | tf_op | source)
XLA Modules:
  0.0 492.1 jit_solution(4754203247546479226)
XLA Ops:
  0.7 0.8 copy.32
  1.4 0.6 pad.4.refs_4_
  2.1 0.7 concatenate.9
  2.7 0.7 broadcast_multiply_fusion
  3.4 0.1 iota_add_fusion
  3.5 0.9 add.91.refs_8_.refs_15_
  4.4 0.7 add.81.refs_9_.refs_16_
  5.0 253.7 %shard_map.260 = (bf16[128,2048]{1,0:T(8,128)(2,1)}, f32[128,2048]{1,0:T(8,128)}, f32[8,2048]{1,0:T(8,128)}, f32[512,256]{1,0:T(8,128)}, f32[512,256]{1,0:T(8,12...) custom-call(f32[64,3072]{1,0:T(8,128)} %weight_ref.4, ...), custom_call_target="tpu_custom_call" | custom-call | tf_op jit(solution)/shard_map/pallas_call | solution.py:1017
  258.8 0.0 copy-start.11
  258.8 0.0 copy-start.3
  258.8 201.0 %shard_map.261 = (bf16[64,8192]{1,0:T(8,128)(2,1)}, bf16[64,8192]{1,0:T(8,128)(2,1)}, bf16[64,8192]{1,0:T(8,128)(2,1)}, bf16[64,2048]{1,0:T(8,128)(2,1)}, bf16[6...) custom-call(bf16[1024,2048]{1,0:T(8,128)(2,1)} %bitcast.37, ...), custom_call_target="tpu_custom_call" | custom-call | tf_op jit(solution)/shard_map/pallas_call | solution.py:1409
  459.8 0.0 copy-start.4
  459.8 0.8 fusion.2
  460.6 1.1 reshape.116
  461.8 0.2 reshape.117
  462.0 1.0 pad_maximum_fusion.1.grad_ref
  463.0 0.0 copy-start.5
  463.0 1.4 copy-done.5
  464.4 2.5 shard_map.262
  466.9 0.0 copy-done.4
  466.9 1.2 copy-done.7
  468.1 0.9 copy-done.8
  469.1 1.7 shard_map.263
  470.8 1.7 pad_maximum_fusion.grad_ref
  472.5 0.0 copy-start.1
  472.5 0.0 copy-start.2
  472.5 11.9 %shard_map.264 = (f32[64,16384]{1,0:T(8,128)}, f32[64,16384]{1,0:T(8,128)}, f32[2,64,16384]{2,1,0:T(8,128)}) custom-call(bf16[64,16384]{1,0:T(8,128)(2,1)S(1)} %pad_maximum_fusion.grad_ref, f32[64,16384]{1,0:T(8,128)S(1)} %copy-done, f32[2,64,16384]{2,1,0:T(8,128)} %state_ref.6), custom_call_target="tpu_custom_call" | custom-call | tf_op jit(solution)/shard_map/pallas_call | solution.py:1485
  484.5 4.7 shard_map.265
  489.2 0.6 fusion.3
  489.7 0.6 pad_maximum_fusion.2
  490.3 0.8 copy.40
  491.1 0.8 copy.41
  (21 shorter events, 0.1 us)
Async XLA Ops:
  258.8 201.1 %copy-start.11 = (f32[2,2,64]{2,1,0:T(2,128)S(1)}, f32[2,2,64]{2,1,0:T(2,128)}, u32[]{:S(2)}) copy-start(f32[2,2,64]{2,1,0:T(2,128)} %param.21) | copy-start | bytes 3076
  258.8 204.2 %copy-start.3 = (f32[64,3072]{1,0:T(8,128)S(1)}, f32[64,3072]{1,0:T(8,128)}, u32[]{:S(2)}) copy-start(f32[64,3072]{1,0:T(8,128)} %weight_ref.4) | copy-start | bytes 2359300
  459.8 7.1 %copy-start.4 = (f32[64,2048]{1,0:T(8,128)S(1)}, f32[64,2048]{1,0:T(8,128)}, u32[]{:S(2)}) copy-start(f32[64,2048]{1,0:T(8,128)} %weight_ref.5) | copy-start | bytes 1572868
  460.6 28.5 %copy-start.13 = (f32[2,64]{1,0:T(2,128)}, f32[2,64]{1,0:T(2,128)S(1)}, u32[]{:S(2)}) copy-start(f32[2,64]{1,0:T(2,128)S(1)} %get-tuple-element.108) | copy-start | bytes 1540
  463.0 1.4 copy-start.5
  464.4 8.1 %copy-start = (f32[64,16384]{1,0:T(8,128)S(1)}, f32[64,16384]{1,0:T(8,128)}, u32[]{:S(2)}) copy-start(f32[64,16384]{1,0:T(8,128)} %weight_ref.6) | copy-start | bytes 12582916
  466.9 1.2 copy-start.7
  468.1 0.9 copy-start.8
  472.5 11.9 %copy-start.1 = (f32[64,8192]{1,0:T(8,128)S(1)}, f32[64,8192]{1,0:T(8,128)}, u32[]{:S(2)}) copy-start(f32[64,8192]{1,0:T(8,128)} %weight_ref.7) | copy-start | bytes 6291460
  472.5 11.9 %copy-start.2 = (f32[2,64,8192]{2,1,0:T(8,128)S(1)}, f32[2,64,8192]{2,1,0:T(8,128)}, u32[]{:S(2)}) copy-start(f32[2,64,8192]{2,1,0:T(8,128)} %state_ref.7) | copy-start | bytes 12582916
  472.5 11.9 %copy-start.6 = (bf16[64,8192]{1,0:T(8,128)(2,1)S(1)}, bf16[64,8192]{1,0:T(8,128)(2,1)}, u32[]{:S(2)}) copy-start(bf16[64,8192]{1,0:T(8,128)(2,1)} %get-tuple-element.75.grad_ref) | copy-start | bytes 3145732
  484.4 4.7 copy-start.12
  484.4 5.9 %copy-start.9 = (bf16[128,2048]{1,0:T(8,128)(2,1)S(1)}, bf16[128,2048]{1,0:T(8,128)(2,1)}, u32[]{:S(2)}) copy-start(bf16[128,2048]{1,0:T(8,128)(2,1)} %get-tuple-element.51) | copy-start | bytes 1572868
  484.5 6.7 %copy-start.10 = (bf16[128,2048]{1,0:T(8,128)(2,1)S(1)}, bf16[128,2048]{1,0:T(8,128)(2,1)}, u32[]{:S(2)}) copy-start(bf16[128,2048]{1,0:T(8,128)(2,1)} %get-tuple-element.65) | copy-start | bytes 1572868
